TPU v7x, 32 devices: a whole 2x2x4 slice. The times are simulated.
32 devices in a mesh: gx: 8 (over z, core), gy: 4 (over y, x).
Axes of the slice: x: 2, y: 2, z: 4, core: 2. Of those that a mesh axis runs over, the one named last changes fastest.
Arguments:
- patches: bfloat16 [512, 6144], P('gy', 'gx'), may hold values from -40 to 40
- ln_gain: float32 [6144], P('gx'), may hold values from 0.5 to 1.5
- weight_in: bfloat16 [6144, 24576], P('gx', 'gy'), may hold values from -0.12757759 to 0.12757759
- weight_out: bfloat16 [24576, 6144], P('gy', 'gx'), may hold values from -0.063788795 to 0.063788795
- upstream: bfloat16 [512, 6144], P('gy', 'gx'), may hold values from -18 to 18
- row_in: float32 [6144], P('gx'), may hold values from 7.68 to 92.16
- col_in: float32 [24576], P('gy'), may hold values from 7.68 to 92.16
- row_out: float32 [24576], P('gy'), may hold values from 7.68 to 92.16
- col_out: float32 [6144], P('gx'), may hold values from 7.68 to 92.16
Outputs:
- output: bfloat16 [512, 6144], P('gy', 'gx')
- input_grad: float32 [512, 6144], P('gy', 'gx')
- update_in: float32 [6144, 24576], P('gx', 'gy')
- update_out: float32 [24576, 6144], P('gy', 'gx')
All inputs are finite; a program needn't handle non-finite values.
Results may differ from a plain program's by a relative error of at most 0.028.
Values may be sent and summed in bfloat16 or wider, within the bound.
No kernel may reach another device: no remote copies, remote signals or barrier semaphores. Data moves between devices by JAX's collectives and lax.ppermute only.
A program may use at most 128 MiB of HBM per device.

v0:
```python
import jax
import jax.numpy as jnp
from jax import lax
from jax.sharding import PartitionSpec as P

D = 6144
FF = 24576


def contract(left, right, left_dim, right_dim):
    return lax.dot_general(
        left, right, (((left_dim,), (right_dim,)), ((), ())), preferred_element_type=jnp.float32
    )


def rounded_once(values):
    return lax.optimization_barrier(values.astype(jnp.bfloat16)).astype(jnp.float32)


def gelu_parts(summed):
    hidden_pre = rounded_once(summed)
    phi = 0.5 * (1.0 + lax.erf(hidden_pre * 0.7071067811865476))
    slope = phi + hidden_pre * jnp.exp(-0.5 * hidden_pre * hidden_pre) * 0.3989422804014327
    return ((hidden_pre * phi).astype(jnp.bfloat16), slope)


def body(patches, ln_gain, weight_in, weight_out, upstream, row_in, col_in, row_out, col_out):
    x_float = patches.astype(jnp.float32)
    row_sums, row_squares = lax.psum(
        (jnp.sum(x_float, axis=1), jnp.sum(x_float * x_float, axis=1)), "gx"
    )
    row_mean = row_sums / D
    row_var = row_squares / D - row_mean * row_mean
    inv_std = lax.rsqrt(row_var + 1e-06)[:, None]
    unit = (x_float - row_mean[:, None]) * inv_std
    normed = (unit * ln_gain[None, :]).astype(jnp.bfloat16)
    normed_full = lax.all_gather(normed, "gy", axis=0, tiled=True)
    summed_pre = lax.psum_scatter(
        jnp.dot(normed_full, weight_in, preferred_element_type=jnp.float32).astype(jnp.bfloat16),
        "gx",
        scatter_dimension=0,
        tiled=True,
    ).astype(jnp.float32)
    hidden, slope = gelu_parts(summed_pre)
    hidden_full = lax.all_gather(hidden, "gx", axis=0, tiled=True)
    branch = lax.psum_scatter(
        jnp.dot(hidden_full, weight_out, preferred_element_type=jnp.float32).astype(jnp.bfloat16),
        "gy",
        scatter_dimension=0,
        tiled=True,
    ).astype(jnp.float32)
    output = (x_float + branch).astype(jnp.bfloat16)
    upstream_full = lax.all_gather(upstream, "gy", axis=0, tiled=True)
    grad_out = contract(hidden_full, upstream_full, 0, 0)
    hidden_grad = rounded_once(
        lax.psum_scatter(
            contract(upstream_full, weight_out, 1, 1).astype(jnp.bfloat16),
            "gx",
            scatter_dimension=0,
            tiled=True,
        ).astype(jnp.float32)
    )
    act_grad = (hidden_grad * slope).astype(jnp.bfloat16)
    act_full = lax.all_gather(act_grad, "gx", axis=0, tiled=True)
    grad_in = contract(normed_full, act_full, 0, 0)
    normed_grad = lax.psum_scatter(
        contract(act_full, weight_in, 1, 1).astype(jnp.bfloat16),
        "gy",
        scatter_dimension=0,
        tiled=True,
    ).astype(jnp.float32)
    scaled = normed_grad * ln_gain[None, :]
    first_sum, second_sum = lax.psum(
        (jnp.sum(scaled, axis=1), jnp.sum(scaled * unit, axis=1)), "gx"
    )
    input_grad = upstream.astype(jnp.float32) + inv_std * (
        scaled - first_sum[:, None] / D - unit * (second_sum[:, None] / D)
    )
    squares_in = grad_in * grad_in + 1e-30
    squares_out = grad_out * grad_out + 1e-30
    row_in_sum, col_out_sum = lax.psum(
        (jnp.sum(squares_in, axis=1), jnp.sum(squares_out, axis=0)), "gy"
    )
    col_in_sum, row_out_sum = lax.psum(
        (jnp.sum(squares_in, axis=0), jnp.sum(squares_out, axis=1)), "gx"
    )
    row_in_new = 0.9 * row_in + 0.1 * (row_in_sum / FF)
    col_in_new = 0.9 * col_in + 0.1 * (col_in_sum / D)
    row_out_new = 0.9 * row_out + 0.1 * (row_out_sum / D)
    col_out_new = 0.9 * col_out + 0.1 * (col_out_sum / FF)
    total_in, total_out = lax.psum(
        (jnp.sum(row_in_new) / lax.axis_size("gy"), jnp.sum(row_out_new) / lax.axis_size("gx")),
        ("gx", "gy"),
    )
    mean_in = total_in / D
    mean_out = total_out / FF
    update_in = grad_in / jnp.sqrt(row_in_new[:, None] * col_in_new[None, :] / mean_in)
    update_out = grad_out / jnp.sqrt(row_out_new[:, None] * col_out_new[None, :] / mean_out)
    return (output, input_grad, update_in, update_out)


def solution(mesh):
    in_specs = (
        P("gy", "gx"),
        P("gx"),
        P("gx", "gy"),
        P("gy", "gx"),
        P("gy", "gx"),
        P("gx"),
        P("gy"),
        P("gy"),
        P("gx"),
    )
    out_specs = (P("gy", "gx"), P("gy", "gx"), P("gx", "gy"), P("gy", "gx"))
    return jax.shard_map(body, mesh=mesh, in_specs=in_specs, out_specs=out_specs, check_vma=False)
```

profile of v0, /device:TPU:0, one launch (start us, length us, event | category | flops | bytes accessed | tf_op | source)
XLA Modules:
  0.0 456.5 jit_solution(13589283070524777777)
XLA Ops:
  7.2 0.0 reduce-scatter.9.cloned.1.call-start
  7.2 13.8 %all_gather.14 = bf16[512,768]{1,0:T(8,128)(2,1)S(1)} all-gather(bf16[128,768]{1,0:T(8,128)(2,1)} %param.13), channel_id=1, replica_groups=mesh['gx'=8,'gy'=4] {'gy'}, dimensions={0}, use_global_device_ids=true | all-gather | bytes 983040 | tf_op jit(solution)/shard_map/all_gather | solution.py:53
  21.0 0.0 copy-start
  21.0 0.0 copy-start.3
  21.0 10.7 %convolution_convert_fusion = bf16[512,6144]{1,0:T(8,128)(2,1)} fusion(bf16[512,768]{1,0:T(8,128)(2,1)S(1)} %all_gather.14, bf16[6144,768]{1,0:T(8,128)(2,1)} %param.12), kind=kOutput, calls=%fused_computation.8 | convolution fusion | flops 4834983936 | bytes 16515072 | tf_op jit(solution)/shard_map/dot_general | solution.py:11
  31.7 0.0 reduce-scatter.9.cloned.1.call-update
  31.8 0.0 reduce-scatter.5.cloned.1.call-start
  31.8 0.0 copy-done
  31.8 0.1 convert_reduce_fusion
  32.0 15.7 %all-reduce.2 = (f32[128]{0:T(128)S(1)}, f32[128]{0:T(128)S(1)}) all-reduce(f32[128]{0:T(128)S(1)} %get-tuple-element.11, f32[128]{0:T(128)S(1)} %get-tuple-element.10), channel_id=1, replica_groups=mesh['gx'=8,'gy'=4] {'gx'}, use_global_device_ids=true, to_apply=%region_3.0 | all-reduce | flops 256 | bytes 2048 | tf_op jit(solution)/shard_map/psum | solution.py:29
  47.6 0.0 copy-done.3
  47.6 0.1 fusion.17
  47.8 10.1 %all_gather.12 = bf16[512,768]{1,0:T(8,128)(2,1)S(1)} all-gather(bf16[128,768]{1,0:T(8,128)(2,1)S(1)} %fusion.17), channel_id=1, replica_groups=mesh['gx'=8,'gy'=4] {'gy'}, dimensions={0}, use_global_device_ids=true | all-gather | bytes 983040 | tf_op jit(solution)/shard_map/all_gather | solution.py:37
  57.9 10.7 %convolution_convert_fusion.1 = bf16[512,6144]{1,0:T(8,128)(2,1)} fusion(bf16[512,768]{1,0:T(8,128)(2,1)S(1)} %all_gather.12, bf16[768,6144]{1,0:T(8,128)(2,1)} %param.11), kind=kOutput, calls=%fused_computation.9 | convolution fusion | flops 4834983936 | bytes 16515072 | tf_op jit(solution)/shard_map/dot_general | solution.py:39
  68.6 0.0 reduce-scatter.5.cloned.1.call-update
  68.6 0.0 all-gather.5.cloned.1.call-start
  68.6 33.5 %reduce-scatter.9.cloned.1.call-done = bf16[64,6144]{1,0:T(8,128)(2,1)} async-done(((bf16[512,6144]{1,0:T(8,128)(2,1)}), bf16[64,6144]{1,0:T(8,128)(2,1)}) %reduce-scatter.9.cloned.1.call-update) | async-done | bytes 786448 | tf_op jit(solution)/shard_map/reduce_scatter | solution.py:56
  102.1 71.1 %reduce-scatter.5.cloned.1.call-done = bf16[64,6144]{1,0:T(8,128)(2,1)} async-done(((bf16[512,6144]{1,0:T(8,128)(2,1)}), bf16[64,6144]{1,0:T(8,128)(2,1)}) %reduce-scatter.5.cloned.1.call-update) | async-done | bytes 786448 | tf_op jit(solution)/shard_map/reduce_scatter | solution.py:38
  173.3 3.3 fusion.12
  176.6 0.0 all-gather.5.cloned.1.call-update
  176.6 0.0 all-gather.3.cloned.1.call-start
  176.6 0.5 all-gather.3.cloned.1.call-update
  177.2 0.0 reduce-scatter.11.cloned.1.call-start
  177.2 62.7 %all-gather.5.cloned.1.call-done = bf16[512,6144]{1,0:T(8,128)(2,1)} async-done(((bf16[64,6144]{1,0:T(8,128)(2,1)}), bf16[512,6144]{1,0:T(8,128)(2,1)}) %all-gather.5.cloned.1.call-update) | async-done | bytes 6291472 | tf_op jit(solution)/shard_map/all_gather | solution.py:64
  239.9 10.7 %convolution_convert_fusion.2 = bf16[512,768]{1,0:T(8,128)(2,1)} fusion(bf16[512,6144]{1,0:T(8,128)(2,1)} %all-gather.5.cloned.1.call-done, bf16[768,6144]{1,0:T(8,128)(2,1)} %param.11), kind=kOutput, calls=%fused_computation.24 | convolution fusion | flops 4832231424 | bytes 16515072 | tf_op jit(solution)/shard_map/dot_general | solution.py:11
  250.6 0.0 reduce-scatter.11.cloned.1.call-update
  250.6 0.2 reduce-scatter.7.cloned.1.call-start
  250.8 54.6 %all-gather.3.cloned.1.call-done = bf16[512,6144]{1,0:T(8,128)(2,1)} async-done(((bf16[64,6144]{1,0:T(8,128)(2,1)}), bf16[512,6144]{1,0:T(8,128)(2,1)}) %all-gather.3.cloned.1.call-update) | async-done | bytes 6291472 | tf_op jit(solution)/shard_map/all_gather | solution.py:45
  305.4 10.6 %convolution_convert_fusion.3 = bf16[512,768]{1,0:T(8,128)(2,1)} fusion(bf16[512,6144]{1,0:T(8,128)(2,1)} %all-gather.3.cloned.1.call-done, bf16[6144,768]{1,0:T(8,128)(2,1)} %param.12), kind=kOutput, calls=%fused_computation.25 | convolution fusion | flops 4832231424 | bytes 16515072 | tf_op jit(solution)/shard_map/dot_general | solution.py:47
  316.0 0.0 reduce-scatter.7.cloned.1.call-update
  316.0 13.6 %fusion = (f32[6144]{0:T(1024)S(1)}, f32[768]{0:T(1024)S(1)}, f32[768,6144]{1,0:T(8,128)}) fusion(bf16[512,768]{1,0:T(8,128)(2,1)S(1)} %all_gather.12, bf16[512,6144]{1,0:T(8,128)(2,1)} %all-gather.5.cloned.1.call-done), kind=kOutput, calls=%fused_computation.4 | convolution fusion | flops 4850705408 | bytes 25979904 | tf_op jit(solution)/shard_map/dot_general | solution.py:11
  329.5 0.0 copy-start.6
  329.5 0.0 copy-start.7
  329.6 0.0 copy-start.4
  329.6 0.0 copy-start.5
  329.6 13.3 %fusion.2 = (f32[768]{0:T(1024)S(1)}, f32[6144]{0:T(1024)S(1)}, f32[6144,768]{1,0:T(8,128)}) fusion(bf16[512,6144]{1,0:T(8,128)(2,1)} %all-gather.3.cloned.1.call-done, bf16[512,768]{1,0:T(8,128)(2,1)S(1)} %all_gather.14), kind=kOutput, calls=%fused_computation.6 | convolution fusion | flops 4850705408 | bytes 25979904 | tf_op jit(solution)/shard_map/dot_general | solution.py:11
  342.8 10.1 %all-reduce.3 = (f32[768]{0:T(1024)S(1)}, f32[768]{0:T(1024)S(1)}) all-reduce(f32[768]{0:T(1024)S(1)} %get-tuple-element.7, f32[768]{0:T(1024)S(1)} %get-tuple-element.4), channel_id=1, replica_groups=mesh['gx'=8,'gy'=4] {'gy'}, use_global_device_ids=true, to_apply=%region_13.0 | all-reduce | flops 1536 | bytes 12288 | tf_op jit(solution)/shard_map/psum | solution.py:81
  353.0 0.0 copy-done.6
  353.0 0.6 fusion.26
  354.3 0.0 copy-done.7
  354.3 0.0 reduce-scatter.11.cloned.1.call-done
  354.3 1.1 fusion.24
  355.4 26.4 %all-reduce.1 = (f32[128]{0:T(128)S(1)}, f32[128]{0:T(128)S(1)}, f32[6144]{0:T(1024)S(1)}, f32[6144]{0:T(1024)S(1)}) all-reduce(f32[128]{0:T(128)S(1)} %get-tuple-element.9, f32[128]{0:T(128)S(1)} %get-tuple-element.8, f32[6144]{0:T(1024)S(1)} %get-tuple-element.5, f32[6144]{0:T(1024)S(1)} %get-tuple-element.6), channel_id=1, replica_groups=mesh['gx'=8,'gy'=4] {'gx'}, use_global_device_ids=true, to_apply=%region_11.0 | all-reduce | flops 12544 | bytes 100352 | tf_op jit(solution)/shard_map/psum | solution.py:73
  381.9 0.0 copy-done.4
  381.9 0.0 copy-done.5
  381.9 0.6 fusion.25
  383.2 36.9 %all-reduce = (f32[]{:T(128)}, f32[]{:T(128)}) all-reduce(f32[]{:T(128)S(6)} %div.50, f32[]{:T(128)S(6)} %div.55), channel_id=1, replica_groups=mesh['gx'=8,'gy'=4] {'gx','gy'}, use_global_device_ids=true, to_apply=%region_17.0 | all-reduce | flops 2 | bytes 16 | tf_op jit(solution)/shard_map/psum | solution.py:91
  421.4 0.0 slice-start
  421.4 0.0 slice-start.1
  421.4 0.0 slice-start.2
  421.4 0.0 slice-start.3
  421.4 0.0 slice-start.4
  421.4 17.4 %rsqrt_multiply_fusion.1 = f32[768,6144]{1,0:T(8,128)} fusion(f32[768,6144]{1,0:T(8,128)} %get-tuple-element.33, f32[]{:T(128)S(6)} %div.51, f32[6144]{0:T(1024)S(1)} %multiply_add_fusion.3, f32[768]{0:T(1024)S(1)} %get-tuple-element.25), kind=kLoop, calls=%fused_computation.2 | loop fusion | flops 14155776 | bytes 37776388 | tf_op jit(solution)/shard_map/div | solution.py:97
  438.8 0.0 slice-done
  438.8 0.0 slice-done.1
  438.8 0.0 slice-done.2
  438.8 0.0 slice-done.3
  438.8 1.3 slice-done.4
  440.1 0.0 copy-start.1
  440.1 0.0 copy-start.2
  440.1 7.6 %rsqrt_multiply_fusion = f32[6144,768]{1,0:T(8,128)} fusion(f32[6144,768]{1,0:T(8,128)S(1)} %bitcast.13, f32[]{:T(128)S(6)} %div.56, f32[768]{0:T(1024)S(1)} %multiply_add_fusion.4, f32[6144]{0:T(1024)S(1)} %get-tuple-element.23), kind=kLoop, calls=%fused_computation | loop fusion | flops 14155776 | bytes 37776388 | tf_op jit(solution)/shard_map/div | solution.py:98
  447.7 0.0 copy-done.1
  447.7 0.0 copy-done.2
  447.7 1.9 fusion.21
  (6 shorter events, 0.0 us)
Async XLA Ops:
  7.2 95.0 %reduce-scatter.9.cloned.1.call-start = ((), (), s32[]{:S(2)}) async-start(), calls=%async_computation.7 | async-start | bytes 7077888 | tf_op jit(solution)/shard_map/reduce_scatter | solution.py:56
  21.0 10.8 %copy-start = (bf16[128,768]{1,0:T(8,128)(2,1)S(1)}, bf16[128,768]{1,0:T(8,128)(2,1)}, u32[]{:S(2)}) copy-start(bf16[128,768]{1,0:T(8,128)(2,1)} %param.9) | copy-start | bytes 589828
  21.0 26.6 %copy-start.3 = (f32[768]{0:T(1024)S(1)}, f32[768]{0:T(1024)}, u32[]{:S(2)}) copy-start(f32[768]{0:T(1024)} %param.10) | copy-start | bytes 9220
  31.8 141.5 %reduce-scatter.5.cloned.1.call-start = ((), (), s32[]{:S(2)}) async-start(), calls=%async_computation.4 | async-start | bytes 7077888 | tf_op jit(solution)/shard_map/reduce_scatter | solution.py:38
  68.6 171.3 %all-gather.5.cloned.1.call-start = ((), (), s32[]{:S(2)}) async-start(), calls=%async_computation.8 | async-start | bytes 7077888 | tf_op jit(solution)/shard_map/all_gather | solution.py:64
  176.6 128.8 %all-gather.3.cloned.1.call-start = ((), (), s32[]{:S(2)}) async-start(), calls=%async_computation.5 | async-start | bytes 7077888 | tf_op jit(solution)/shard_map/all_gather | solution.py:45
  177.2 177.1 %reduce-scatter.11.cloned.1.call-start = ((), (), s32[]{:S(2)}) async-start(), calls=%async_computation.9 | async-start | bytes 983040 | tf_op jit(solution)/shard_map/reduce_scatter | solution.py:66
  250.6 197.1 %reduce-scatter.7.cloned.1.call-start = ((), (), s32[]{:S(2)}) async-start(), calls=%async_computation.6 | async-start | bytes 983040 | tf_op jit(solution)/shard_map/reduce_scatter | solution.py:46
  329.5 23.4 %copy-start.6 = (f32[768]{0:T(1024)S(1)}, f32[768]{0:T(1024)}, u32[]{:S(2)}) copy-start(f32[768]{0:T(1024)} %param.14) | copy-start | bytes 9220
  329.5 24.7 %copy-start.7 = (f32[768]{0:T(1024)S(1)}, f32[768]{0:T(1024)}, u32[]{:S(2)}) copy-start(f32[768]{0:T(1024)} %param.17) | copy-start | bytes 9220
  329.6 52.3 %copy-start.4 = (f32[6144]{0:T(1024)S(1)}, f32[6144]{0:T(1024)}, u32[]{:S(2)}) copy-start(f32[6144]{0:T(1024)} %param.15) | copy-start | bytes 73732
  329.6 52.4 %copy-start.5 = (f32[6144]{0:T(1024)S(1)}, f32[6144]{0:T(1024)}, u32[]{:S(2)}) copy-start(f32[6144]{0:T(1024)} %param.16) | copy-start | bytes 73732
  421.4 17.4 %slice-start = ((s8[18874368]{0:T(1024)(128)(4,1)}), s8[4194304]{0:T(1024)(128)(4,1)S(1)}, s32[]{:S(2)}) async-start(s8[18874368]{0:T(1024)(128)(4,1)} %bitcast.12), calls=%async_computation.10 | async-start | bytes 8388608
  421.4 17.4 %slice-start.1 = ((s8[18874368]{0:T(1024)(128)(4,1)}), s8[4194304]{0:T(1024)(128)(4,1)S(1)}, s32[]{:S(2)}) async-start(s8[18874368]{0:T(1024)(128)(4,1)} %bitcast.12), calls=%async_computation.11 | async-start | bytes 8388608
  421.4 17.4 %slice-start.2 = ((s8[18874368]{0:T(1024)(128)(4,1)}), s8[4194304]{0:T(1024)(128)(4,1)S(1)}, s32[]{:S(2)}) async-start(s8[18874368]{0:T(1024)(128)(4,1)} %bitcast.12), calls=%async_computation.12 | async-start | bytes 8388608
  421.4 17.4 %slice-start.3 = ((s8[18874368]{0:T(1024)(128)(4,1)}), s8[4194304]{0:T(1024)(128)(4,1)S(1)}, s32[]{:S(2)}) async-start(s8[18874368]{0:T(1024)(128)(4,1)} %bitcast.12), calls=%async_computation.13 | async-start | bytes 8388608
  421.4 18.7 %slice-start.4 = ((s8[18874368]{0:T(1024)(128)(4,1)}), s8[2097152]{0:T(1024)(128)(4,1)S(1)}, s32[]{:S(2)}) async-start(s8[18874368]{0:T(1024)(128)(4,1)} %bitcast.12), calls=%async_computation.14 | async-start | bytes 4194304
  440.1 7.7 %copy-start.1 = (bf16[128,768]{1,0:T(8,128)(2,1)S(1)}, bf16[128,768]{1,0:T(8,128)(2,1)}, u32[]{:S(2)}) copy-start(bf16[128,768]{1,0:T(8,128)(2,1)} %reduce-scatter.11.cloned.1.call-done) | copy-start | bytes 589828
  440.1 7.7 %copy-start.2 = (bf16[128,768]{1,0:T(8,128)(2,1)S(1)}, bf16[128,768]{1,0:T(8,128)(2,1)}, u32[]{:S(2)}) copy-start(bf16[128,768]{1,0:T(8,128)(2,1)} %param.13) | copy-start | bytes 589828
Sparse Core Ops, SparseCore 0:
  31.9 70.2 reduce-scatter.8
  105.0 68.1 reduce-scatter.4
  176.7 63.1 all-gather.4
  241.9 63.3 all-gather.2
  308.1 24.7 reduce-scatter.10
  335.6 26.4 reduce-scatter.6
where the time goes:
time: 458 us; the launch traced here: 457 us
  waiting for transfers between devices  222 us (48%)
  blocking collectives  113 us (25%)
  matrix products  69.5 us (15%)
  other arithmetic  32.9 us (7%)
  between operations  16.9 us (4%)
    reduce_scatter x1, waiting for transfers between devices, body(): lax.psum_scatter(jnp.dot(normed_full, weight_in, preferred_element_type=j...  71.1 us
    all_gather x1, waiting for transfers between devices, body(): act_full = lax.all_gather(act_grad, 'gx', axis=0, tiled=True)  62.7 us
    all_gather x1, waiting for transfers between devices, body(): hidden_full = lax.all_gather(hidden, 'gx', axis=0, tiled=True)  54.6 us
    dot_general x4, matrix products, contract(): lax.dot_general(left, right, (((left_dim,), (right_dim,)), ((), ())), pre...  48.2 us
    psum x1, blocking collectives, body(): lax.psum((jnp.sum(row_in_new) / lax.axis_size('gy'), jnp.sum(row_out_new)...  36.9 us
    reduce_scatter x1, waiting for transfers between devices, body(): lax.psum_scatter(contract(upstream_full, weight_out, 1, 1).astype(jnp.bfl...  33.5 us
    psum x1, blocking collectives, body(): lax.psum((jnp.sum(scaled, axis=1), jnp.sum(scaled * unit, axis=1)), 'gx')  26.4 us
    div x1, other arithmetic, body(): grad_in / jnp.sqrt(row_in_new[:, None] * col_in_new[None, :] / mean_in)  17.4 us
  transfers between devices with their start and end apart: 6, of which 4 were waited for; matrix products, arithmetic and copies ran while one was open for 19% of the time, Pallas kernels for 0%

commit v1 on v0

v1 whole, which is shorter than its diff:
```python
import functools

import jax
import jax.numpy as jnp
from jax import lax
from jax.experimental import pallas as pl
from jax.experimental.pallas import tpu as pltpu
from jax.sharding import PartitionSpec as P

F32 = jnp.float32
BF16 = jnp.bfloat16
VMEM = 58 * 2**20
RUNS = (12,)


def block(total, limit):
    best = 128
    for width in range(128, min(total, limit) + 1, 128):
        if total % width == 0:
            best = width
    return best


def launch(kernel, grid, in_specs, out_specs, out_shape, args, after=(), carry=(), name="kernel"):
    many = isinstance(out_shape, list)
    shapes = out_shape if many else [out_shape]
    specs = out_specs if many else [out_specs]
    hidden = len(after) + len(carry)
    idle = [pl.BlockSpec(memory_space=pl.ANY)]

    def wrapped(*refs):
        inputs, rest = refs[: len(args)], refs[len(args) + hidden :]
        kernel(*inputs, *rest[: len(shapes)])

    results = pl.pallas_call(
        wrapped,
        grid=grid,
        in_specs=list(in_specs) + idle * hidden,
        out_specs=specs + idle * len(carry),
        out_shape=shapes + [jax.ShapeDtypeStruct(c.shape, c.dtype) for c in carry],
        input_output_aliases={len(args) + len(after) + n: len(shapes) + n for n in range(len(carry))},
        compiler_params=pltpu.CompilerParams(vmem_limit_bytes=VMEM),
        cost_estimate=pl.CostEstimate(flops=0, bytes_accessed=0, transcendentals=0),
        name=name,
    )(*args, *after, *carry)
    own = results[: len(shapes)]
    return (list(own) if many else own[0]), list(results[len(shapes) :])


def aligned(width, start, limit):
    step = block(width, limit)
    while start % step:
        step = block(width, step - 128)
    return step, start // step


def project(rows, weight, start, width, dim, after=(), carry=(), limit=1536):
    count, depth = rows.shape
    step, first = aligned(width, start, limit)

    def kernel(x, w, o):
        dims = (((1,), (dim,)), ((), ()))
        o[...] = lax.dot_general(x[...], w[...], dims, preferred_element_type=F32).astype(o.dtype)

    if dim == 0:
        spec = pl.BlockSpec((depth, step), lambda i: (0, first + i))
    else:
        spec = pl.BlockSpec((step, depth), lambda i: (first + i, 0))
    return launch(
        kernel,
        (width // step,),
        [pl.BlockSpec((count, depth), lambda i: (0, 0)), spec],
        pl.BlockSpec((count, step), lambda i: (0, i)),
        jax.ShapeDtypeStruct((count, width), BF16),
        (rows, weight),
        after,
        carry,
        name="project",
    )


def parts_specs(parts, which, step, index):
    blocks, _, rows, _ = parts[0].shape
    return [pl.BlockSpec((blocks, 1, rows, step), lambda i: (0, which, 0, index(i)))] * len(parts)


def whole_rows(refs):
    blocks, _, rows, step = refs[0].shape
    whole = [r[:, 0].reshape(blocks * rows, step) for r in refs]
    return whole[0] if len(whole) == 1 else jnp.concatenate(whole)


def consume(parts, which, left, weight, start, dim, before=None, after=(), carry=(), limit=1536):
    depth, count = left.shape
    width = parts[0].shape[3]
    step, first = aligned(width, start, limit)
    earlier = () if before is None else tuple(before)

    def kernel(x, w, *rest):
        prior, (cols, lanes, product) = rest[len(parts) : -3], rest[-3:]
        a = whole_rows(rest[: len(parts)])
        g = jnp.dot(x[...], a, preferred_element_type=F32)
        s = g * g
        cols[...] = jnp.sum(s, axis=0, keepdims=True)
        folded = s[:, :128]
        for j in range(1, step // 128):
            folded += s[:, j * 128 : (j + 1) * 128]
        part = lax.dot_general(a, w[...], (((1,), (dim,)), ((), ())), preferred_element_type=F32)

        @pl.when(pl.program_id(0) == 0)
        def _():
            lanes[...] = folded + prior[0][...] if prior else folded
            product[...] = part + prior[1][...] if prior else part

        @pl.when(pl.program_id(0) != 0)
        def _():
            lanes[...] += folded
            product[...] += part

    if dim == 0:
        spec = pl.BlockSpec((step, depth), lambda i: (first + i, 0))
    else:
        spec = pl.BlockSpec((depth, step), lambda i: (0, first + i))
    lane_spec = pl.BlockSpec((depth, 128), lambda i: (0, 0))
    product_spec = pl.BlockSpec((count, depth), lambda i: (0, 0))
    return launch(
        kernel,
        (width // step,),
        [pl.BlockSpec((depth, count), lambda i: (0, 0)), spec]
        + parts_specs(parts, which, step, lambda i: i)
        + ([lane_spec, product_spec] if earlier else []),
        [pl.BlockSpec((1, step), lambda i: (0, i)), lane_spec, product_spec],
        [
            jax.ShapeDtypeStruct((1, width), F32),
            jax.ShapeDtypeStruct((depth, 128), F32),
            jax.ShapeDtypeStruct((count, depth), F32),
        ],
        (left, weight, *parts, *earlier),
        after,
        carry,
        name="consume",
    )


def gelu(pre):
    phi = 0.5 * (1.0 + lax.erf(pre * 0.7071067811865476))
    slope = phi + pre * jnp.exp(-0.5 * pre * pre) * 0.3989422804014327
    return pre * phi, slope


def activate(pre, grad=None, after=(), carry=()):
    rows, width = pre.shape
    step = block(width, 1024)

    def kernel(p, *refs):
        value, slope = gelu(p[...].astype(F32))
        if grad is None:
            refs[0][0] = value.astype(BF16)
            refs[1][...] = slope
        else:
            refs[1][0] = value.astype(BF16)
            refs[1][1] = (refs[0][...].astype(F32) * slope).astype(BF16)

    spec = pl.BlockSpec((rows, step), lambda i: (0, i))
    kinds = 1 if grad is None else 2
    out_specs = [pl.BlockSpec((kinds, rows, step), lambda i: (0, 0, i))]
    out_shape = [jax.ShapeDtypeStruct((kinds, rows, width), BF16)]
    if grad is None:
        out_specs, out_shape = out_specs + [spec], out_shape + [jax.ShapeDtypeStruct((rows, width), F32)]
    return launch(
        kernel,
        (width // step,),
        [spec] if grad is None else [spec, spec],
        out_specs,
        out_shape,
        (pre,) if grad is None else (pre, grad),
        after,
        carry,
        name="activate",
    )


def write_update(side, pieces, row_scale, col_scale, hidden_rows, after=(), carry=(), limit=1024):
    widths = [parts[0].shape[3] for parts, _ in pieces]
    per = len(pieces[0][0])
    step = block(functools.reduce(gcd, widths), limit)
    counts = [w // step for w in widths]
    offsets = [sum(counts[:n]) for n in range(len(counts))]
    total = sum(widths)
    features = side.shape[1] if hidden_rows else side.shape[0]

    def kernel(*refs):
        x, acts, rows, cols, o = refs[0], refs[1 : 1 + per * len(pieces)], refs[-3], refs[-2], refs[-1]
        i = pl.program_id(0)
        for n, (first, blocks) in enumerate(zip(offsets, counts)):

            @pl.when(jnp.logical_and(i >= first, i < first + blocks))
            def _(n=n):
                a = whole_rows(acts[n * per : (n + 1) * per])
                if hidden_rows:
                    g = lax.dot_general(a, x[...], (((0,), (0,)), ((), ())), preferred_element_type=F32)
                    tall = jnp.transpose(jnp.broadcast_to(rows[...], (8, step)))[:, :1]
                    o[...] = g * tall * cols[...]
                else:
                    g = jnp.dot(x[...], a, preferred_element_type=F32)
                    o[...] = g * rows[...] * cols[...]

    def place(n):
        return lambda i: jnp.clip(i - offsets[n], 0, counts[n] - 1)

    if hidden_rows:
        scale_specs = [pl.BlockSpec((1, step), lambda i: (0, i)), pl.BlockSpec((1, features), lambda i: (0, 0))]
        out_spec = pl.BlockSpec((step, features), lambda i: (i, 0))
        shape = (total, features)
    else:
        scale_specs = [pl.BlockSpec((features, 1), lambda i: (0, 0)), pl.BlockSpec((1, step), lambda i: (0, i))]
        out_spec = pl.BlockSpec((features, step), lambda i: (0, i))
        shape = (features, total)
    piece_specs = [s for n, (parts, which) in enumerate(pieces) for s in parts_specs(parts, which, step, place(n))]
    return launch(
        kernel,
        (total // step,),
        [pl.BlockSpec(side.shape, lambda i: (0, 0))] + piece_specs + scale_specs,
        out_spec,
        jax.ShapeDtypeStruct(shape, F32),
        (side, *[a for parts, _ in pieces for a in parts], row_scale, col_scale),
        after,
        carry,
        name="write_update",
    )


def gcd(a, b):
    while b:
        a, b = b, a % b
    return a


def power_of_two(size):
    return size & (size - 1) == 0


def all_sum(value, axis, during=()):
    size = lax.axis_size(axis)
    if not power_of_two(size):
        return lax.psum(value, axis)
    bit, turn = 1, 0
    while bit < size:
        arrived = lax.ppermute(value, axis, [(i, i ^ bit) for i in range(size)])
        if turn < len(during):
            value = during[turn](value)
        value = value + arrived
        bit, turn = bit * 2, turn + 1
    return value


def gather_rows(share, axis):
    size = lax.axis_size(axis)
    if not power_of_two(size):
        return lax.all_gather(share, axis, axis=0, tiled=True)
    blocks = [share]
    for bits in range(1, size):
        blocks.append(lax.ppermute(share, axis, [(i, i ^ bits) for i in range(size)]))
    return jnp.concatenate(blocks)


def scatter_rows(partial, axis):
    size = lax.axis_size(axis)
    if not power_of_two(size):
        return lax.psum_scatter(partial, axis, scatter_dimension=0, tiled=True).astype(F32)
    share = partial.shape[0] // size
    total = partial[:share].astype(F32)
    for bits in range(1, size):
        part = partial[bits * share : (bits + 1) * share]
        total = total + lax.ppermute(part, axis, [(i, i ^ bits) for i in range(size)]).astype(F32)
    return total


def body(patches, ln_gain, weight_in, weight_out, upstream, row_in, col_in, row_out, col_out):
    gx, gy = lax.axis_size("gx"), lax.axis_size("gy")
    width = weight_in.shape[1]
    features = patches.shape[1]
    model, hidden_units = features * gx, width * gy
    widths = [width * n // 12 for n in RUNS]
    starts = [sum(widths[:n]) for n in range(len(widths))]

    state = [lax.axis_index("gx").astype(jnp.int32)[None]]

    def run(function, *args, **kwargs):
        results, carried = function(*args, carry=[state[0]], **kwargs)
        state[0] = carried[0]
        return results

    def share_sum(partial):
        return lax.psum_scatter(partial, "gx", scatter_dimension=0, tiled=True)

    up_full = gather_rows(upstream, "gy")
    x_float = patches.astype(F32)
    stats = all_sum(jnp.stack([jnp.sum(x_float, axis=1), jnp.sum(x_float * x_float, axis=1)]), "gx") / model
    row_mean = stats[0][:, None]
    inv_std = lax.rsqrt(stats[1][:, None] - row_mean * row_mean + 1e-06)
    unit = (x_float - row_mean) * inv_std
    normed = (unit * ln_gain[None, :]).astype(BF16)
    normed_full = gather_rows(normed, "gy")

    grad = share_sum(run(project, up_full, weight_out, 0, width, 1))
    pre = share_sum(run(project, normed_full, weight_in, 0, width, 0))
    up_side, normed_side = up_full.T, normed_full.T

    def all_rows(share):
        return [lax.all_gather(share, "gx", axis=0)]

    outer = {"pieces": [], "cols": [], "sums": None}
    inner = {"pieces": [], "cols": [], "sums": None}

    def take(side, parts, left, weight, start, dim):
        cols, lanes, product = run(consume, parts, 0, left, weight, start, dim, side["sums"])
        side["pieces"].append((parts, 0))
        side["cols"].append(cols[0])
        side["sums"] = (lanes, product)

    hidden, slope = run(activate, pre)
    hidden_parts = all_rows(hidden)
    act = (grad.astype(F32) * slope).astype(BF16)[None]
    act_parts = [all_rows(act[:, :, s : s + w]) for s, w in zip(starts, widths)]
    take(outer, hidden_parts, up_side, weight_out, 0, 0)

    def factors(feature_sum, hidden_sum, grand, along_features, along_hidden):
        feature_new = 0.9 * along_features + 0.1 * (feature_sum / hidden_units + 1e-30)
        hidden_new = 0.9 * along_hidden + 0.1 * (hidden_sum / model + 1e-30)
        return feature_new, hidden_new, 0.1 * (grand / model / hidden_units + 1e-30)

    def lane_sums(lanes, extra):
        feature_sum = jnp.sum(lanes, axis=1)
        return jnp.concatenate([feature_sum, jnp.full((64,), jnp.sum(feature_sum)), jnp.full((64,), extra)])

    lanes, branch = outer["sums"]
    feature_sum = all_sum(lane_sums(lanes, jnp.sum(row_out)), "gy")
    hidden_sum = all_sum(jnp.concatenate(outer["cols"] + [feature_sum[features:]]), "gx")
    col_out_new, row_out_new, mean_out = factors(feature_sum[:features], hidden_sum[:width], hidden_sum[width], col_out, row_out)
    mean_out = 0.9 * (feature_sum[features + 64] / hidden_units) + mean_out
    row_scale, col_scale = (lax.rsqrt(row_out_new) * jnp.sqrt(mean_out))[None, :], lax.rsqrt(col_out_new)[None, :]
    output = (x_float + scatter_rows(branch.astype(BF16), "gy")).astype(BF16)

    update_out = run(write_update, up_full, outer["pieces"], row_scale, col_scale, True, after=[output])

    for parts, start in zip(act_parts, starts):
        take(inner, parts, normed_side, weight_in, start, 1)
    lanes, normed_grad = inner["sums"]
    feature_sum = all_sum(lane_sums(lanes, 0.0), "gy")
    scaled = scatter_rows(normed_grad.astype(BF16), "gy") * ln_gain[None, :]
    norm_sums = [jnp.sum(scaled, axis=1), jnp.sum(scaled * unit, axis=1)]
    hidden_sum = jnp.concatenate(inner["cols"] + [feature_sum[features:], jnp.full((128,), jnp.sum(row_in))] + norm_sums)
    hidden_sum = all_sum(hidden_sum, "gx")
    row_in_new, col_in_new, mean_in = factors(feature_sum[:features], hidden_sum[:width], hidden_sum[width], row_in, col_in)
    mean_in = 0.9 * (hidden_sum[width + 128] / model) + mean_in
    row_scale, col_scale = lax.rsqrt(row_in_new)[:, None], (lax.rsqrt(col_in_new) * jnp.sqrt(mean_in))[None, :]
    update_in = run(write_update, normed_side, inner["pieces"], row_scale, col_scale, False)
    means = hidden_sum[width + 256 :].reshape(2, -1, 1) / model
    input_grad = upstream.astype(F32) + inv_std * (scaled - means[0] - unit * means[1])
    return (output, input_grad, update_in, update_out)


def solution(mesh):
    in_specs = (
        P("gy", "gx"),
        P("gx"),
        P("gx", "gy"),
        P("gy", "gx"),
        P("gy", "gx"),
        P("gx"),
        P("gy"),
        P("gy"),
        P("gx"),
    )
    out_specs = (P("gy", "gx"), P("gy", "gx"), P("gx", "gy"), P("gy", "gx"))
    return jax.shard_map(body, mesh=mesh, in_specs=in_specs, out_specs=out_specs, check_vma=False)
```

time: 458 us -> 394 us (0.86)
  blocking collectives: 113 us -> 0 us
  Pallas kernels: 0 us -> 85.8 us
  matrix products: 69.5 us -> 0 us
  starting transfers between devices: 0.42 us -> 28.5 us
  other arithmetic: 32.9 us -> 11.3 us
  local copies, waits for them, and re-layouts: 1.32 us -> 16.6 us
  waiting for transfers between devices: 222 us -> 234 us
    psum x4 -> x0, blocking collectives: 89.1 us -> none  [the longest x1 36.9 us: body(): lax.psum((jnp.sum(row_in_new) / lax.axis_size('gy'), jnp.sum(row_out_new)...]
    pallas_call x0 -> x7, Pallas kernels: none -> 85.8 us  [launch(): pl.pallas_call(wrapped, grid=grid, in_specs=list(in_specs) + idle * hidde...]
    dot_general x6 -> x0, matrix products: 69.5 us -> none  [the longest x4 48.2 us: contract(): lax.dot_general(left, right, (((left_dim,), (right_dim,)), ((), ())), pre...]
    all_gather x2, waiting for transfers between devices: 117 us -> 67.2 us  [all_rows(): return [lax.all_gather(share, 'gx', axis=0)]]
    ppermute x0 -> x25, waiting for transfers between devices: none -> 31.1 us  [the longest x13 23.6 us: all_sum(): arrived = lax.ppermute(value, axis, [(i, i ^ bit) for i in range(size)])]
    reduce_scatter x4 -> x2, waiting for transfers between devices: 105 us -> 135 us  [share_sum(): return lax.psum_scatter(partial, 'gx', scatter_dimension=0, tiled=True)]
    ppermute x0 -> x25, starting transfers between devices: none -> 28.2 us  [the longest x13 13.2 us: all_sum(): arrived = lax.ppermute(value, axis, [(i, i ^ bit) for i in range(size)])]
    div x4 -> x2, other arithmetic: 25 us -> 0.01 us  [the longest x1 0.01 us: body(): means = hidden_sum[width + 256:].reshape(2, -1, 1) / model]
  transfers between devices with their start and end apart: 6 -> 29, of which waited for: 4 -> 17; matrix products, arithmetic and copies ran while one was open for 19% -> 5% of each run, Pallas kernels for 0% -> 12%
where the time goes in v1:
time: 394 us; the launch traced here: 393 us
  waiting for transfers between devices  234 us (59%)
  Pallas kernels  85.8 us (22%)
  starting transfers between devices  28.5 us (7%)
  between operations  16.7 us (4%)
  local copies, waits for them, and re-layouts  16.6 us (4%)
  other arithmetic  11.3 us (3%)
    reduce_scatter x2, waiting for transfers between devices, share_sum(): return lax.psum_scatter(partial, 'gx', scatter_dimension=0, tiled=True)  135 us
    pallas_call x7, Pallas kernels, launch(): pl.pallas_call(wrapped, grid=grid, in_specs=list(in_specs) + idle * hidde...  85.8 us
    all_gather x2, waiting for transfers between devices, all_rows(): return [lax.all_gather(share, 'gx', axis=0)]  67.2 us
    ppermute x13, waiting for transfers between devices, all_sum(): arrived = lax.ppermute(value, axis, [(i, i ^ bit) for i in range(size)])  23.6 us
    ppermute x13, starting transfers between devices, all_sum(): arrived = lax.ppermute(value, axis, [(i, i ^ bit) for i in range(size)])  13.2 us
    ppermute x6, starting transfers between devices, gather_rows(): lax.ppermute(share, axis, [(i, i ^ bits) for i in range(size)])  7.95 us
  transfers between devices with their start and end apart: 29, of which 17 were waited for; matrix products, arithmetic and copies ran while one was open for 5% of the time, Pallas kernels for 12%

profile of v1, /device:TPU:0, one launch (start us, length us, event | category | flops | bytes accessed | tf_op | source)
XLA Modules:
  0.0 392.6 jit_solution(8897481121060202567)
XLA Ops:
  7.2 1.1 copy.39
  8.9 0.8 collective-permute-done.3
  9.8 3.0 collective-permute-start.4
  12.7 2.4 collective-permute-start.2
  16.2 2.7 collective-permute-start.5
  18.9 0.9 constant_dynamic-update-slice_fusion.3
  19.8 0.9 collective-permute-done.5
  20.8 0.9 fusion.5
  21.7 2.5 collective-permute-start.8
  24.7 1.3 collective-permute-done
  25.9 1.4 collective-permute-start.6
  27.5 0.9 copy-done
  28.4 10.2 %project.2 = (bf16[512,6144]{1,0:T(8,128)(2,1)}, s32[1]{0:T(128)}) custom-call(bf16[512,768]{1,0:T(8,128)(2,1)} %copy-done, bf16[6144,768]{1,0:T(8,128)(2,1)} %refs_1_.6, s32[1]{0:T(128)} %bitcast.5.refs_2_), custom_call_target="tpu_custom_call", output_to_operand_aliasing={{1}: (2, {})} | custom-call | tf_op jit(solution)/shard_map/project/pallas_call | solution.py:35
  38.6 1.1 fusion.27
  39.7 1.2 copy.40.refs_0_
  40.8 10.7 %project.3 = (bf16[512,6144]{1,0:T(8,128)(2,1)}, s32[1]{0:T(128)}) custom-call(bf16[512,768]{1,0:T(8,128)(2,1)} %copy.40.refs_0_, bf16[768,6144]{1,0:T(8,128)(2,1)} %refs_1_.7, s32[1]{0:T(128)} %get-tuple-element.22.refs_2_), custom_call_target="tpu_custom_call", output_to_operand_aliasing={{1}: (2, {})} | custom-call | tf_op jit(solution)/shard_map/project/pallas_call | solution.py:35
  51.6 0.7 reduce-scatter.5.cloned.1.call-update
  52.3 69.6 %reduce-scatter.3.cloned.1.call-done.refs_0_ = bf16[64,6144]{1,0:T(8,128)(2,1)} async-done(((bf16[512,6144]{1,0:T(8,128)(2,1)}), bf16[64,6144]{1,0:T(8,128)(2,1)}) %reduce-scatter.3.cloned.1.call-update) | async-done | bytes 786448 | tf_op jit(solution)/shard_map/reduce_scatter | solution.py:295
  121.9 5.7 %activate.1 = (bf16[1,64,6144]{2,1,0:T(8,128)(2,1)}, f32[64,6144]{1,0:T(8,128)}, s32[1]{0:T(128)}) custom-call(bf16[64,6144]{1,0:T(8,128)(2,1)} %reduce-scatter.3.cloned.1.call-done.refs_0_, s32[1]{0:T(128)} %get-tuple-element.24.refs_1_), custom_call_target="tpu_custom_call", output_to_operand_aliasing={{2}: (1, {})} | custom-call | tf_op jit(solution)/shard_map/activate/pallas_call | solution.py:35
  127.9 65.1 %reduce-scatter.5.cloned.1.call-done = bf16[64,6144]{1,0:T(8,128)(2,1)} async-done(((bf16[512,6144]{1,0:T(8,128)(2,1)}), bf16[64,6144]{1,0:T(8,128)(2,1)}) %reduce-scatter.5.cloned.1.call-update) | async-done | bytes 786448 | tf_op jit(solution)/shard_map/reduce_scatter | solution.py:295
  193.0 2.7 multiply_convert_fusion
  195.7 0.6 reduce_sum.94
  196.4 1.2 copy.41.refs_0_
  197.5 60.3 %all-gather.5.cloned.1.call-done = bf16[8,64,6144]{2,1,0:T(8,128)(2,1)} async-done(((bf16[1,64,6144]{2,1,0:T(8,128)(2,1)}), bf16[8,64,6144]{2,1,0:T(8,128)(2,1)}) %all-gather.5.cloned.1.call-update) | async-done | bytes 6291472 | tf_op jit(solution)/shard_map/all_gather | solution.py:311
  257.8 16.6 %consume.2 = (f32[1,6144]{1,0:T(1,128)}, f32[768,128]{1,0:T(8,128)}, f32[512,768]{1,0:T(8,128)}, s32[1]{0:T(128)}) custom-call(bf16[768,512]{1,0:T(8,128)(2,1)} %copy.41.refs_0_, bf16[6144,768]{1,0:T(8,128)(2,1)} %refs_1_.6, bf16[8,1,64,6144]{3,2,1,0:T(8,128)(2,1)} %bitcast.26, s32[1]{0:T(128)} %get-tuple-element.26.refs_3_), custom_call_target="tpu_custom_call", output_to_operand_aliasing={{3}: (3, {})} | custom-call | tf_op jit(solution)/shard_map/consume/pallas_call | solution.py:35
  274.4 1.8 fusion.29
  276.2 0.6 broadcast_in_dim.34
  276.8 0.6 broadcast_in_dim.33
  277.5 1.5 collective-permute-start.12
  279.0 2.1 collective-permute-done.12
  281.2 1.5 collective-permute-start.13
  282.7 2.1 collective-permute-done.13
  284.8 0.7 pad_maximum_fusion.1
  285.6 1.7 copy.42
  287.5 1.5 collective-permute-start.9
  289.1 1.5 collective-permute-start.10
  291.1 2.7 collective-permute-done.15
  293.8 0.6 slice.89
  295.6 5.1 %collective-permute-done.16 = f32[6272]{0:T(1024)S(1)} collective-permute-done((f32[6272]{0:T(1024)S(1)}, f32[6272]{0:T(1024)S(1)}, u32[]{:S(2)}, u32[]{:S(2)}) %collective-permute-start.16) | collective-permute-done | bytes 25120 | tf_op jit(solution)/shard_map/ppermute | solution.py:249
  301.9 0.6 fusion.20
  302.7 0.8 copy.47.refs_4_
  303.5 13.5 %write_update.2 = (f32[6144,768]{1,0:T(8,128)}, s32[1]{0:T(128)}) custom-call(bf16[512,768]{1,0:T(8,128)(2,1)} %copy-done, bf16[8,1,64,6144]{3,2,1,0:T(8,128)(2,1)} %bitcast.27, f32[1,6144]{1,0:T(1,128)} %bitcast.32, f32[1,768]{1,0:T(1,128)} %broadcast_in_dim.36.refs_3_, bf16[128,768]{1,0:T(8,128)(2,1)} %copy.47.refs_4_, ...), custom_call_target="tpu_custom_call", output_to_operand_aliasing={{1}: (5, {})} | custom-call | tf_op jit(solution)/shard_map/write_update/pallas_call | solution.py:35
  317.1 6.9 %all-gather.7.cloned.1.call-done = bf16[512,6144]{1,0:T(8,128)(2,1)} async-done(((bf16[64,6144]{1,0:T(8,128)(2,1)}), bf16[512,6144]{1,0:T(8,128)(2,1)}) %all-gather.7.cloned.1.call-update) | async-done | bytes 6291472 | tf_op jit(solution)/shard_map/all_gather | solution.py:311
  324.0 15.9 %consume.3 = (f32[1,6144]{1,0:T(1,128)}, f32[768,128]{1,0:T(8,128)}, f32[512,768]{1,0:T(8,128)}, s32[1]{0:T(128)}) custom-call(bf16[768,512]{1,0:T(8,128)(2,1)} %get-tuple-element.64.refs_0_, bf16[768,6144]{1,0:T(8,128)(2,1)} %refs_1_.7, bf16[8,1,64,6144]{3,2,1,0:T(8,128)(2,1)} %bitcast.24, s32[1]{0:T(128)} %get-tuple-element.33.refs_3_), custom_call_target="tpu_custom_call", output_to_operand_aliasing={{3}: (3, {})} | custom-call | tf_op jit(solution)/shard_map/consume/pallas_call | solution.py:35
  339.9 1.7 copy.45
  341.7 0.7 fusion.28
  342.4 0.6 broadcast_in_dim.37
  343.1 1.5 collective-permute-start.20
  344.7 2.0 collective-permute-done.20
  346.8 1.5 collective-permute-start.21
  348.3 1.5 collective-permute-start.17
  350.3 1.5 collective-permute-start.19
  351.8 0.6 add_rsqrt_fusion
  352.4 0.6 constant_dynamic-update-slice_fusion.7
  353.1 2.8 collective-permute-done.17
  355.9 3.4 collective-permute-done.18
  359.6 1.2 collective-permute-done.22
  360.8 3.9 collective-permute-done.23
  364.7 1.0 collective-permute-start.24
  365.9 0.9 broadcast_in_dim.42.refs_2_
  366.8 2.7 collective-permute-done.24
  370.1 0.9 copy.48
  372.3 0.6 fusion.15
  372.9 13.2 %write_update.3 = (f32[768,6144]{1,0:T(8,128)}, s32[1]{0:T(128)}) custom-call(bf16[768,512]{1,0:T(8,128)(2,1)} %get-tuple-element.64.refs_0_, bf16[8,1,64,6144]{3,2,1,0:T(8,128)(2,1)} %bitcast.25, f32[768,1]{1,0:T(8,128)} %broadcast_in_dim.42.refs_2_, f32[1,6144]{1,0:T(1,128)} %bitcast.29, s32[1]{0:T(128)} %get-tuple-element.37.refs_4_), custom_call_target="tpu_custom_call", output_to_operand_aliasing={{1}: (4, {})} | custom-call | tf_op jit(solution)/shard_map/write_update/pallas_call | solution.py:35
  (91 shorter events, 6.8 us)
Async XLA Ops:
  7.2 114.8 %reduce-scatter.3.cloned.1.call-start = ((), (), s32[]{:S(2)}) async-start(), calls=%async_computation.2 | async-start | bytes 7077888 | tf_op jit(solution)/shard_map/reduce_scatter | solution.py:295
  8.4 1.3 collective-permute-start.3
  9.8 6.5 %collective-permute-start.4 = (f32[2,128]{1,0:T(2,128)S(1)}, f32[2,128]{1,0:T(2,128)S(1)}, u32[]{:S(2)}, u32[]{:S(2)}) collective-permute-start(f32[2,128]{1,0:T(2,128)S(1)} %fusion.23), channel_id=1, source_target_pairs={{0,8},{4,12},{8,0},{12,4},{16,24},{20,28},{24,16},{28,20},{1,9},{5... | collective-permute-start | bytes 3080 | tf_op jit(solution)/shard_map/ppermute | solution.py:249
  12.7 14.7 %collective-permute-start.2 = (bf16[128,768]{1,0:T(8,128)(2,1)}, bf16[128,768]{1,0:T(8,128)(2,1)S(1)}, u32[]{:S(2)}, u32[]{:S(2)}) collective-permute-start(bf16[128,768]{1,0:T(8,128)(2,1)} %param.13), channel_id=1, source_target_pairs={{0,3},{1,2},{2,1},{3,0},{4,7},{5,6},{6,5},{7,4},{8,11},{9,10},{10,... | collective-permute-start | bytes 589832 | tf_op jit(solution)/shard_map/ppermute | solution.py:263
  15.2 12.2 %collective-permute-start.1 = (bf16[128,768]{1,0:T(8,128)(2,1)}, bf16[128,768]{1,0:T(8,128)(2,1)S(1)}, u32[]{:S(2)}, u32[]{:S(2)}) collective-permute-start(bf16[128,768]{1,0:T(8,128)(2,1)} %param.13), channel_id=1, source_target_pairs={{0,2},{1,3},{2,0},{3,1},{4,6},{5,7},{6,4},{7,5},{8,10},{9,11},{10,... | collective-permute-start | bytes 589832 | tf_op jit(solution)/shard_map/ppermute | solution.py:263
  15.7 10.3 %collective-permute-start = (bf16[128,768]{1,0:T(8,128)(2,1)}, bf16[128,768]{1,0:T(8,128)(2,1)S(1)}, u32[]{:S(2)}, u32[]{:S(2)}) collective-permute-start(bf16[128,768]{1,0:T(8,128)(2,1)} %param.13), channel_id=1, source_target_pairs={{0,1},{1,0},{2,3},{3,2},{4,5},{5,4},{6,7},{7,6},{8,9},{9,8},{10,11... | collective-permute-start | bytes 589832 | tf_op jit(solution)/shard_map/ppermute | solution.py:263
  16.2 4.5 %collective-permute-start.5 = (f32[2,128]{1,0:T(2,128)S(1)}, f32[2,128]{1,0:T(2,128)S(1)}, u32[]{:S(2)}, u32[]{:S(2)}) collective-permute-start(f32[2,128]{1,0:T(2,128)S(1)} %fusion.34), channel_id=1, source_target_pairs={{0,16},{4,20},{8,24},{12,28},{16,0},{20,4},{24,8},{28,12},{1,17},{... | collective-permute-start | bytes 3080 | tf_op jit(solution)/shard_map/ppermute | solution.py:249
  21.7 16.9 %collective-permute-start.8 = (bf16[128,768]{0,1:T(8,128)(2,1)S(1)}, bf16[128,768]{0,1:T(8,128)(2,1)S(1)}, u32[]{:S(2)}, u32[]{:S(2)}) collective-permute-start(bf16[128,768]{0,1:T(8,128)(2,1)S(1)} %fusion.5), channel_id=1, source_target_pairs={{0,3},{1,2},{2,1},{3,0},{4,7},{5,6},{6,5},{7,4},{8,11},{9,10},{10,... | collective-permute-start | bytes 589832 | tf_op jit(solution)/shard_map/ppermute | solution.py:263
  24.2 14.4 %collective-permute-start.7 = (bf16[128,768]{0,1:T(8,128)(2,1)S(1)}, bf16[128,768]{0,1:T(8,128)(2,1)S(1)}, u32[]{:S(2)}, u32[]{:S(2)}) collective-permute-start(bf16[128,768]{0,1:T(8,128)(2,1)S(1)} %fusion.5), channel_id=1, source_target_pairs={{0,2},{1,3},{2,0},{3,1},{4,6},{5,7},{6,4},{7,5},{8,10},{9,11},{10,... | collective-permute-start | bytes 589832 | tf_op jit(solution)/shard_map/ppermute | solution.py:263
  25.9 12.6 %collective-permute-start.6 = (bf16[128,768]{0,1:T(8,128)(2,1)S(1)}, bf16[128,768]{0,1:T(8,128)(2,1)S(1)}, u32[]{:S(2)}, u32[]{:S(2)}) collective-permute-start(bf16[128,768]{0,1:T(8,128)(2,1)S(1)} %fusion.5), channel_id=1, source_target_pairs={{0,1},{1,0},{2,3},{3,2},{4,5},{5,4},{6,7},{7,6},{8,9},{9,8},{10,11... | collective-permute-start | bytes 589832 | tf_op jit(solution)/shard_map/ppermute | solution.py:263
  27.5 0.9 copy-start
  51.5 141.5 %reduce-scatter.5.cloned.1.call-start = ((), (), s32[]{:S(2)}) async-start(), calls=%async_computation.3 | async-start | bytes 7077888 | tf_op jit(solution)/shard_map/reduce_scatter | solution.py:295
  52.3 205.5 %all-gather.5.cloned.1.call-start = ((), (), s32[]{:S(2)}) async-start(), calls=%async_computation.4 | async-start | bytes 7077888 | tf_op jit(solution)/shard_map/all_gather | solution.py:311
  127.7 196.3 %all-gather.7.cloned.1.call-start = ((), (), s32[]{:S(2)}) async-start(), calls=%async_computation.5 | async-start | bytes 7077888 | tf_op jit(solution)/shard_map/all_gather | solution.py:311
  193.0 2.7 copy-start.4
  193.0 3.3 copy-start.1
  274.4 12.9 %copy-start.5 = (f32[1,6144]{1,0:T(1,128)S(1)}, f32[1,6144]{1,0:T(1,128)}, u32[]{:S(2)}) copy-start(f32[1,6144]{1,0:T(1,128)} %get-tuple-element.30) | copy-start | bytes 73732
  277.5 3.6 collective-permute-start.12
  281.2 3.6 collective-permute-start.13
  285.6 1.7 collective-permute-start.14
  285.6 8.2 %copy-start.9 = (f32[768]{0:T(1024)S(1)}, f32[768]{0:T(1024)}, u32[]{:S(2)}) copy-start(f32[768]{0:T(1024)} %param.17) | copy-start | bytes 9220
  287.3 6.5 %collective-permute-start.15 = (f32[6272]{0:T(1024)S(1)}, f32[6272]{0:T(1024)S(1)}, u32[]{:S(2)}, u32[]{:S(2)}) collective-permute-start(f32[6272]{0:T(1024)S(1)} %fusion.26), channel_id=1, source_target_pairs={{0,8},{4,12},{8,0},{12,4},{16,24},{20,28},{24,16},{28,20},{1,9},{5... | collective-permute-start | bytes 75272 | tf_op jit(solution)/shard_map/ppermute | solution.py:249
  287.5 15.0 %collective-permute-start.9 = (bf16[128,768]{0,1:T(8,128)(2,1)S(1)}, bf16[128,768]{0,1:T(8,128)(2,1)S(1)}, u32[]{:S(2)}, u32[]{:S(2)}) collective-permute-start(bf16[128,768]{0,1:T(8,128)(2,1)S(1)} %get-tuple-element.66), channel_id=1, source_target_pairs={{0,1},{1,0},{2,3},{3,2},{4,5},{5,4},{6,7},{7,6},{8,9},{9,8},{10,11... | collective-permute-start | bytes 589832 | tf_op jit(solution)/shard_map/ppermute | solution.py:275
  289.1 13.5 %collective-permute-start.10 = (bf16[128,768]{0,1:T(8,128)(2,1)S(1)}, bf16[128,768]{0,1:T(8,128)(2,1)S(1)}, u32[]{:S(2)}, u32[]{:S(2)}) collective-permute-start(bf16[128,768]{0,1:T(8,128)(2,1)S(1)} %get-tuple-element.67), channel_id=1, source_target_pairs={{0,2},{1,3},{2,0},{3,1},{4,6},{5,7},{6,4},{7,5},{8,10},{9,11},{10,... | collective-permute-start | bytes 589832 | tf_op jit(solution)/shard_map/ppermute | solution.py:275
  290.5 12.0 %collective-permute-start.11 = (bf16[128,768]{0,1:T(8,128)(2,1)S(1)}, bf16[128,768]{0,1:T(8,128)(2,1)S(1)}, u32[]{:S(2)}, u32[]{:S(2)}) collective-permute-start(bf16[128,768]{0,1:T(8,128)(2,1)S(1)} %get-tuple-element.68), channel_id=1, source_target_pairs={{0,3},{1,2},{2,1},{3,0},{4,7},{5,6},{6,5},{7,4},{8,11},{9,10},{10,... | collective-permute-start | bytes 589832 | tf_op jit(solution)/shard_map/ppermute | solution.py:275
  293.8 6.9 %collective-permute-start.16 = (f32[6272]{0:T(1024)S(1)}, f32[6272]{0:T(1024)S(1)}, u32[]{:S(2)}, u32[]{:S(2)}) collective-permute-start(f32[6272]{0:T(1024)S(1)} %add.134), channel_id=1, source_target_pairs={{0,16},{4,20},{8,24},{12,28},{16,0},{20,4},{24,8},{28,12},{1,17},{... | collective-permute-start | bytes 75272 | tf_op jit(solution)/shard_map/ppermute | solution.py:249
  339.9 1.8 copy-start.3
  339.9 8.4 %copy-start.6 = (f32[1,6144]{1,0:T(1,128)S(1)}, f32[1,6144]{1,0:T(1,128)}, u32[]{:S(2)}) copy-start(f32[1,6144]{1,0:T(1,128)} %get-tuple-element.35) | copy-start | bytes 73732
  339.9 11.9 %copy-start.10 = (f32[768]{0:T(1024)S(1)}, f32[768]{0:T(1024)}, u32[]{:S(2)}) copy-start(f32[768]{0:T(1024)} %param.14) | copy-start | bytes 9220
  339.9 19.4 %copy-start.8 = (f32[768]{0:T(1024)S(1)}, f32[768]{0:T(1024)}, u32[]{:S(2)}) copy-start(f32[768]{0:T(1024)} %param.10) | copy-start | bytes 9220
  341.7 24.1 %copy-start.2 = (bf16[128,768]{1,0:T(8,128)(2,1)S(1)}, bf16[128,768]{1,0:T(8,128)(2,1)}, u32[]{:S(2)}) copy-start(bf16[128,768]{1,0:T(8,128)(2,1)} %param.13) | copy-start | bytes 589828
  343.1 3.6 collective-permute-start.20
  346.8 5.0 %collective-permute-start.21 = (f32[896]{0:T(1024)S(1)}, f32[896]{0:T(1024)S(1)}, u32[]{:S(2)}, u32[]{:S(2)}) collective-permute-start(f32[896]{0:T(1024)S(1)} %fusion.24), channel_id=1, source_target_pairs={{0,2},{1,3},{2,0},{3,1},{4,6},{5,7},{6,4},{7,5},{8,10},{9,11},{10,... | collective-permute-start | bytes 10760 | tf_op jit(solution)/shard_map/ppermute | solution.py:249
  348.3 7.6 %collective-permute-start.17 = (bf16[128,768]{0,1:T(8,128)(2,1)S(1)}, bf16[128,768]{0,1:T(8,128)(2,1)S(1)}, u32[]{:S(2)}, u32[]{:S(2)}) collective-permute-start(bf16[128,768]{0,1:T(8,128)(2,1)S(1)} %get-tuple-element.61), channel_id=1, source_target_pairs={{0,1},{1,0},{2,3},{3,2},{4,5},{5,4},{6,7},{7,6},{8,9},{9,8},{10,11... | collective-permute-start | bytes 589832 | tf_op jit(solution)/shard_map/ppermute | solution.py:275
  349.8 9.6 %collective-permute-start.18 = (bf16[128,768]{0,1:T(8,128)(2,1)S(1)}, bf16[128,768]{0,1:T(8,128)(2,1)S(1)}, u32[]{:S(2)}, u32[]{:S(2)}) collective-permute-start(bf16[128,768]{0,1:T(8,128)(2,1)S(1)} %get-tuple-element.62), channel_id=1, source_target_pairs={{0,2},{1,3},{2,0},{3,1},{4,6},{5,7},{6,4},{7,5},{8,10},{9,11},{10,... | collective-permute-start | bytes 589832 | tf_op jit(solution)/shard_map/ppermute | solution.py:275
  350.3 9.0 %collective-permute-start.19 = (bf16[128,768]{0,1:T(8,128)(2,1)S(1)}, bf16[128,768]{0,1:T(8,128)(2,1)S(1)}, u32[]{:S(2)}, u32[]{:S(2)}) collective-permute-start(bf16[128,768]{0,1:T(8,128)(2,1)S(1)} %get-tuple-element.63), channel_id=1, source_target_pairs={{0,3},{1,2},{2,1},{3,0},{4,7},{5,6},{6,5},{7,4},{8,11},{9,10},{10,... | collective-permute-start | bytes 589832 | tf_op jit(solution)/shard_map/ppermute | solution.py:275
  359.5 12.8 %copy-start.7 = (f32[6144]{0:T(1024)S(1)}, f32[6144]{0:T(1024)}, u32[]{:S(2)}) copy-start(f32[6144]{0:T(1024)} %param.15) | copy-start | bytes 73732
  359.6 1.3 collective-permute-start.22
  360.8 3.9 collective-permute-start.23
  364.7 4.8 %collective-permute-start.24 = (f32[6656]{0:T(1024)S(1)}, f32[6656]{0:T(1024)S(1)}, u32[]{:S(2)}, u32[]{:S(2)}) collective-permute-start(f32[6656]{0:T(1024)S(1)} %add.149), channel_id=1, source_target_pairs={{0,16},{4,20},{8,24},{12,28},{16,0},{20,4},{24,8},{28,12},{1,17},{... | collective-permute-start | bytes 79880 | tf_op jit(solution)/shard_map/ppermute | solution.py:249
Sparse Core Ops, SparseCore 0:
  51.7 70.2 reduce-scatter.2
  124.8 68.1 reduce-scatter.4
  194.7 63.1 all-gather.4
  259.3 64.6 all-gather.6

commit v2 on v1

v2 whole, which is shorter than its diff:
```python
import functools

import jax
import jax.numpy as jnp
from jax import lax
from jax.experimental import pallas as pl
from jax.experimental.pallas import tpu as pltpu
from jax.sharding import PartitionSpec as P

F32 = jnp.float32
BF16 = jnp.bfloat16
VMEM = 58 * 2**20


def block(total, limit):
    best = 128
    for width in range(128, min(total, limit) + 1, 128):
        if total % width == 0:
            best = width
    return best


def launch(kernel, grid, in_specs, out_specs, out_shape, args, after=(), carry=(), scratch=(), flops=0, name="kernel"):
    many = isinstance(out_shape, list)
    shapes = out_shape if many else [out_shape]
    specs = out_specs if many else [out_specs]
    hidden = len(after) + len(carry)
    idle = [pl.BlockSpec(memory_space=pl.ANY)]

    def wrapped(*refs):
        inputs, rest = refs[: len(args)], refs[len(args) + hidden :]
        kernel(*inputs, *rest[: len(shapes)], *rest[len(shapes) + len(carry) :])

    results = pl.pallas_call(
        wrapped,
        grid=grid,
        in_specs=list(in_specs) + idle * hidden,
        out_specs=specs + idle * len(carry),
        out_shape=shapes + [jax.ShapeDtypeStruct(c.shape, c.dtype) for c in carry],
        input_output_aliases={len(args) + len(after) + n: len(shapes) + n for n in range(len(carry))},
        scratch_shapes=list(scratch),
        compiler_params=pltpu.CompilerParams(vmem_limit_bytes=VMEM),
        cost_estimate=pl.CostEstimate(flops=int(flops), bytes_accessed=int(flops / 300), transcendentals=0),
        name=name,
    )(*args, *after, *carry)
    own = results[: len(shapes)]
    return (list(own) if many else own[0]), list(results[len(shapes) :])


def aligned(width, start, limit):
    step = block(width, limit)
    while start % step:
        step = block(width, step - 128)
    return step, start // step


def project(rows, weight, start, width, dim, after=(), carry=(), limit=1536):
    count, depth = rows.shape
    step, first = aligned(width, start, limit)

    def kernel(x, w, o):
        dims = (((1,), (dim,)), ((), ()))
        o[...] = lax.dot_general(x[...], w[...], dims, preferred_element_type=F32).astype(o.dtype)

    if dim == 0:
        spec = pl.BlockSpec((depth, step), lambda i: (0, first + i))
    else:
        spec = pl.BlockSpec((step, depth), lambda i: (first + i, 0))
    return launch(
        kernel,
        (width // step,),
        [pl.BlockSpec((count, depth), lambda i: (0, 0)), spec],
        pl.BlockSpec((count, step), lambda i: (0, i)),
        jax.ShapeDtypeStruct((count, width), BF16),
        (rows, weight),
        after,
        carry,
        flops=4 * count * depth * width,
        name="project",
    )


def parts_specs(parts, which, step, index):
    blocks, _, rows, _ = parts[0].shape
    return [pl.BlockSpec((blocks, 1, rows, step), lambda i: (0, which, 0, index(i)))] * len(parts)


def whole_rows(refs):
    blocks, _, rows, step = refs[0].shape
    whole = [r[:, 0].reshape(blocks * rows, step) for r in refs]
    return whole[0] if len(whole) == 1 else jnp.concatenate(whole)


def consume(parts, left, weight, dim, after=(), carry=(), limit=2048):
    depth, count = left.shape
    width = parts[0].shape[3]
    step = block(width, limit)

    def kernel(x, w, *rest):
        cols, feature, product, lanes, total = rest[-5:]
        a = whole_rows(rest[:-5])
        g = jnp.dot(x[...], a, preferred_element_type=F32)
        s = g * g
        cols[...] = jnp.sum(s, axis=0, keepdims=True)
        folded = s[:, :128]
        for j in range(1, step // 128):
            folded += s[:, j * 128 : (j + 1) * 128]
        part = lax.dot_general(a, w[...], (((1,), (dim,)), ((), ())), preferred_element_type=F32)

        @pl.when(pl.program_id(0) == 0)
        def _():
            lanes[...] = folded
            total[...] = part

        @pl.when(pl.program_id(0) != 0)
        def _():
            lanes[...] += folded
            total[...] += part

        @pl.when(pl.program_id(0) == width // step - 1)
        def _():
            row = jnp.sum(jnp.transpose(lanes[...]), axis=0, keepdims=True)
            feature[:, :depth] = jnp.broadcast_to(row, (8, depth))
            feature[:, depth:] = jnp.broadcast_to(jnp.sum(row, axis=1, keepdims=True), (8, 128))
            product[...] = total[...].astype(BF16)

    spec = pl.BlockSpec((step, depth), lambda i: (i, 0)) if dim == 0 else pl.BlockSpec((depth, step), lambda i: (0, i))
    return launch(
        kernel,
        (width // step,),
        [pl.BlockSpec((depth, count), lambda i: (0, 0)), spec] + parts_specs(parts, 0, step, lambda i: i),
        [
            pl.BlockSpec((1, step), lambda i: (0, i)),
            pl.BlockSpec((8, depth + 128), lambda i: (0, 0)),
            pl.BlockSpec((count, depth), lambda i: (0, 0)),
        ],
        [
            jax.ShapeDtypeStruct((1, width), F32),
            jax.ShapeDtypeStruct((8, depth + 128), F32),
            jax.ShapeDtypeStruct((count, depth), BF16),
        ],
        (left, weight, *parts),
        after,
        carry,
        scratch=[pltpu.VMEM((depth, 128), F32), pltpu.VMEM((count, depth), F32)],
        flops=8 * count * depth * width,
        name="consume",
    )


def gelu(pre):
    phi = 0.5 * (1.0 + lax.erf(pre * 0.7071067811865476))
    slope = phi + pre * jnp.exp(-0.5 * pre * pre) * 0.3989422804014327
    return pre * phi, slope


def activate(pre, grad, after=(), carry=()):
    rows, width = pre.shape
    step = block(width, 3072)

    def kernel(p, g, hidden, act):
        value, slope = gelu(p[...].astype(F32))
        hidden[0] = value.astype(BF16)
        act[0] = (g[...].astype(F32) * slope).astype(BF16)

    spec = pl.BlockSpec((rows, step), lambda i: (0, i))
    return launch(
        kernel,
        (width // step,),
        [spec, spec],
        [pl.BlockSpec((1, rows, step), lambda i: (0, 0, i))] * 2,
        [jax.ShapeDtypeStruct((1, rows, width), BF16)] * 2,
        (pre, grad),
        after,
        carry,
        flops=1e9,
        name="activate",
    )


def write_update(side, parts, feature_sum, hidden_sums, before, sizes, hidden_rows, after=(), carry=(), limit=1536):
    total = parts[0].shape[3]
    step = block(total, limit)
    features = side.shape[1] if hidden_rows else side.shape[0]
    model, hidden_units = sizes

    def tall(row):
        return jnp.transpose(jnp.broadcast_to(row, (8, row.shape[1])))[:, :1]

    def kernel(x, *rest):
        across, near_sum, far_sum, near_all, far_all, feature_before, hidden_before, mean_before, o = rest[-9:]
        a = whole_rows(rest[:-9])
        if hidden_rows:
            g = lax.dot_general(a, x[...], (((0,), (0,)), ((), ())), preferred_element_type=F32)
        else:
            g = jnp.dot(x[...], a, preferred_element_type=F32)
        grand = (near_all[:, :1] + far_all[:, :1]) / model / hidden_units + 1e-30
        mean = 0.9 * mean_before[:, :1] + 0.1 * grand
        by_feature = 0.9 * feature_before[...] + 0.1 * (across[:1, :features] / hidden_units + 1e-30)
        by_hidden = 0.9 * hidden_before[...] + 0.1 * ((near_sum[...] + far_sum[...]) / model + 1e-30)
        by_feature = lax.rsqrt(by_feature) * jnp.sqrt(mean)
        by_hidden = lax.rsqrt(by_hidden)
        if hidden_rows:
            o[...] = g * tall(by_hidden) * by_feature
        else:
            o[...] = g * tall(by_feature) * by_hidden

    along_hidden = pl.BlockSpec((1, step), lambda i: (0, i))
    behind = pl.BlockSpec((1, 128), lambda i: (0, total // 128))
    scale_specs = [
        pl.BlockSpec((8, features + 128), lambda i: (0, 0)),
        along_hidden,
        along_hidden,
        behind,
        behind,
        pl.BlockSpec((1, features), lambda i: (0, 0)),
        along_hidden,
        pl.BlockSpec((1, 128), lambda i: (0, 0)),
    ]
    if hidden_rows:
        out_spec = pl.BlockSpec((step, features), lambda i: (i, 0))
        shape = (total, features)
    else:
        out_spec = pl.BlockSpec((features, step), lambda i: (0, i))
        shape = (features, total)
    return launch(
        kernel,
        (total // step,),
        [pl.BlockSpec(side.shape, lambda i: (0, 0))] + parts_specs(parts, 0, step, lambda i: i) + scale_specs,
        out_spec,
        jax.ShapeDtypeStruct(shape, F32),
        (side, *parts, feature_sum, *hidden_sums, *hidden_sums, *before),
        after,
        carry,
        flops=3000 * features * total,
        name="write_update",
    )


def power_of_two(size):
    return size & (size - 1) == 0


def all_sum(value, axis, split=False):
    size = lax.axis_size(axis)
    if not power_of_two(size):
        value = lax.psum(value, axis)
        return (value, jnp.zeros_like(value)) if split else value
    bit = 1
    while bit < size:
        count = min(4, size // bit)
        arrived = [lax.ppermute(value, axis, [(i, i ^ (bit * n)) for i in range(size)]) for n in range(1, count)]
        bit *= count
        if split and bit >= size:
            return functools.reduce(jnp.add, arrived[1:], value), arrived[0]
        value = functools.reduce(jnp.add, arrived, value)
    return (value, jnp.zeros_like(value)) if split else value


def gather_rows(share, axis):
    size = lax.axis_size(axis)
    if not power_of_two(size):
        return lax.all_gather(share, axis, axis=0, tiled=True)
    blocks = [share]
    for bits in range(1, size):
        blocks.append(lax.ppermute(share, axis, [(i, i ^ bits) for i in range(size)]))
    return jnp.concatenate(blocks)


def scatter_rows(partial, axis):
    size = lax.axis_size(axis)
    if not power_of_two(size):
        return lax.psum_scatter(partial, axis, scatter_dimension=0, tiled=True).astype(F32)
    share = partial.shape[0] // size
    total = partial[:share].astype(F32)
    for bits in range(1, size):
        part = partial[bits * share : (bits + 1) * share]
        total = total + lax.ppermute(part, axis, [(i, i ^ bits) for i in range(size)]).astype(F32)
    return total


def body(patches, ln_gain, weight_in, weight_out, upstream, row_in, col_in, row_out, col_out):
    gx, gy = lax.axis_size("gx"), lax.axis_size("gy")
    width = weight_in.shape[1]
    features = patches.shape[1]
    model, hidden_units = features * gx, width * gy

    state = [lax.axis_index("gx").astype(jnp.int32)[None]]

    def run(function, *args, **kwargs):
        results, carried = function(*args, carry=[state[0]], **kwargs)
        state[0] = carried[0]
        return results

    def share_sum(partial):
        return lax.psum_scatter(partial, "gx", scatter_dimension=0, tiled=True)

    up_full = gather_rows(upstream, "gy")
    x_float = patches.astype(F32)
    stats = all_sum(jnp.stack([jnp.sum(x_float, axis=1), jnp.sum(x_float * x_float, axis=1)]), "gx") / model
    row_mean = stats[0][:, None]
    inv_std = lax.rsqrt(stats[1][:, None] - row_mean * row_mean + 1e-06)
    unit = (x_float - row_mean) * inv_std
    normed = (unit * ln_gain[None, :]).astype(BF16)
    normed_full = gather_rows(normed, "gy")

    grad = share_sum(run(project, up_full, weight_out, 0, width, 1))
    pre = share_sum(run(project, normed_full, weight_in, 0, width, 0))
    up_side, normed_side = up_full.T, normed_full.T

    def all_rows(share):
        return [lax.all_gather(share, "gx", axis=0)]

    outer = {"pieces": [], "cols": [], "sums": None}
    inner = {"pieces": [], "cols": [], "sums": None}

    def take(side, parts, left, weight, start, dim):
        cols, lanes, product = run(consume, parts, 0, left, weight, start, dim, side["sums"])
        side["pieces"].append((parts, 0))
        side["cols"].append(cols[0])
        side["sums"] = (lanes, product)

    hidden, act = run(activate, pre, grad)
    act_parts, hidden_parts = all_rows(act), all_rows(hidden)

    def mean_of(factor, axis):
        return jnp.full((1, 128), all_sum(jnp.full((128,), jnp.sum(factor)), axis)[0] / (factor.shape[0] * lax.axis_size(axis)))

    mean_in, mean_out = mean_of(row_in, "gx"), mean_of(row_out, "gy")
    sizes = (float(model), float(hidden_units))

    hidden_sum, feature_sum, normed_grad = run(consume, act_parts, normed_side, weight_in, 1, after=[mean_in, mean_out])
    feature_sum = all_sum(feature_sum, "gy")
    scaled = scatter_rows(normed_grad, "gy") * ln_gain[None, :]
    norm_sums = jnp.concatenate([jnp.sum(scaled, axis=1), jnp.sum(scaled * unit, axis=1)])[None, :]
    hidden_sum = jnp.concatenate([hidden_sum, feature_sum[:1, features:], norm_sums], axis=1)
    hidden_sums = all_sum(hidden_sum, "gx", True)
    means = (hidden_sums[0] + hidden_sums[1])[0, width + 128 :].reshape(2, -1, 1) / model
    input_grad = upstream.astype(F32) + inv_std * (scaled - means[0] - unit * means[1])
    before = (row_in[None, :], col_in[None, :], mean_in)
    update_in = run(
        write_update, normed_side, act_parts, feature_sum, hidden_sums, before, sizes, False, after=[input_grad]
    )

    hidden_sum, feature_sum, branch = run(consume, hidden_parts, up_side, weight_out, 0)
    feature_sum = all_sum(feature_sum, "gy")
    hidden_sums = all_sum(jnp.concatenate([hidden_sum, feature_sum[:1, features:]], axis=1), "gx", True)
    before = (col_out[None, :], row_out[None, :], mean_out)
    update_out = run(write_update, up_full, hidden_parts, feature_sum, hidden_sums, before, sizes, True)
    output = (x_float + scatter_rows(branch, "gy")).astype(BF16)
    return (output, input_grad, update_in, update_out)


def solution(mesh):
    in_specs = (
        P("gy", "gx"),
        P("gx"),
        P("gx", "gy"),
        P("gy", "gx"),
        P("gy", "gx"),
        P("gx"),
        P("gy"),
        P("gy"),
        P("gx"),
    )
    out_specs = (P("gy", "gx"), P("gy", "gx"), P("gx", "gy"), P("gy", "gx"))
    return jax.shard_map(body, mesh=mesh, in_specs=in_specs, out_specs=out_specs, check_vma=False)
```

time: 394 us -> 367 us (0.931)
  waiting for transfers between devices: 234 us -> 205 us
  starting transfers between devices: 28.5 us -> 39.2 us
  local copies, waits for them, and re-layouts: 16.6 us -> 11.6 us
    reduce_scatter x2, waiting for transfers between devices: 135 us -> 109 us  [share_sum(): return lax.psum_scatter(partial, 'gx', scatter_dimension=0, tiled=True)]
    all_gather x2, waiting for transfers between devices: 67.2 us -> 48.4 us  [all_rows(): return [lax.all_gather(share, 'gx', axis=0)]]
    ppermute x6, waiting for transfers between devices: 1.28 us -> 15.8 us  [gather_rows(): lax.ppermute(share, axis, [(i, i ^ bits) for i in range(size)])]
    ppermute x13 -> x25, starting transfers between devices: 13.2 us -> 23.8 us  [all_sum(): lax.ppermute(value, axis, [(i, i ^ bit * n) for i in range(size)])]
    add x12 -> x8, other arithmetic: 0.21 us -> 4.43 us  [all_sum(): value = functools.reduce(jnp.add, arrived, value)]
    ppermute x13 -> x25, waiting for transfers between devices: 23.6 us -> 23.1 us  [all_sum(): lax.ppermute(value, axis, [(i, i ^ bit * n) for i in range(size)])]
  transfers between devices with their start and end apart: 29 -> 41, of which waited for: 17 -> 23; matrix products, arithmetic and copies ran while one was open for 5% -> 5% of each run, Pallas kernels for 12% -> 14%
where the time goes in v2:
time: 367 us; the launch traced here: 366 us
  waiting for transfers between devices  205 us (56%)
  Pallas kernels  83.5 us (23%)
  starting transfers between devices  39.2 us (11%)
  between operations  14.2 us (4%)
  other arithmetic  12.3 us (3%)
  local copies, waits for them, and re-layouts  11.6 us (3%)
    reduce_scatter x2, waiting for transfers between devices, share_sum(): return lax.psum_scatter(partial, 'gx', scatter_dimension=0, tiled=True)  109 us
    pallas_call x7, Pallas kernels, launch(): pl.pallas_call(wrapped, grid=grid, in_specs=list(in_specs) + idle * hidde...  83.5 us
    all_gather x2, waiting for transfers between devices, all_rows(): return [lax.all_gather(share, 'gx', axis=0)]  48.4 us
    ppermute x25, starting transfers between devices, all_sum(): lax.ppermute(value, axis, [(i, i ^ bit * n) for i in range(size)])  23.8 us
    ppermute x25, waiting for transfers between devices, all_sum(): lax.ppermute(value, axis, [(i, i ^ bit * n) for i in range(size)])  23.1 us
    ppermute x6, waiting for transfers between devices, gather_rows(): lax.ppermute(share, axis, [(i, i ^ bits) for i in range(size)])  15.8 us
    ppermute x6, waiting for transfers between devices, scatter_rows(): lax.ppermute(part, axis, [(i, i ^ bits) for i in range(size)]).astype(F32)  8.53 us
    ppermute x6, starting transfers between devices, gather_rows(): lax.ppermute(share, axis, [(i, i ^ bits) for i in range(size)])  8.1 us
  transfers between devices with their start and end apart: 41, of which 23 were waited for; matrix products, arithmetic and copies ran while one was open for 5% of the time, Pallas kernels for 14%

profile of v2, /device:TPU:0, one launch (start us, length us, event | category | flops | bytes accessed | tf_op | source)
XLA Modules:
  0.0 366.2 jit_solution(5686569742999360874)
XLA Ops:
  7.2 3.0 collective-permute-start
  10.2 1.5 collective-permute-start.2
  11.8 1.0 constant_dynamic-update-slice_fusion.3
  12.8 3.4 collective-permute-done
  16.2 6.0 %collective-permute-done.1 = bf16[128,768]{1,0:T(8,128)(2,1)S(1)} collective-permute-done((bf16[128,768]{1,0:T(8,128)(2,1)}, bf16[128,768]{1,0:T(8,128)(2,1)S(1)}, u32[]{:S(2)}, u32[]{:S(2)}) %collective-permute-start.1) | collective-permute-done | bytes 196640 | tf_op jit(solution)/shard_map/ppermute | solution.py:266
  22.3 0.9 copy-done.1
  23.1 10.2 %project.2 = (bf16[512,6144]{1,0:T(8,128)(2,1)}, s32[1]{0:T(128)}) custom-call(bf16[512,768]{1,0:T(8,128)(2,1)} %copy-done.1, bf16[6144,768]{1,0:T(8,128)(2,1)} %refs_1_.7, s32[1]{0:T(128)} %bitcast.5.refs_2_), custom_call_target="tpu_custom_call", output_to_operand_aliasing={{1}: (2, {})} | custom-call | flops 9663676416 | bytes 32212254 | tf_op jit(solution)/shard_map/project/pallas_call | solution.py:34
  33.4 0.8 copy-done
  34.4 1.6 collective-permute-start.4
  36.6 1.4 collective-permute-done.4
  38.1 1.0 collective-permute-done.5
  39.1 2.7 collective-permute-start.6
  41.7 1.9 collective-permute-done.6
  43.8 1.5 collective-permute-start.9
  45.3 1.5 collective-permute-start.8
  47.4 4.4 %collective-permute-done.9 = bf16[128,768]{1,0:T(8,128)(2,1)S(1)} collective-permute-done((bf16[128,768]{1,0:T(8,128)(2,1)S(1)}, bf16[128,768]{1,0:T(8,128)(2,1)S(1)}, u32[]{:S(2)}, u32[]{:S(2)}) %collective-permute-start.9) | collective-permute-done | bytes 196640 | tf_op jit(solution)/shard_map/ppermute | solution.py:266
  51.8 2.0 collective-permute-done.8
  53.7 1.0 fusion.14
  54.8 10.8 %project.3 = (bf16[512,6144]{1,0:T(8,128)(2,1)}, s32[1]{0:T(128)}) custom-call(bf16[512,768]{1,0:T(8,128)(2,1)} %get-tuple-element.52.refs_0_, bf16[768,6144]{1,0:T(8,128)(2,1)} %refs_1_.6, s32[1]{0:T(128)} %get-tuple-element.22.refs_2_), custom_call_target="tpu_custom_call", output_to_operand_aliasing={{1}: (2, {})} | custom-call | flops 9663676416 | bytes 32212254 | tf_op jit(solution)/shard_map/project/pallas_call | solution.py:34
  65.6 38.0 %reduce-scatter.5.cloned.1.call-done.refs_1_ = bf16[64,6144]{1,0:T(8,128)(2,1)} async-done(((bf16[512,6144]{1,0:T(8,128)(2,1)}), bf16[64,6144]{1,0:T(8,128)(2,1)}) %reduce-scatter.5.cloned.1.call-update) | async-done | bytes 786448 | tf_op jit(solution)/shard_map/reduce_scatter | solution.py:296
  103.6 71.1 %reduce-scatter.3.cloned.1.call-done.refs_0_ = bf16[64,6144]{1,0:T(8,128)(2,1)} async-done(((bf16[512,6144]{1,0:T(8,128)(2,1)}), bf16[64,6144]{1,0:T(8,128)(2,1)}) %reduce-scatter.3.cloned.1.call-update) | async-done | bytes 786448 | tf_op jit(solution)/shard_map/reduce_scatter | solution.py:296
  174.7 3.8 %activate.1 = (bf16[1,64,6144]{2,1,0:T(8,128)(2,1)}, bf16[1,64,6144]{2,1,0:T(8,128)(2,1)}, s32[1]{0:T(128)}) custom-call(bf16[64,6144]{1,0:T(8,128)(2,1)} %reduce-scatter.3.cloned.1.call-done.refs_0_, bf16[64,6144]{1,0:T(8,128)(2,1)} %reduce-scatter.5.cloned.1.call-done.refs_1_, s32[1]{0:T(128)} %get-tuple-element.25.refs_2_), custom_call_target="tpu_custom_call", output_to_operand_aliasing={{2}: (2, {})} | custom-call | flops 1000000000 | bytes 3333333 | tf_op jit(solution)/shard_map/activate/pallas_call | solution.py:34
  180.6 2.0 collective-permute-start.10
  183.3 0.6 broadcast_in_dim.35
  183.9 1.5 collective-permute-start.15
  185.5 1.5 collective-permute-start.16
  187.5 0.7 add_add_fusion.6
  188.2 1.7 collective-permute-done.16
  190.5 0.6 add_add_fusion.5
  191.2 1.6 collective-permute-done.13
  192.8 1.2 copy.24.refs_0_
  194.0 47.9 %all-gather.7.cloned.1.call-done = bf16[8,64,6144]{2,1,0:T(8,128)(2,1)} async-done(((bf16[1,64,6144]{2,1,0:T(8,128)(2,1)}), bf16[8,64,6144]{2,1,0:T(8,128)(2,1)}) %all-gather.7.cloned.1.call-update) | async-done | bytes 6291472 | tf_op jit(solution)/shard_map/all_gather | solution.py:312
  242.9 16.1 %consume.2 = (f32[1,6144]{1,0:T(1,128)}, f32[8,896]{1,0:T(8,128)}, bf16[512,768]{1,0:T(8,128)(2,1)}, s32[1]{0:T(128)}) custom-call(bf16[768,512]{1,0:T(8,128)(2,1)} %copy.24.refs_0_, bf16[768,6144]{1,0:T(8,128)(2,1)} %refs_1_.6, bf16[8,1,64,6144]{3,2,1,0:T(8,128)(2,1)} %bitcast.40, ...), custom_call_target="tpu_custom_call", output_to_operand_aliasing={{3}: (5, {})} | custom-call | flops 19327352832 | bytes 64424508 | tf_op jit(solution)/shard_map/consume/pallas_call | solution.py:34
  259.1 2.4 collective-permute-start.19
  262.6 1.2 fusion.17
  263.7 1.5 collective-permute-start.20
  265.2 1.5 collective-permute-start.22
  267.3 0.8 add_add_fusion.1.refs_2_
  268.1 3.6 collective-permute-done.20
  271.6 3.9 %collective-permute-done.22 = bf16[128,768]{1,0:T(8,128)(2,1)S(1)} collective-permute-done((bf16[128,768]{1,0:T(8,128)(2,1)S(1)}, bf16[128,768]{1,0:T(8,128)(2,1)S(1)}, u32[]{:S(2)}, u32[]{:S(2)}) %collective-permute-start.22) | collective-permute-done | bytes 196640 | tf_op jit(solution)/shard_map/ppermute | solution.py:278
  275.5 1.1 collective-permute-done.21
  276.6 1.2 fusion.15
  277.8 0.8 pad_maximum_fusion.1
  278.7 2.0 collective-permute-start.23
  280.8 5.3 %collective-permute-done.24 = f32[1,6528]{1,0:T(1,128)S(1)} collective-permute-done((f32[1,6528]{1,0:T(1,128)S(1)}, f32[1,6528]{1,0:T(1,128)S(1)}, u32[]{:S(2)}, u32[]{:S(2)}) %collective-permute-start.24) | collective-permute-done | bytes 26144 | tf_op jit(solution)/shard_map/ppermute | solution.py:252
  286.1 0.8 add_add_fusion.2.refs_3_.refs_5_
  287.6 1.2 copy.25.refs_0_
  288.7 4.9 %collective-permute-done.26.refs_4_.refs_6_ = f32[1,6528]{1,0:T(1,128)S(1)} collective-permute-done((f32[1,6528]{1,0:T(1,128)S(1)}, f32[1,6528]{1,0:T(1,128)S(1)}, u32[]{:S(2)}, u32[]{:S(2)}) %collective-permute-start.26) | collective-permute-done | bytes 26144 | tf_op jit(solution)/shard_map/ppermute | solution.py:252
  293.7 0.9 fusion.9.refs_10_
  294.6 12.8 %write_update.2 = (f32[768,6144]{1,0:T(8,128)}, s32[1]{0:T(128)}) custom-call(bf16[768,512]{1,0:T(8,128)(2,1)} %copy.24.refs_0_, bf16[8,1,64,6144]{3,2,1,0:T(8,128)(2,1)} %bitcast.41, f32[8,896]{1,0:T(8,128)} %copy-done.4, f32[1,6528]{1,0:T(1,128)} %copy-done.6, f32[1,6528]{1,0:T(1,128)} %copy-done.12, ...), custom_call_target="tpu_custom_call", output_to_operand_aliasing={{1}: (11, {})} | custom-call | flops 14155776000 | bytes 47185920 | tf_op jit(solution)/shard_map/write_update/pallas_call | solution.py:34
  307.9 16.8 %consume.3 = (f32[1,6144]{1,0:T(1,128)}, f32[8,896]{1,0:T(8,128)}, bf16[512,768]{1,0:T(8,128)(2,1)}, s32[1]{0:T(128)}) custom-call(bf16[768,512]{1,0:T(8,128)(2,1)} %copy.25.refs_0_, bf16[6144,768]{1,0:T(8,128)(2,1)} %refs_1_.7, bf16[8,1,64,6144]{3,2,1,0:T(8,128)(2,1)} %bitcast.38, s32[1]{0:T(128)} %get-tuple-element.33.refs_3_), custom_call_target="tpu_custom_call", output_to_operand_aliasing={{3}: (3, {})} | custom-call | flops 19327352832 | bytes 64424508 | tf_op jit(solution)/shard_map/consume/pallas_call | solution.py:34
  324.6 2.3 collective-permute-start.32
  328.1 1.5 collective-permute-done.32
  329.6 1.4 collective-permute-done.31
  331.7 0.8 add_add_fusion.refs_2_
  332.5 0.8 pad_maximum_fusion.2
  333.4 2.0 collective-permute-start.33
  336.0 1.1 collective-permute-done.34
  337.1 0.8 add_add_fusion.3.refs_3_.refs_5_
  337.9 1.7 collective-permute-start.36
  339.6 1.2 fusion.16
  341.4 2.4 collective-permute-start.29
  345.0 12.9 %write_update.3 = (f32[6144,768]{1,0:T(8,128)}, s32[1]{0:T(128)}) custom-call(bf16[512,768]{1,0:T(8,128)(2,1)} %copy-done.1, bf16[8,1,64,6144]{3,2,1,0:T(8,128)(2,1)} %bitcast.39, f32[8,896]{1,0:T(8,128)} %copy-done.5, f32[1,6272]{1,0:T(1,128)} %copy-done.7, f32[1,6272]{1,0:T(1,128)} %copy-done.13, ...), custom_call_target="tpu_custom_call", output_to_operand_aliasing={{1}: (10, {})} | custom-call | flops 14155776000 | bytes 47185920 | tf_op jit(solution)/shard_map/write_update/pallas_call | solution.py:34
  357.9 1.7 fusion.10
  (98 shorter events, 13.8 us)
Async XLA Ops:
  7.2 96.5 %reduce-scatter.5.cloned.1.call-start = ((), (), s32[]{:S(2)}) async-start(), calls=%async_computation.3 | async-start | bytes 7077888 | tf_op jit(solution)/shard_map/reduce_scatter | solution.py:296
  7.2 8.9 %collective-permute-start = (bf16[128,768]{1,0:T(8,128)(2,1)}, bf16[128,768]{1,0:T(8,128)(2,1)S(1)}, u32[]{:S(2)}, u32[]{:S(2)}) collective-permute-start(bf16[128,768]{1,0:T(8,128)(2,1)} %param.13), channel_id=1, source_target_pairs={{0,1},{1,0},{2,3},{3,2},{4,5},{5,4},{6,7},{7,6},{8,9},{9,8},{10,11... | collective-permute-start | bytes 589832 | tf_op jit(solution)/shard_map/ppermute | solution.py:266
  10.2 12.0 %collective-permute-start.2 = (bf16[128,768]{1,0:T(8,128)(2,1)}, bf16[128,768]{1,0:T(8,128)(2,1)S(1)}, u32[]{:S(2)}, u32[]{:S(2)}) collective-permute-start(bf16[128,768]{1,0:T(8,128)(2,1)} %param.13), channel_id=1, source_target_pairs={{0,3},{1,2},{2,1},{3,0},{4,7},{5,6},{6,5},{7,4},{8,11},{9,10},{10,... | collective-permute-start | bytes 589832 | tf_op jit(solution)/shard_map/ppermute | solution.py:266
  11.7 10.5 %collective-permute-start.1 = (bf16[128,768]{1,0:T(8,128)(2,1)}, bf16[128,768]{1,0:T(8,128)(2,1)S(1)}, u32[]{:S(2)}, u32[]{:S(2)}) collective-permute-start(bf16[128,768]{1,0:T(8,128)(2,1)} %param.13), channel_id=1, source_target_pairs={{0,2},{1,3},{2,0},{3,1},{4,6},{5,7},{6,4},{7,5},{8,10},{9,11},{10,... | collective-permute-start | bytes 589832 | tf_op jit(solution)/shard_map/ppermute | solution.py:266
  22.3 0.9 copy-start.1
  33.3 0.9 copy-start
  33.4 10.3 %copy-start.9 = (f32[768]{0:T(1024)S(1)}, f32[768]{0:T(1024)}, u32[]{:S(2)}) copy-start(f32[768]{0:T(1024)} %param.10) | copy-start | bytes 9220
  33.4 141.4 %reduce-scatter.3.cloned.1.call-start = ((), (), s32[]{:S(2)}) async-start(), calls=%async_computation.2 | async-start | bytes 7077888 | tf_op jit(solution)/shard_map/reduce_scatter | solution.py:296
  34.4 3.6 collective-permute-start.4
  36.1 3.0 collective-permute-start.5
  36.1 3.0 collective-permute-start.3
  39.1 4.5 %collective-permute-start.6 = (f32[2,128]{1,0:T(2,128)S(1)}, f32[2,128]{1,0:T(2,128)S(1)}, u32[]{:S(2)}, u32[]{:S(2)}) collective-permute-start(f32[2,128]{1,0:T(2,128)S(1)} %add_add_fusion.4), channel_id=1, source_target_pairs={{0,16},{4,20},{8,24},{12,28},{16,0},{20,4},{24,8},{28,12},{1,17},{... | collective-permute-start | bytes 3080 | tf_op jit(solution)/shard_map/ppermute | solution.py:252
  43.8 8.0 %collective-permute-start.9 = (bf16[128,768]{1,0:T(8,128)(2,1)S(1)}, bf16[128,768]{1,0:T(8,128)(2,1)S(1)}, u32[]{:S(2)}, u32[]{:S(2)}) collective-permute-start(bf16[128,768]{1,0:T(8,128)(2,1)S(1)} %fusion.5), channel_id=1, source_target_pairs={{0,3},{1,2},{2,1},{3,0},{4,7},{5,6},{6,5},{7,4},{8,11},{9,10},{10,... | collective-permute-start | bytes 589832 | tf_op jit(solution)/shard_map/ppermute | solution.py:266
  45.3 8.4 %collective-permute-start.8 = (bf16[128,768]{1,0:T(8,128)(2,1)S(1)}, bf16[128,768]{1,0:T(8,128)(2,1)S(1)}, u32[]{:S(2)}, u32[]{:S(2)}) collective-permute-start(bf16[128,768]{1,0:T(8,128)(2,1)S(1)} %fusion.5), channel_id=1, source_target_pairs={{0,2},{1,3},{2,0},{3,1},{4,6},{5,7},{6,4},{7,5},{8,10},{9,11},{10,... | collective-permute-start | bytes 589832 | tf_op jit(solution)/shard_map/ppermute | solution.py:266
  46.8 6.9 %collective-permute-start.7 = (bf16[128,768]{1,0:T(8,128)(2,1)S(1)}, bf16[128,768]{1,0:T(8,128)(2,1)S(1)}, u32[]{:S(2)}, u32[]{:S(2)}) collective-permute-start(bf16[128,768]{1,0:T(8,128)(2,1)S(1)} %fusion.5), channel_id=1, source_target_pairs={{0,1},{1,0},{2,3},{3,2},{4,5},{5,4},{6,7},{7,6},{8,9},{9,8},{10,11... | collective-permute-start | bytes 589832 | tf_op jit(solution)/shard_map/ppermute | solution.py:266
  65.5 113.6 %copy-start.10 = (f32[768]{0:T(1024)S(1)}, f32[768]{0:T(1024)}, u32[]{:S(2)}) copy-start(f32[768]{0:T(1024)} %param.14) | copy-start | bytes 9220
  65.5 117.1 %copy-start.8 = (f32[6144]{0:T(1024)S(1)}, f32[6144]{0:T(1024)}, u32[]{:S(2)}) copy-start(f32[6144]{0:T(1024)} %param.16) | copy-start | bytes 73732
  65.6 176.3 %all-gather.7.cloned.1.call-start = ((), (), s32[]{:S(2)}) async-start(), calls=%async_computation.5 | async-start | bytes 7077888 | tf_op jit(solution)/shard_map/all_gather | solution.py:312
  178.6 129.3 %all-gather.5.cloned.1.call-start = ((), (), s32[]{:S(2)}) async-start(), calls=%async_computation.4 | async-start | bytes 7077888 | tf_op jit(solution)/shard_map/all_gather | solution.py:312
  180.4 6.5 %collective-permute-start.11 = (f32[128]{0:T(128)S(1)}, f32[128]{0:T(128)S(1)}, u32[]{:S(2)}, u32[]{:S(2)}) collective-permute-start(f32[128]{0:T(128)S(1)} %broadcast_in_dim.33), channel_id=1, source_target_pairs={{0,8},{4,12},{8,0},{12,4},{16,24},{20,28},{24,16},{28,20},{1,9},{5... | collective-permute-start | bytes 1544 | tf_op jit(solution)/shard_map/ppermute | solution.py:252
  180.5 7.0 %collective-permute-start.12 = (f32[128]{0:T(128)S(1)}, f32[128]{0:T(128)S(1)}, u32[]{:S(2)}, u32[]{:S(2)}) collective-permute-start(f32[128]{0:T(128)S(1)} %broadcast_in_dim.33), channel_id=1, source_target_pairs={{0,12},{4,8},{8,4},{12,0},{16,28},{20,24},{24,20},{28,16},{1,13},{... | collective-permute-start | bytes 1544 | tf_op jit(solution)/shard_map/ppermute | solution.py:252
  180.6 6.9 %collective-permute-start.10 = (f32[128]{0:T(128)S(1)}, f32[128]{0:T(128)S(1)}, u32[]{:S(2)}, u32[]{:S(2)}) collective-permute-start(f32[128]{0:T(128)S(1)} %broadcast_in_dim.33), channel_id=1, source_target_pairs={{0,4},{4,0},{8,12},{12,8},{16,20},{20,16},{24,28},{28,24},{1,5},{5... | collective-permute-start | bytes 1544 | tf_op jit(solution)/shard_map/ppermute | solution.py:252
  183.9 4.3 %collective-permute-start.15 = (f32[128]{0:T(128)S(1)}, f32[128]{0:T(128)S(1)}, u32[]{:S(2)}, u32[]{:S(2)}) collective-permute-start(f32[128]{0:T(128)S(1)} %broadcast_in_dim.35), channel_id=1, source_target_pairs={{0,2},{1,3},{2,0},{3,1},{4,6},{5,7},{6,4},{7,5},{8,10},{9,11},{10,... | collective-permute-start | bytes 1544 | tf_op jit(solution)/shard_map/ppermute | solution.py:252
  185.5 4.4 %collective-permute-start.16 = (f32[128]{0:T(128)S(1)}, f32[128]{0:T(128)S(1)}, u32[]{:S(2)}, u32[]{:S(2)}) collective-permute-start(f32[128]{0:T(128)S(1)} %broadcast_in_dim.35), channel_id=1, source_target_pairs={{0,3},{1,2},{2,1},{3,0},{4,7},{5,6},{6,5},{7,4},{8,11},{9,10},{10,... | collective-permute-start | bytes 1544 | tf_op jit(solution)/shard_map/ppermute | solution.py:252
  186.9 3.5 collective-permute-start.14
  188.1 4.6 %collective-permute-start.13 = (f32[128]{0:T(128)S(1)}, f32[128]{0:T(128)S(1)}, u32[]{:S(2)}, u32[]{:S(2)}) collective-permute-start(f32[128]{0:T(128)S(1)} %add_add_fusion.6), channel_id=1, source_target_pairs={{0,16},{4,20},{8,24},{12,28},{16,0},{20,4},{24,8},{28,12},{1,17},{... | collective-permute-start | bytes 1544 | tf_op jit(solution)/shard_map/ppermute | solution.py:252
  242.9 44.6 %copy-start.2 = (bf16[512,768]{1,0:T(8,128)(2,1)S(1)}, bf16[512,768]{1,0:T(8,128)(2,1)}, u32[]{:S(2)}) copy-start(bf16[512,768]{1,0:T(8,128)(2,1)} %copy-done.1) | copy-start | bytes 2359300
  242.9 50.7 %copy-start.3 = (bf16[128,768]{1,0:T(8,128)(2,1)S(1)}, bf16[128,768]{1,0:T(8,128)(2,1)}, u32[]{:S(2)}) copy-start(bf16[128,768]{1,0:T(8,128)(2,1)} %param.13) | copy-start | bytes 589828
  259.1 7.7 %collective-permute-start.19 = (f32[8,896]{1,0:T(8,128)}, f32[8,896]{1,0:T(8,128)S(1)}, u32[]{:S(2)}, u32[]{:S(2)}) collective-permute-start(f32[8,896]{1,0:T(8,128)} %get-tuple-element.29), channel_id=1, source_target_pairs={{0,3},{1,2},{2,1},{3,0},{4,7},{5,6},{6,5},{7,4},{8,11},{9,10},{10,... | collective-permute-start | bytes 86024 | tf_op jit(solution)/shard_map/ppermute | solution.py:252
  261.4 5.8 %collective-permute-start.18 = (f32[8,896]{1,0:T(8,128)}, f32[8,896]{1,0:T(8,128)S(1)}, u32[]{:S(2)}, u32[]{:S(2)}) collective-permute-start(f32[8,896]{1,0:T(8,128)} %get-tuple-element.29), channel_id=1, source_target_pairs={{0,2},{1,3},{2,0},{3,1},{4,6},{5,7},{6,4},{7,5},{8,10},{9,11},{10,... | collective-permute-start | bytes 86024 | tf_op jit(solution)/shard_map/ppermute | solution.py:252
  262.0 5.3 %collective-permute-start.17 = (f32[8,896]{1,0:T(8,128)}, f32[8,896]{1,0:T(8,128)S(1)}, u32[]{:S(2)}, u32[]{:S(2)}) collective-permute-start(f32[8,896]{1,0:T(8,128)} %get-tuple-element.29), channel_id=1, source_target_pairs={{0,1},{1,0},{2,3},{3,2},{4,5},{5,4},{6,7},{7,6},{8,9},{9,8},{10,11... | collective-permute-start | bytes 86024 | tf_op jit(solution)/shard_map/ppermute | solution.py:252
  263.7 7.9 %collective-permute-start.20 = (bf16[128,768]{1,0:T(8,128)(2,1)S(1)}, bf16[128,768]{1,0:T(8,128)(2,1)S(1)}, u32[]{:S(2)}, u32[]{:S(2)}) collective-permute-start(bf16[128,768]{1,0:T(8,128)(2,1)S(1)} %get-tuple-element.48), channel_id=1, source_target_pairs={{0,1},{1,0},{2,3},{3,2},{4,5},{5,4},{6,7},{7,6},{8,9},{9,8},{10,11... | collective-permute-start | bytes 589832 | tf_op jit(solution)/shard_map/ppermute | solution.py:278
  265.2 10.3 %collective-permute-start.22 = (bf16[128,768]{1,0:T(8,128)(2,1)S(1)}, bf16[128,768]{1,0:T(8,128)(2,1)S(1)}, u32[]{:S(2)}, u32[]{:S(2)}) collective-permute-start(bf16[128,768]{1,0:T(8,128)(2,1)S(1)} %get-tuple-element.49), channel_id=1, source_target_pairs={{0,3},{1,2},{2,1},{3,0},{4,7},{5,6},{6,5},{7,4},{8,11},{9,10},{10,... | collective-permute-start | bytes 589832 | tf_op jit(solution)/shard_map/ppermute | solution.py:278
  266.7 9.9 %collective-permute-start.21 = (bf16[128,768]{1,0:T(8,128)(2,1)S(1)}, bf16[128,768]{1,0:T(8,128)(2,1)S(1)}, u32[]{:S(2)}, u32[]{:S(2)}) collective-permute-start(bf16[128,768]{1,0:T(8,128)(2,1)S(1)} %get-tuple-element.50), channel_id=1, source_target_pairs={{0,2},{1,3},{2,0},{3,1},{4,6},{5,7},{6,4},{7,5},{8,10},{9,11},{10,... | collective-permute-start | bytes 589832 | tf_op jit(solution)/shard_map/ppermute | solution.py:278
  268.0 26.6 %copy-start.4 = (f32[8,896]{1,0:T(8,128)}, f32[8,896]{1,0:T(8,128)S(1)}, u32[]{:S(2)}) copy-start(f32[8,896]{1,0:T(8,128)S(1)} %add_add_fusion.1.refs_2_) | copy-start | bytes 86020
  278.6 7.5 %collective-permute-start.24 = (f32[1,6528]{1,0:T(1,128)S(1)}, f32[1,6528]{1,0:T(1,128)S(1)}, u32[]{:S(2)}, u32[]{:S(2)}) collective-permute-start(f32[1,6528]{1,0:T(1,128)S(1)} %pad_maximum_fusion.1), channel_id=1, source_target_pairs={{0,8},{4,12},{8,0},{12,4},{16,24},{20,28},{24,16},{28,20},{1,9},{5... | collective-permute-start | bytes 78344 | tf_op jit(solution)/shard_map/ppermute | solution.py:252
  278.6 7.5 %collective-permute-start.25 = (f32[1,6528]{1,0:T(1,128)S(1)}, f32[1,6528]{1,0:T(1,128)S(1)}, u32[]{:S(2)}, u32[]{:S(2)}) collective-permute-start(f32[1,6528]{1,0:T(1,128)S(1)} %pad_maximum_fusion.1), channel_id=1, source_target_pairs={{0,12},{4,8},{8,4},{12,0},{16,28},{20,24},{24,20},{28,16},{1,13},{... | collective-permute-start | bytes 78344 | tf_op jit(solution)/shard_map/ppermute | solution.py:252
  278.7 7.4 %collective-permute-start.23 = (f32[1,6528]{1,0:T(1,128)S(1)}, f32[1,6528]{1,0:T(1,128)S(1)}, u32[]{:S(2)}, u32[]{:S(2)}) collective-permute-start(f32[1,6528]{1,0:T(1,128)S(1)} %pad_maximum_fusion.1), channel_id=1, source_target_pairs={{0,4},{4,0},{8,12},{12,8},{16,20},{20,16},{24,28},{28,24},{1,5},{5... | collective-permute-start | bytes 78344 | tf_op jit(solution)/shard_map/ppermute | solution.py:252
  286.9 7.7 %copy-start.6 = (f32[1,6528]{1,0:T(1,128)}, f32[1,6528]{1,0:T(1,128)S(1)}, u32[]{:S(2)}) copy-start(f32[1,6528]{1,0:T(1,128)S(1)} %add_add_fusion.2.refs_3_.refs_5_) | copy-start | bytes 78340
  286.9 6.7 %collective-permute-start.26 = (f32[1,6528]{1,0:T(1,128)S(1)}, f32[1,6528]{1,0:T(1,128)S(1)}, u32[]{:S(2)}, u32[]{:S(2)}) collective-permute-start(f32[1,6528]{1,0:T(1,128)S(1)} %add_add_fusion.2.refs_3_.refs_5_), channel_id=1, source_target_pairs={{0,16},{4,20},{8,24},{12,28},{16,0},{20,4},{24,8},{28,12},{1,17},{... | collective-permute-start | bytes 78344 | tf_op jit(solution)/shard_map/ppermute | solution.py:252
  293.6 1.0 copy-start.12
  307.9 27.6 %copy-start.11 = (f32[768]{0:T(1024)S(1)}, f32[768]{0:T(1024)}, u32[]{:S(2)}) copy-start(f32[768]{0:T(1024)} %param.17) | copy-start | bytes 9220
  324.6 5.0 %collective-permute-start.32 = (f32[8,896]{1,0:T(8,128)}, f32[8,896]{1,0:T(8,128)S(1)}, u32[]{:S(2)}, u32[]{:S(2)}) collective-permute-start(f32[8,896]{1,0:T(8,128)} %get-tuple-element.36), channel_id=1, source_target_pairs={{0,3},{1,2},{2,1},{3,0},{4,7},{5,6},{6,5},{7,4},{8,11},{9,10},{10,... | collective-permute-start | bytes 86024 | tf_op jit(solution)/shard_map/ppermute | solution.py:252
  327.0 4.1 %collective-permute-start.31 = (f32[8,896]{1,0:T(8,128)}, f32[8,896]{1,0:T(8,128)S(1)}, u32[]{:S(2)}, u32[]{:S(2)}) collective-permute-start(f32[8,896]{1,0:T(8,128)} %get-tuple-element.36), channel_id=1, source_target_pairs={{0,2},{1,3},{2,0},{3,1},{4,6},{5,7},{6,4},{7,5},{8,10},{9,11},{10,... | collective-permute-start | bytes 86024 | tf_op jit(solution)/shard_map/ppermute | solution.py:252
  327.6 4.1 %collective-permute-start.30 = (f32[8,896]{1,0:T(8,128)}, f32[8,896]{1,0:T(8,128)S(1)}, u32[]{:S(2)}, u32[]{:S(2)}) collective-permute-start(f32[8,896]{1,0:T(8,128)} %get-tuple-element.36), channel_id=1, source_target_pairs={{0,1},{1,0},{2,3},{3,2},{4,5},{5,4},{6,7},{7,6},{8,9},{9,8},{10,11... | collective-permute-start | bytes 86024 | tf_op jit(solution)/shard_map/ppermute | solution.py:252
  332.5 11.9 %copy-start.5 = (f32[8,896]{1,0:T(8,128)}, f32[8,896]{1,0:T(8,128)S(1)}, u32[]{:S(2)}) copy-start(f32[8,896]{1,0:T(8,128)S(1)} %add_add_fusion.refs_2_) | copy-start | bytes 86020
  333.2 3.9 %collective-permute-start.34 = (f32[1,6272]{1,0:T(1,128)S(1)}, f32[1,6272]{1,0:T(1,128)S(1)}, u32[]{:S(2)}, u32[]{:S(2)}) collective-permute-start(f32[1,6272]{1,0:T(1,128)S(1)} %pad_maximum_fusion.2), channel_id=1, source_target_pairs={{0,8},{4,12},{8,0},{12,4},{16,24},{20,28},{24,16},{28,20},{1,9},{5... | collective-permute-start | bytes 75272 | tf_op jit(solution)/shard_map/ppermute | solution.py:252
  333.3 3.8 %collective-permute-start.35 = (f32[1,6272]{1,0:T(1,128)S(1)}, f32[1,6272]{1,0:T(1,128)S(1)}, u32[]{:S(2)}, u32[]{:S(2)}) collective-permute-start(f32[1,6272]{1,0:T(1,128)S(1)} %pad_maximum_fusion.2), channel_id=1, source_target_pairs={{0,12},{4,8},{8,4},{12,0},{16,28},{20,24},{24,20},{28,16},{1,13},{... | collective-permute-start | bytes 75272 | tf_op jit(solution)/shard_map/ppermute | solution.py:252
  333.4 3.7 %collective-permute-start.33 = (f32[1,6272]{1,0:T(1,128)S(1)}, f32[1,6272]{1,0:T(1,128)S(1)}, u32[]{:S(2)}, u32[]{:S(2)}) collective-permute-start(f32[1,6272]{1,0:T(1,128)S(1)} %pad_maximum_fusion.2), channel_id=1, source_target_pairs={{0,4},{4,0},{8,12},{12,8},{16,20},{20,16},{24,28},{28,24},{1,5},{5... | collective-permute-start | bytes 75272 | tf_op jit(solution)/shard_map/ppermute | solution.py:252
  337.9 6.4 %copy-start.7 = (f32[1,6272]{1,0:T(1,128)}, f32[1,6272]{1,0:T(1,128)S(1)}, u32[]{:S(2)}) copy-start(f32[1,6272]{1,0:T(1,128)S(1)} %add_add_fusion.3.refs_3_.refs_5_) | copy-start | bytes 75268
  337.9 6.4 %collective-permute-start.36 = (f32[1,6272]{1,0:T(1,128)S(1)}, f32[1,6272]{1,0:T(1,128)S(1)}, u32[]{:S(2)}, u32[]{:S(2)}) collective-permute-start(f32[1,6272]{1,0:T(1,128)S(1)} %add_add_fusion.3.refs_3_.refs_5_), channel_id=1, source_target_pairs={{0,16},{4,20},{8,24},{12,28},{16,0},{20,4},{24,8},{28,12},{1,17},{... | collective-permute-start | bytes 75272 | tf_op jit(solution)/shard_map/ppermute | solution.py:252
  340.8 17.1 %collective-permute-start.27 = (bf16[128,768]{1,0:T(8,128)(2,1)S(1)}, bf16[128,768]{1,0:T(8,128)(2,1)S(1)}, u32[]{:S(2)}, u32[]{:S(2)}) collective-permute-start(bf16[128,768]{1,0:T(8,128)(2,1)S(1)} %get-tuple-element.45), channel_id=1, source_target_pairs={{0,1},{1,0},{2,3},{3,2},{4,5},{5,4},{6,7},{7,6},{8,9},{9,8},{10,11... | collective-permute-start | bytes 589832 | tf_op jit(solution)/shard_map/ppermute | solution.py:278
  341.4 16.5 %collective-permute-start.29 = (bf16[128,768]{1,0:T(8,128)(2,1)S(1)}, bf16[128,768]{1,0:T(8,128)(2,1)S(1)}, u32[]{:S(2)}, u32[]{:S(2)}) collective-permute-start(bf16[128,768]{1,0:T(8,128)(2,1)S(1)} %get-tuple-element.46), channel_id=1, source_target_pairs={{0,3},{1,2},{2,1},{3,0},{4,7},{5,6},{6,5},{7,4},{8,11},{9,10},{10,... | collective-permute-start | bytes 589832 | tf_op jit(solution)/shard_map/ppermute | solution.py:278
  343.8 14.1 %collective-permute-start.28 = (bf16[128,768]{1,0:T(8,128)(2,1)S(1)}, bf16[128,768]{1,0:T(8,128)(2,1)S(1)}, u32[]{:S(2)}, u32[]{:S(2)}) collective-permute-start(bf16[128,768]{1,0:T(8,128)(2,1)S(1)} %get-tuple-element.47), channel_id=1, source_target_pairs={{0,2},{1,3},{2,0},{3,1},{4,6},{5,7},{6,4},{7,5},{8,10},{9,11},{10,... | collective-permute-start | bytes 589832 | tf_op jit(solution)/shard_map/ppermute | solution.py:278
  344.4 0.6 copy-start.13
Sparse Core Ops, SparseCore 0:
  33.5 70.0 reduce-scatter.4
  106.5 68.1 reduce-scatter.2
  178.7 63.1 all-gather.6
  243.4 64.4 all-gather.4

commit v3 on v2

--- a/solution.py
+++ b/solution.py
@@ -9,7 +9,7 @@
 
 F32 = jnp.float32
 BF16 = jnp.bfloat16
-VMEM = 58 * 2**20
+VMEM = 44 * 2**20
 
 
 def block(total, limit):
@@ -47,31 +47,25 @@
     return (list(own) if many else own[0]), list(results[len(shapes) :])
 
 
-def aligned(width, start, limit):
+def project(rows, weight, dim, halves=1, after=(), carry=(), limit=1536):
+    count, depth = rows.shape
+    width = weight.shape[1 - dim]
     step = block(width, limit)
-    while start % step:
-        step = block(width, step - 128)
-    return step, start // step
-
-
-def project(rows, weight, start, width, dim, after=(), carry=(), limit=1536):
-    count, depth = rows.shape
-    step, first = aligned(width, start, limit)
-
-    def kernel(x, w, o):
+    part_rows = count // halves
+
+    def kernel(x, w, *outs):
         dims = (((1,), (dim,)), ((), ()))
-        o[...] = lax.dot_general(x[...], w[...], dims, preferred_element_type=F32).astype(o.dtype)
-
-    if dim == 0:
-        spec = pl.BlockSpec((depth, step), lambda i: (0, first + i))
-    else:
-        spec = pl.BlockSpec((step, depth), lambda i: (first + i, 0))
+        part = lax.dot_general(x[...], w[...], dims, preferred_element_type=F32).astype(BF16)
+        for n, o in enumerate(outs):
+            o[...] = part[n * part_rows : (n + 1) * part_rows]
+
+    spec = pl.BlockSpec((depth, step), lambda i: (0, i)) if dim == 0 else pl.BlockSpec((step, depth), lambda i: (i, 0))
     return launch(
         kernel,
         (width // step,),
         [pl.BlockSpec((count, depth), lambda i: (0, 0)), spec],
-        pl.BlockSpec((count, step), lambda i: (0, i)),
-        jax.ShapeDtypeStruct((count, width), BF16),
+        [pl.BlockSpec((part_rows, step), lambda i: (0, i))] * halves,
+        [jax.ShapeDtypeStruct((part_rows, width), BF16)] * halves,
         (rows, weight),
         after,
         carry,
@@ -91,35 +85,49 @@
     return whole[0] if len(whole) == 1 else jnp.concatenate(whole)
 
 
-def consume(parts, left, weight, dim, after=(), carry=(), limit=2048):
-    depth, count = left.shape
+def consume(parts, side, weight, dim, hidden_rows, after=(), carry=(), limit=1536):
+    count, depth = side.shape if hidden_rows else side.shape[::-1]
     width = parts[0].shape[3]
     step = block(width, limit)
 
+    def fold(squares):
+        folded = squares[:, :128]
+        for j in range(1, squares.shape[1] // 128):
+            folded += squares[:, j * 128 : (j + 1) * 128]
+        return folded
+
     def kernel(x, w, *rest):
-        cols, feature, product, lanes, total = rest[-5:]
-        a = whole_rows(rest[:-5])
-        g = jnp.dot(x[...], a, preferred_element_type=F32)
-        s = g * g
-        cols[...] = jnp.sum(s, axis=0, keepdims=True)
-        folded = s[:, :128]
-        for j in range(1, step // 128):
-            folded += s[:, j * 128 : (j + 1) * 128]
+        grad, cols, feature, product, sums, total = rest[-6:]
+        i = pl.program_id(0)
+        a = whole_rows(rest[:-6])
+        here = pl.ds(pl.multiple_of(i * step, step), step)
+        if hidden_rows:
+            g = lax.dot_general(a, x[...], (((0,), (0,)), ((), ())), preferred_element_type=F32)
+            grad[here, :] = g.astype(BF16)
+            s = g * g
+            cols[...] = jnp.sum(jnp.transpose(fold(s)), axis=0, keepdims=True)
+            across = jnp.broadcast_to(jnp.sum(s, axis=0, keepdims=True), (8, depth))
+        else:
+            g = jnp.dot(x[...], a, preferred_element_type=F32)
+            grad[:, here] = g.astype(BF16)
+            s = g * g
+            cols[...] = jnp.sum(s, axis=0, keepdims=True)
+            across = fold(s)
         part = lax.dot_general(a, w[...], (((1,), (dim,)), ((), ())), preferred_element_type=F32)
 
-        @pl.when(pl.program_id(0) == 0)
+        @pl.when(i == 0)
         def _():
-            lanes[...] = folded
+            sums[...] = across
             total[...] = part
 
-        @pl.when(pl.program_id(0) != 0)
+        @pl.when(i != 0)
         def _():
-            lanes[...] += folded
+            sums[...] += across
             total[...] += part
 
-        @pl.when(pl.program_id(0) == width // step - 1)
+        @pl.when(i == width // step - 1)
         def _():
-            row = jnp.sum(jnp.transpose(lanes[...]), axis=0, keepdims=True)
+            row = sums[:1, :] if hidden_rows else jnp.sum(jnp.transpose(sums[...]), axis=0, keepdims=True)
             feature[:, :depth] = jnp.broadcast_to(row, (8, depth))
             feature[:, depth:] = jnp.broadcast_to(jnp.sum(row, axis=1, keepdims=True), (8, 128))
             product[...] = total[...].astype(BF16)
@@ -128,21 +136,23 @@
     return launch(
         kernel,
         (width // step,),
-        [pl.BlockSpec((depth, count), lambda i: (0, 0)), spec] + parts_specs(parts, 0, step, lambda i: i),
+        [pl.BlockSpec(side.shape, lambda i: (0, 0)), spec] + parts_specs(parts, 0, step, lambda i: i),
         [
+            pl.BlockSpec(memory_space=pltpu.VMEM),
             pl.BlockSpec((1, step), lambda i: (0, i)),
             pl.BlockSpec((8, depth + 128), lambda i: (0, 0)),
             pl.BlockSpec((count, depth), lambda i: (0, 0)),
         ],
         [
+            pltpu.VMEM((width, depth) if hidden_rows else (depth, width), BF16),
             jax.ShapeDtypeStruct((1, width), F32),
             jax.ShapeDtypeStruct((8, depth + 128), F32),
             jax.ShapeDtypeStruct((count, depth), BF16),
         ],
-        (left, weight, *parts),
+        (side, weight, *parts),
         after,
         carry,
-        scratch=[pltpu.VMEM((depth, 128), F32), pltpu.VMEM((count, depth), F32)],
+        scratch=[pltpu.VMEM((8, depth) if hidden_rows else (depth, 128), F32), pltpu.VMEM((count, depth), F32)],
         flops=8 * count * depth * width,
         name="consume",
     )
@@ -178,22 +188,21 @@
     )
 
 
-def write_update(side, parts, feature_sum, hidden_sums, before, sizes, hidden_rows, after=(), carry=(), limit=1536):
-    total = parts[0].shape[3]
+def settle(after, carry):
+    return launch(lambda: None, (1,), [], [], [], (), after, carry, name="settle")
+
+
+def write_update(grad, feature_sum, hidden_sums, before, sizes, hidden_rows, after=(), carry=(), limit=768):
+    total, features = grad.shape if hidden_rows else grad.shape[::-1]
     step = block(total, limit)
-    features = side.shape[1] if hidden_rows else side.shape[0]
     model, hidden_units = sizes
 
     def tall(row):
         return jnp.transpose(jnp.broadcast_to(row, (8, row.shape[1])))[:, :1]
 
-    def kernel(x, *rest):
-        across, near_sum, far_sum, near_all, far_all, feature_before, hidden_before, mean_before, o = rest[-9:]
-        a = whole_rows(rest[:-9])
-        if hidden_rows:
-            g = lax.dot_general(a, x[...], (((0,), (0,)), ((), ())), preferred_element_type=F32)
-        else:
-            g = jnp.dot(x[...], a, preferred_element_type=F32)
+    def kernel(whole, across, near_sum, far_sum, near_all, far_all, feature_before, hidden_before, mean_before, o):
+        here = pl.ds(pl.multiple_of(pl.program_id(0) * step, step), step)
+        g = (whole[here, :] if hidden_rows else whole[:, here]).astype(F32)
         grand = (near_all[:, :1] + far_all[:, :1]) / model / hidden_units + 1e-30
         mean = 0.9 * mean_before[:, :1] + 0.1 * grand
         by_feature = 0.9 * feature_before[...] + 0.1 * (across[:1, :features] / hidden_units + 1e-30)
@@ -226,13 +235,13 @@
     return launch(
         kernel,
         (total // step,),
-        [pl.BlockSpec(side.shape, lambda i: (0, 0))] + parts_specs(parts, 0, step, lambda i: i) + scale_specs,
+        [pl.BlockSpec(memory_space=pltpu.VMEM)] + scale_specs,
         out_spec,
         jax.ShapeDtypeStruct(shape, F32),
-        (side, *parts, feature_sum, *hidden_sums, *hidden_sums, *before),
+        (grad, feature_sum, *hidden_sums, *hidden_sums, *before),
         after,
         carry,
-        flops=3000 * features * total,
+        flops=1500 * features * total,
         name="write_update",
     )
 
@@ -285,6 +294,8 @@
     features = patches.shape[1]
     model, hidden_units = features * gx, width * gy
 
+    core = lax.axis_index("gx") % 2
+
     state = [lax.axis_index("gx").astype(jnp.int32)[None]]
 
     def run(function, *args, **kwargs):
@@ -304,22 +315,28 @@
     normed = (unit * ln_gain[None, :]).astype(BF16)
     normed_full = gather_rows(normed, "gy")
 
-    grad = share_sum(run(project, up_full, weight_out, 0, width, 1))
-    pre = share_sum(run(project, normed_full, weight_in, 0, width, 0))
-    up_side, normed_side = up_full.T, normed_full.T
+    (grad,) = run(project, up_full, weight_out, 1)
+    grad = share_sum(grad)
+
+    own = lax.dynamic_index_in_dim(normed_full.reshape(gx // 2, 2, -1, features), core, 1, keepdims=False)
+    other = lax.dynamic_index_in_dim(normed_full.reshape(gx // 2, 2, -1, features), 1 - core, 1, keepdims=False)
+    halves = jnp.concatenate([own, other]).reshape(normed_full.shape)
+    pre_own, pre_other = run(project, halves, weight_in, 0, 2)
+    pre_other = lax.ppermute(pre_other, "gx", [(i, i ^ 1) for i in range(gx)])
+    both = (pre_own.astype(F32) + pre_other.astype(F32)).astype(BF16)
+    (both,) = settle([grad], [both])[1]
+    pre = lax.psum_scatter(
+        both,
+        "gx",
+        scatter_dimension=0,
+        axis_index_groups=[list(range(c, gx, 2)) for c in (0, 1)],
+        tiled=True,
+    )
+    normed_side = normed_full.T
 
     def all_rows(share):
         return [lax.all_gather(share, "gx", axis=0)]
 
-    outer = {"pieces": [], "cols": [], "sums": None}
-    inner = {"pieces": [], "cols": [], "sums": None}
-
-    def take(side, parts, left, weight, start, dim):
-        cols, lanes, product = run(consume, parts, 0, left, weight, start, dim, side["sums"])
-        side["pieces"].append((parts, 0))
-        side["cols"].append(cols[0])
-        side["sums"] = (lanes, product)
-
     hidden, act = run(activate, pre, grad)
     act_parts, hidden_parts = all_rows(act), all_rows(hidden)
 
@@ -329,7 +346,9 @@
     mean_in, mean_out = mean_of(row_in, "gx"), mean_of(row_out, "gy")
     sizes = (float(model), float(hidden_units))
 
-    hidden_sum, feature_sum, normed_grad = run(consume, act_parts, normed_side, weight_in, 1, after=[mean_in, mean_out])
+    grad_in, hidden_sum, feature_sum, normed_grad = run(
+        consume, act_parts, normed_side, weight_in, 1, False, after=[mean_in, mean_out]
+    )
     feature_sum = all_sum(feature_sum, "gy")
     scaled = scatter_rows(normed_grad, "gy") * ln_gain[None, :]
     norm_sums = jnp.concatenate([jnp.sum(scaled, axis=1), jnp.sum(scaled * unit, axis=1)])[None, :]
@@ -338,15 +357,13 @@
     means = (hidden_sums[0] + hidden_sums[1])[0, width + 128 :].reshape(2, -1, 1) / model
     input_grad = upstream.astype(F32) + inv_std * (scaled - means[0] - unit * means[1])
     before = (row_in[None, :], col_in[None, :], mean_in)
-    update_in = run(
-        write_update, normed_side, act_parts, feature_sum, hidden_sums, before, sizes, False, after=[input_grad]
-    )
-
-    hidden_sum, feature_sum, branch = run(consume, hidden_parts, up_side, weight_out, 0)
+    update_in = run(write_update, grad_in, feature_sum, hidden_sums, before, sizes, False, after=[input_grad])
+
+    grad_out, hidden_sum, feature_sum, branch = run(consume, hidden_parts, up_full, weight_out, 0, True)
     feature_sum = all_sum(feature_sum, "gy")
     hidden_sums = all_sum(jnp.concatenate([hidden_sum, feature_sum[:1, features:]], axis=1), "gx", True)
     before = (col_out[None, :], row_out[None, :], mean_out)
-    update_out = run(write_update, up_full, hidden_parts, feature_sum, hidden_sums, before, sizes, True)
+    update_out = run(write_update, grad_out, feature_sum, hidden_sums, before, sizes, True)
     output = (x_float + scatter_rows(branch, "gy")).astype(BF16)
     return (output, input_grad, update_in, update_out)
 

time: 367 us -> 350 us (0.954)
  Pallas kernels: 83.5 us -> 70 us
  starting transfers between devices: 39.2 us -> 44.4 us
  other arithmetic: 12.3 us -> 7.35 us
    reduce_scatter x2 -> x1, waiting for transfers between devices: 109 us -> 32 us  [share_sum(): return lax.psum_scatter(partial, 'gx', scatter_dimension=0, tiled=True)]
    reduce_scatter x0 -> x1, waiting for transfers between devices: none -> 60.3 us  [body(): lax.psum_scatter(both, 'gx', scatter_dimension=0, axis_index_groups=[list...]
    all_gather x2, waiting for transfers between devices: 48.4 us -> 62.2 us  [all_rows(): return [lax.all_gather(share, 'gx', axis=0)]]
    pallas_call x7 -> x8, Pallas kernels: 83.5 us -> 70 us  [launch(): pl.pallas_call(wrapped, grid=grid, in_specs=list(in_specs) + idle * hidde...]
    ppermute x0 -> x1, waiting for transfers between devices: none -> 5.65 us  [body(): pre_other = lax.ppermute(pre_other, 'gx', [(i, i ^ 1) for i in range(gx)])]
    ppermute x25, starting transfers between devices: 23.8 us -> 28.7 us  [all_sum(): lax.ppermute(value, axis, [(i, i ^ bit * n) for i in range(size)])]
    ppermute x25, waiting for transfers between devices: 23.1 us -> 18.2 us  [all_sum(): lax.ppermute(value, axis, [(i, i ^ bit * n) for i in range(size)])]
  transfers between devices with their start and end apart: 41 -> 42, of which waited for: 23 -> 24; matrix products, arithmetic and copies ran while one was open for 5% -> 3% of each run, Pallas kernels for 14% -> 12%
where the time goes in v3:
time: 350 us
  waiting for transfers between devices  204 us (58%)
  Pallas kernels  70 us (20%)
  starting transfers between devices  44.4 us (13%)
  between operations  14.2 us (4%)
  local copies, waits for them, and re-layouts  9.52 us (3%)
  other arithmetic  7.35 us (2%)
    pallas_call x8, Pallas kernels, launch(): pl.pallas_call(wrapped, grid=grid, in_specs=list(in_specs) + idle * hidde...  70 us
    all_gather x2, waiting for transfers between devices, all_rows(): return [lax.all_gather(share, 'gx', axis=0)]  62.2 us
    reduce_scatter x1, waiting for transfers between devices, body(): lax.psum_scatter(both, 'gx', scatter_dimension=0, axis_index_groups=[list...  60.3 us
    reduce_scatter x1, waiting for transfers between devices, share_sum(): return lax.psum_scatter(partial, 'gx', scatter_dimension=0, tiled=True)  32 us
    ppermute x25, starting transfers between devices, all_sum(): lax.ppermute(value, axis, [(i, i ^ bit * n) for i in range(size)])  28.7 us
    ppermute x25, waiting for transfers between devices, all_sum(): lax.ppermute(value, axis, [(i, i ^ bit * n) for i in range(size)])  18.2 us
    ppermute x6, waiting for transfers between devices, gather_rows(): lax.ppermute(share, axis, [(i, i ^ bits) for i in range(size)])  15.8 us
    ppermute x6, waiting for transfers between devices, scatter_rows(): lax.ppermute(part, axis, [(i, i ^ bits) for i in range(size)]).astype(F32)  9.54 us
  transfers between devices with their start and end apart: 42, of which 24 were waited for; matrix products, arithmetic and copies ran while one was open for 3% of the time, Pallas kernels for 12%

profile of v3, /device:TPU:0, one launch (start us, length us, event | category | flops | bytes accessed | tf_op | source)
XLA Modules:
  0.0 349.6 jit_solution(773544041288265997)
XLA Ops:
  7.2 3.0 collective-permute-start
  10.2 1.5 collective-permute-start.2
  11.8 1.0 constant_dynamic-update-slice_fusion.3
  12.8 3.4 collective-permute-done
  16.2 6.0 %collective-permute-done.1 = bf16[128,768]{1,0:T(8,128)(2,1)S(1)} collective-permute-done((bf16[128,768]{1,0:T(8,128)(2,1)}, bf16[128,768]{1,0:T(8,128)(2,1)S(1)}, u32[]{:S(2)}, u32[]{:S(2)}) %collective-permute-start.1) | collective-permute-done | bytes 196640 | tf_op jit(solution)/shard_map/ppermute | solution.py:275
  22.3 8.5 %project.2 = (bf16[512,6144]{1,0:T(8,128)(2,1)S(1)}, s32[1]{0:T(128)}) custom-call(bf16[512,768]{1,0:T(8,128)(2,1)S(1)} %constant_dynamic-update-slice_fusion.refs_0_, bf16[6144,768]{1,0:T(8,128)(2,1)} %refs_1_.7, s32[1]{0:T(128)} %bitcast.refs_2_), custom_call_target="tpu_custom_call", output_to_operand_aliasing={{1}: (2, {})} | custom-call | flops 9663676416 | bytes 32212254 | tf_op jit(solution)/shard_map/project/pallas_call | solution.py:34
  30.8 2.7 copy-done
  33.5 0.8 copy-done.8
  34.5 1.6 collective-permute-start.4
  36.7 1.4 collective-permute-done.4
  38.2 1.0 collective-permute-done.5
  39.2 2.7 collective-permute-start.6
  41.8 1.9 collective-permute-done.6
  43.9 1.5 collective-permute-start.9
  45.4 1.5 collective-permute-start.8
  47.5 4.4 %collective-permute-done.9 = bf16[128,768]{1,0:T(8,128)(2,1)S(1)} collective-permute-done((bf16[128,768]{1,0:T(8,128)(2,1)S(1)}, bf16[128,768]{1,0:T(8,128)(2,1)S(1)}, u32[]{:S(2)}, u32[]{:S(2)}) %collective-permute-start.9) | collective-permute-done | bytes 196640 | tf_op jit(solution)/shard_map/ppermute | solution.py:275
  51.9 2.0 collective-permute-done.8
  54.1 9.0 %project.3 = (bf16[256,6144]{1,0:T(8,128)(2,1)S(1)}, bf16[256,6144]{1,0:T(8,128)(2,1)S(1)}, s32[1]{0:T(128)}) custom-call(bf16[512,768]{1,0:T(8,128)(2,1)S(1)} %bitcast.34, bf16[768,6144]{1,0:T(8,128)(2,1)} %refs_1_.6, s32[1]{0:T(128)} %get-tuple-element.26.refs_2_), custom_call_target="tpu_custom_call", output_to_operand_aliasing={{2}: (2, {})} | custom-call | flops 9663676416 | bytes 32212254 | tf_op jit(solution)/shard_map/project/pallas_call | solution.py:34
  63.2 5.6 %collective-permute-done.10 = bf16[256,6144]{1,0:T(8,128)(2,1)S(1)} collective-permute-done((bf16[256,6144]{1,0:T(8,128)(2,1)S(1)}, bf16[256,6144]{1,0:T(8,128)(2,1)S(1)}, u32[]{:S(2)}, u32[]{:S(2)}) %collective-permute-start.10) | collective-permute-done | bytes 3145760 | tf_op jit(solution)/shard_map/ppermute | solution.py:325
  68.9 2.8 add_convert_fusion.refs_1_
  71.7 32.0 %reduce-scatter.3.cloned.1.call-done.refs_0_.refs_1_ = bf16[64,6144]{1,0:T(8,128)(2,1)} async-done(((bf16[512,6144]{1,0:T(8,128)(2,1)}), bf16[64,6144]{1,0:T(8,128)(2,1)}) %reduce-scatter.3.cloned.1.call-update) | async-done | bytes 786448 | tf_op jit(solution)/shard_map/reduce_scatter | solution.py:307
  103.7 1.1 copy-done.1
  105.0 60.3 %reduce-scatter.5.cloned.1.call-done.refs_0_ = bf16[64,6144]{1,0:T(8,128)(2,1)} async-done(((bf16[256,6144]{1,0:T(8,128)(2,1)}), bf16[64,6144]{1,0:T(8,128)(2,1)}) %reduce-scatter.5.cloned.1.call-update) | async-done | bytes 786448 | tf_op jit(solution)/shard_map/reduce_scatter | solution.py:328
  165.3 1.1 copy-done.6
  166.4 2.9 activate.1
  169.9 0.6 reduce_sum.56
  170.5 0.6 broadcast_in_dim.33
  171.2 1.1 collective-permute-start.12
  172.3 1.1 collective-permute-start.11
  173.4 0.7 reduce_sum.57
  174.1 0.6 broadcast_in_dim.35
  174.7 1.5 collective-permute-start.16
  176.2 1.4 collective-permute-start.17
  178.2 0.7 add_add_fusion.6
  178.9 2.5 collective-permute-start.14
  181.4 0.6 add_add_fusion.5
  182.1 2.0 collective-permute-done.14
  184.1 1.2 copy.22.refs_0_
  185.3 49.0 %all-gather.7.cloned.1.call-done = bf16[8,64,6144]{2,1,0:T(8,128)(2,1)} async-done(((bf16[1,64,6144]{2,1,0:T(8,128)(2,1)}), bf16[8,64,6144]{2,1,0:T(8,128)(2,1)}) %all-gather.7.cloned.1.call-update) | async-done | bytes 6291472 | tf_op jit(solution)/shard_map/all_gather | solution.py:338
  234.3 14.9 %consume.2 = (bf16[768,6144]{1,0:T(8,128)(2,1)S(1)}, f32[1,6144]{1,0:T(1,128)S(1)}, f32[8,896]{1,0:T(8,128)S(1)}, bf16[512,768]{1,0:T(8,128)(2,1)S(1)}, s32[1]{0:T(128)}) custom-call(bf16[768,512]{1,0:T(8,128)(2,1)} %copy.22.refs_0_, bf16[768,6144]{1,0:T(8,128)(2,1)} %refs_1_.6, bf16[8,1,64,6144]{3,2,1,0:T(8,128)(2,1)} %bitcast.46, ...), custom_call_target="tpu_custom_call", output_to_operand_aliasing={{4}: (5, {})} | custom-call | flops 19327352832 | bytes 64424508 | tf_op jit(solution)/shard_map/consume/pallas_call | solution.py:34
  249.3 2.4 collective-permute-start.20
  252.9 1.5 collective-permute-start.21
  254.4 1.5 collective-permute-start.23
  256.4 4.3 %collective-permute-done.21 = bf16[128,768]{1,0:T(8,128)(2,1)S(1)} collective-permute-done((bf16[128,768]{1,0:T(8,128)(2,1)S(1)}, bf16[128,768]{1,0:T(8,128)(2,1)S(1)}, u32[]{:S(2)}, u32[]{:S(2)}) %collective-permute-start.21) | collective-permute-done | bytes 196640 | tf_op jit(solution)/shard_map/ppermute | solution.py:287
  260.8 3.9 %collective-permute-done.23 = bf16[128,768]{1,0:T(8,128)(2,1)S(1)} collective-permute-done((bf16[128,768]{1,0:T(8,128)(2,1)S(1)}, bf16[128,768]{1,0:T(8,128)(2,1)S(1)}, u32[]{:S(2)}, u32[]{:S(2)}) %collective-permute-start.23) | collective-permute-done | bytes 196640 | tf_op jit(solution)/shard_map/ppermute | solution.py:287
  264.7 1.1 collective-permute-done.22
  266.2 2.0 collective-permute-start.24
  268.2 3.0 collective-permute-done.25
  271.4 2.3 collective-permute-start.27
  273.7 3.9 %collective-permute-done.27.refs_3_.refs_5_ = f32[1,6528]{1,0:T(1,128)S(1)} collective-permute-done((f32[1,6528]{1,0:T(1,128)S(1)}, f32[1,6528]{1,0:T(1,128)S(1)}, u32[]{:S(2)}, u32[]{:S(2)}) %collective-permute-start.27) | collective-permute-done | bytes 26144 | tf_op jit(solution)/shard_map/ppermute | solution.py:261
  277.8 9.7 %write_update.2 = (f32[768,6144]{1,0:T(8,128)}, s32[1]{0:T(128)}) custom-call(bf16[768,6144]{1,0:T(8,128)(2,1)S(1)} %get-tuple-element.33.refs_0_, f32[8,896]{1,0:T(8,128)S(1)} %add_add_fusion.1.refs_1_, f32[1,6528]{1,0:T(1,128)S(1)} %add_add_fusion.2.refs_2_.refs_4_, ...), custom_call_target="tpu_custom_call", output_to_operand_aliasing={{1}: (10, {})} | custom-call | flops 7077888000 | bytes 23592960 | tf_op jit(solution)/shard_map/write_update/pallas_call | solution.py:34
  287.5 13.3 %all-gather.5.cloned.1.call-done = bf16[8,64,6144]{2,1,0:T(8,128)(2,1)} async-done(((bf16[1,64,6144]{2,1,0:T(8,128)(2,1)}), bf16[8,64,6144]{2,1,0:T(8,128)(2,1)}) %all-gather.5.cloned.1.call-update) | async-done | bytes 6291472 | tf_op jit(solution)/shard_map/all_gather | solution.py:338
  300.8 15.5 %consume.3 = (bf16[6144,768]{1,0:T(8,128)(2,1)S(1)}, f32[1,6144]{1,0:T(1,128)S(1)}, f32[8,896]{1,0:T(8,128)S(1)}, bf16[512,768]{1,0:T(8,128)(2,1)S(1)}, s32[1]{0:T(128)}) custom-call(bf16[512,768]{1,0:T(8,128)(2,1)} %copy-done.4, bf16[6144,768]{1,0:T(8,128)(2,1)} %refs_1_.7, bf16[8,1,64,6144]{3,2,1,0:T(8,128)(2,1)} %bitcast.45, ...), custom_call_target="tpu_custom_call", output_to_operand_aliasing={{4}: (3, {})} | custom-call | flops 19327352832 | bytes 64424508 | tf_op jit(solution)/shard_map/consume/pallas_call | solution.py:34
  316.4 2.5 collective-permute-start.33
  319.3 0.6 collective-permute-start.31
  319.9 1.3 collective-permute-done.33
  321.2 1.6 collective-permute-done.32
  323.4 2.0 collective-permute-start.34
  325.5 1.7 collective-permute-done.35
  327.2 1.8 collective-permute-start.37
  329.0 0.6 collective-permute-start.28
  329.7 2.3 collective-permute-start.30
  332.6 9.4 %write_update.3 = (f32[6144,768]{1,0:T(8,128)}, s32[1]{0:T(128)}) custom-call(bf16[6144,768]{1,0:T(8,128)(2,1)S(1)} %get-tuple-element.41.refs_0_, f32[8,896]{1,0:T(8,128)S(1)} %add_add_fusion.refs_1_, f32[1,6272]{1,0:T(1,128)S(1)} %add_add_fusion.3.refs_2_.refs_4_, ...), custom_call_target="tpu_custom_call", output_to_operand_aliasing={{1}: (9, {})} | custom-call | flops 7077888000 | bytes 23592960 | tf_op jit(solution)/shard_map/write_update/pallas_call | solution.py:34
  342.3 0.8 fusion.10
  (101 shorter events, 7.8 us)
Async XLA Ops:
  7.2 96.6 %reduce-scatter.3.cloned.1.call-start = ((), (), s32[]{:S(2)}) async-start(), calls=%async_computation.2 | async-start | bytes 7077888 | tf_op jit(solution)/shard_map/reduce_scatter | solution.py:307
  7.2 8.9 %collective-permute-start = (bf16[128,768]{1,0:T(8,128)(2,1)}, bf16[128,768]{1,0:T(8,128)(2,1)S(1)}, u32[]{:S(2)}, u32[]{:S(2)}) collective-permute-start(bf16[128,768]{1,0:T(8,128)(2,1)} %param.13), channel_id=1, source_target_pairs={{0,1},{1,0},{2,3},{3,2},{4,5},{5,4},{6,7},{7,6},{8,9},{9,8},{10,11... | collective-permute-start | bytes 589832 | tf_op jit(solution)/shard_map/ppermute | solution.py:275
  10.2 12.0 %collective-permute-start.2 = (bf16[128,768]{1,0:T(8,128)(2,1)}, bf16[128,768]{1,0:T(8,128)(2,1)S(1)}, u32[]{:S(2)}, u32[]{:S(2)}) collective-permute-start(bf16[128,768]{1,0:T(8,128)(2,1)} %param.13), channel_id=1, source_target_pairs={{0,3},{1,2},{2,1},{3,0},{4,7},{5,6},{6,5},{7,4},{8,11},{9,10},{10,... | collective-permute-start | bytes 589832 | tf_op jit(solution)/shard_map/ppermute | solution.py:275
  11.7 10.5 %collective-permute-start.1 = (bf16[128,768]{1,0:T(8,128)(2,1)}, bf16[128,768]{1,0:T(8,128)(2,1)S(1)}, u32[]{:S(2)}, u32[]{:S(2)}) collective-permute-start(bf16[128,768]{1,0:T(8,128)(2,1)} %param.13), channel_id=1, source_target_pairs={{0,2},{1,3},{2,0},{3,1},{4,6},{5,7},{6,4},{7,5},{8,10},{9,11},{10,... | collective-permute-start | bytes 589832 | tf_op jit(solution)/shard_map/ppermute | solution.py:275
  22.3 8.5 %copy-start.4 = (bf16[512,768]{1,0:T(8,128)(2,1)}, bf16[512,768]{1,0:T(8,128)(2,1)S(1)}, u32[]{:S(2)}) copy-start(bf16[512,768]{1,0:T(8,128)(2,1)S(1)} %constant_dynamic-update-slice_fusion.refs_0_) | copy-start | bytes 2359300
  30.7 2.7 copy-start
  33.5 0.9 copy-start.8
  33.5 10.3 %copy-start.10 = (f32[768]{0:T(1024)S(1)}, f32[768]{0:T(1024)}, u32[]{:S(2)}) copy-start(f32[768]{0:T(1024)} %param.10) | copy-start | bytes 9220
  33.5 131.8 %reduce-scatter.5.cloned.1.call-start = ((), (), s32[]{:S(2)}) async-start(), calls=%async_computation.3 | async-start | bytes 3932160 | tf_op jit(solution)/shard_map/reduce_scatter | solution.py:328
  34.5 3.6 %collective-permute-start.4 = (f32[2,128]{1,0:T(2,128)S(1)}, f32[2,128]{1,0:T(2,128)S(1)}, u32[]{:S(2)}, u32[]{:S(2)}) collective-permute-start(f32[2,128]{1,0:T(2,128)S(1)} %pad_maximum_fusion.4), channel_id=1, source_target_pairs={{0,8},{4,12},{8,0},{12,4},{16,24},{20,28},{24,16},{28,20},{1,9},{5... | collective-permute-start | bytes 3080 | tf_op jit(solution)/shard_map/ppermute | solution.py:261
  36.2 3.0 collective-permute-start.5
  36.2 3.0 collective-permute-start.3
  39.2 4.5 %collective-permute-start.6 = (f32[2,128]{1,0:T(2,128)S(1)}, f32[2,128]{1,0:T(2,128)S(1)}, u32[]{:S(2)}, u32[]{:S(2)}) collective-permute-start(f32[2,128]{1,0:T(2,128)S(1)} %add_add_fusion.4), channel_id=1, source_target_pairs={{0,16},{4,20},{8,24},{12,28},{16,0},{20,4},{24,8},{28,12},{1,17},{... | collective-permute-start | bytes 3080 | tf_op jit(solution)/shard_map/ppermute | solution.py:261
  43.9 8.0 %collective-permute-start.9 = (bf16[128,768]{1,0:T(8,128)(2,1)S(1)}, bf16[128,768]{1,0:T(8,128)(2,1)S(1)}, u32[]{:S(2)}, u32[]{:S(2)}) collective-permute-start(bf16[128,768]{1,0:T(8,128)(2,1)S(1)} %fusion.5), channel_id=1, source_target_pairs={{0,3},{1,2},{2,1},{3,0},{4,7},{5,6},{6,5},{7,4},{8,11},{9,10},{10,... | collective-permute-start | bytes 589832 | tf_op jit(solution)/shard_map/ppermute | solution.py:275
  45.4 8.4 %collective-permute-start.8 = (bf16[128,768]{1,0:T(8,128)(2,1)S(1)}, bf16[128,768]{1,0:T(8,128)(2,1)S(1)}, u32[]{:S(2)}, u32[]{:S(2)}) collective-permute-start(bf16[128,768]{1,0:T(8,128)(2,1)S(1)} %fusion.5), channel_id=1, source_target_pairs={{0,2},{1,3},{2,0},{3,1},{4,6},{5,7},{6,4},{7,5},{8,10},{9,11},{10,... | collective-permute-start | bytes 589832 | tf_op jit(solution)/shard_map/ppermute | solution.py:275
  46.9 6.9 %collective-permute-start.7 = (bf16[128,768]{1,0:T(8,128)(2,1)S(1)}, bf16[128,768]{1,0:T(8,128)(2,1)S(1)}, u32[]{:S(2)}, u32[]{:S(2)}) collective-permute-start(bf16[128,768]{1,0:T(8,128)(2,1)S(1)} %fusion.5), channel_id=1, source_target_pairs={{0,1},{1,0},{2,3},{3,2},{4,5},{5,4},{6,7},{7,6},{8,9},{9,8},{10,11... | collective-permute-start | bytes 589832 | tf_op jit(solution)/shard_map/ppermute | solution.py:275
  63.1 5.7 %collective-permute-start.10 = (bf16[256,6144]{1,0:T(8,128)(2,1)S(1)}, bf16[256,6144]{1,0:T(8,128)(2,1)S(1)}, u32[]{:S(2)}, u32[]{:S(2)}) collective-permute-start(bf16[256,6144]{1,0:T(8,128)(2,1)S(1)} %get-tuple-element.28), channel_id=1, source_target_pairs={{0,4},{4,0},{8,12},{12,8},{16,20},{20,16},{24,28},{28,24},{1,5},{5... | collective-permute-start | bytes 9437192 | tf_op jit(solution)/shard_map/ppermute | solution.py:325
  103.7 1.1 copy-start.1
  104.9 60.4 %copy-start.2 = (bf16[64,6144]{1,0:T(8,128)(2,1)S(1)}, bf16[64,6144]{1,0:T(8,128)(2,1)}, u32[]{:S(2)}) copy-start(bf16[64,6144]{1,0:T(8,128)(2,1)} %reduce-scatter.3.cloned.1.call-done.refs_0_.refs_1_) | copy-start | bytes 2359300
  104.9 65.0 %copy-start.11 = (f32[768]{0:T(1024)S(1)}, f32[768]{0:T(1024)}, u32[]{:S(2)}) copy-start(f32[768]{0:T(1024)} %param.14) | copy-start | bytes 9220
  104.9 68.5 %copy-start.5 = (f32[6144]{0:T(1024)S(1)}, f32[6144]{0:T(1024)}, u32[]{:S(2)}) copy-start(f32[6144]{0:T(1024)} %param.16) | copy-start | bytes 73732
  104.9 129.4 %all-gather.7.cloned.1.call-start = ((), (), s32[]{:S(2)}) async-start(), calls=%async_computation.5 | async-start | bytes 7077888 | tf_op jit(solution)/shard_map/all_gather | solution.py:338
  165.3 1.1 copy-start.6
  169.3 131.5 %all-gather.5.cloned.1.call-start = ((), (), s32[]{:S(2)}) async-start(), calls=%async_computation.4 | async-start | bytes 7077888 | tf_op jit(solution)/shard_map/all_gather | solution.py:338
  171.2 6.5 %collective-permute-start.12 = (f32[128]{0:T(128)S(1)}, f32[128]{0:T(128)S(1)}, u32[]{:S(2)}, u32[]{:S(2)}) collective-permute-start(f32[128]{0:T(128)S(1)} %broadcast_in_dim.33), channel_id=1, source_target_pairs={{0,8},{4,12},{8,0},{12,4},{16,24},{20,28},{24,16},{28,20},{1,9},{5... | collective-permute-start | bytes 1544 | tf_op jit(solution)/shard_map/ppermute | solution.py:261
  172.2 6.0 %collective-permute-start.13 = (f32[128]{0:T(128)S(1)}, f32[128]{0:T(128)S(1)}, u32[]{:S(2)}, u32[]{:S(2)}) collective-permute-start(f32[128]{0:T(128)S(1)} %broadcast_in_dim.33), channel_id=1, source_target_pairs={{0,12},{4,8},{8,4},{12,0},{16,28},{20,24},{24,20},{28,16},{1,13},{... | collective-permute-start | bytes 1544 | tf_op jit(solution)/shard_map/ppermute | solution.py:261
  172.3 6.0 %collective-permute-start.11 = (f32[128]{0:T(128)S(1)}, f32[128]{0:T(128)S(1)}, u32[]{:S(2)}, u32[]{:S(2)}) collective-permute-start(f32[128]{0:T(128)S(1)} %broadcast_in_dim.33), channel_id=1, source_target_pairs={{0,4},{4,0},{8,12},{12,8},{16,20},{20,16},{24,28},{28,24},{1,5},{5... | collective-permute-start | bytes 1544 | tf_op jit(solution)/shard_map/ppermute | solution.py:261
  174.7 6.8 %collective-permute-start.16 = (f32[128]{0:T(128)S(1)}, f32[128]{0:T(128)S(1)}, u32[]{:S(2)}, u32[]{:S(2)}) collective-permute-start(f32[128]{0:T(128)S(1)} %broadcast_in_dim.35), channel_id=1, source_target_pairs={{0,2},{1,3},{2,0},{3,1},{4,6},{5,7},{6,4},{7,5},{8,10},{9,11},{10,... | collective-permute-start | bytes 1544 | tf_op jit(solution)/shard_map/ppermute | solution.py:261
  176.2 5.2 %collective-permute-start.17 = (f32[128]{0:T(128)S(1)}, f32[128]{0:T(128)S(1)}, u32[]{:S(2)}, u32[]{:S(2)}) collective-permute-start(f32[128]{0:T(128)S(1)} %broadcast_in_dim.35), channel_id=1, source_target_pairs={{0,3},{1,2},{2,1},{3,0},{4,7},{5,6},{6,5},{7,4},{8,11},{9,10},{10,... | collective-permute-start | bytes 1544 | tf_op jit(solution)/shard_map/ppermute | solution.py:261
  177.7 3.8 %collective-permute-start.15 = (f32[128]{0:T(128)S(1)}, f32[128]{0:T(128)S(1)}, u32[]{:S(2)}, u32[]{:S(2)}) collective-permute-start(f32[128]{0:T(128)S(1)} %broadcast_in_dim.35), channel_id=1, source_target_pairs={{0,1},{1,0},{2,3},{3,2},{4,5},{5,4},{6,7},{7,6},{8,9},{9,8},{10,11... | collective-permute-start | bytes 1544 | tf_op jit(solution)/shard_map/ppermute | solution.py:261
  178.9 5.2 %collective-permute-start.14 = (f32[128]{0:T(128)S(1)}, f32[128]{0:T(128)S(1)}, u32[]{:S(2)}, u32[]{:S(2)}) collective-permute-start(f32[128]{0:T(128)S(1)} %add_add_fusion.6), channel_id=1, source_target_pairs={{0,16},{4,20},{8,24},{12,28},{16,0},{20,4},{24,8},{28,12},{1,17},{... | collective-permute-start | bytes 1544 | tf_op jit(solution)/shard_map/ppermute | solution.py:261
  234.3 43.3 %copy-start.9 = (bf16[128,768]{1,0:T(8,128)(2,1)S(1)}, bf16[128,768]{1,0:T(8,128)(2,1)}, u32[]{:S(2)}) copy-start(bf16[128,768]{1,0:T(8,128)(2,1)} %param.13) | copy-start | bytes 589828
  249.2 28.5 %copy-start.7 = (f32[6144]{0:T(1024)S(1)}, f32[6144]{0:T(1024)}, u32[]{:S(2)}) copy-start(f32[6144]{0:T(1024)} %param.15) | copy-start | bytes 73732
  249.3 6.6 %collective-permute-start.20 = (f32[8,896]{1,0:T(8,128)S(1)}, f32[8,896]{1,0:T(8,128)S(1)}, u32[]{:S(2)}, u32[]{:S(2)}) collective-permute-start(f32[8,896]{1,0:T(8,128)S(1)} %get-tuple-element.34), channel_id=1, source_target_pairs={{0,3},{1,2},{2,1},{3,0},{4,7},{5,6},{6,5},{7,4},{8,11},{9,10},{10,... | collective-permute-start | bytes 86024 | tf_op jit(solution)/shard_map/ppermute | solution.py:261
  251.7 4.7 %collective-permute-start.19 = (f32[8,896]{1,0:T(8,128)S(1)}, f32[8,896]{1,0:T(8,128)S(1)}, u32[]{:S(2)}, u32[]{:S(2)}) collective-permute-start(f32[8,896]{1,0:T(8,128)S(1)} %get-tuple-element.34), channel_id=1, source_target_pairs={{0,2},{1,3},{2,0},{3,1},{4,6},{5,7},{6,4},{7,5},{8,10},{9,11},{10,... | collective-permute-start | bytes 86024 | tf_op jit(solution)/shard_map/ppermute | solution.py:261
  252.3 4.2 %collective-permute-start.18 = (f32[8,896]{1,0:T(8,128)S(1)}, f32[8,896]{1,0:T(8,128)S(1)}, u32[]{:S(2)}, u32[]{:S(2)}) collective-permute-start(f32[8,896]{1,0:T(8,128)S(1)} %get-tuple-element.34), channel_id=1, source_target_pairs={{0,1},{1,0},{2,3},{3,2},{4,5},{5,4},{6,7},{7,6},{8,9},{9,8},{10,11... | collective-permute-start | bytes 86024 | tf_op jit(solution)/shard_map/ppermute | solution.py:261
  252.9 7.9 %collective-permute-start.21 = (bf16[128,768]{1,0:T(8,128)(2,1)S(1)}, bf16[128,768]{1,0:T(8,128)(2,1)S(1)}, u32[]{:S(2)}, u32[]{:S(2)}) collective-permute-start(bf16[128,768]{1,0:T(8,128)(2,1)S(1)} %get-tuple-element.54), channel_id=1, source_target_pairs={{0,1},{1,0},{2,3},{3,2},{4,5},{5,4},{6,7},{7,6},{8,9},{9,8},{10,11... | collective-permute-start | bytes 589832 | tf_op jit(solution)/shard_map/ppermute | solution.py:287
  254.4 10.3 %collective-permute-start.23 = (bf16[128,768]{1,0:T(8,128)(2,1)S(1)}, bf16[128,768]{1,0:T(8,128)(2,1)S(1)}, u32[]{:S(2)}, u32[]{:S(2)}) collective-permute-start(bf16[128,768]{1,0:T(8,128)(2,1)S(1)} %get-tuple-element.55), channel_id=1, source_target_pairs={{0,3},{1,2},{2,1},{3,0},{4,7},{5,6},{6,5},{7,4},{8,11},{9,10},{10,... | collective-permute-start | bytes 589832 | tf_op jit(solution)/shard_map/ppermute | solution.py:287
  255.9 9.9 %collective-permute-start.22 = (bf16[128,768]{1,0:T(8,128)(2,1)S(1)}, bf16[128,768]{1,0:T(8,128)(2,1)S(1)}, u32[]{:S(2)}, u32[]{:S(2)}) collective-permute-start(bf16[128,768]{1,0:T(8,128)(2,1)S(1)} %get-tuple-element.56), channel_id=1, source_target_pairs={{0,2},{1,3},{2,0},{3,1},{4,6},{5,7},{6,4},{7,5},{8,10},{9,11},{10,... | collective-permute-start | bytes 589832 | tf_op jit(solution)/shard_map/ppermute | solution.py:287
  266.0 5.2 %collective-permute-start.25 = (f32[1,6528]{1,0:T(1,128)S(1)}, f32[1,6528]{1,0:T(1,128)S(1)}, u32[]{:S(2)}, u32[]{:S(2)}) collective-permute-start(f32[1,6528]{1,0:T(1,128)S(1)} %pad_maximum_fusion.2), channel_id=1, source_target_pairs={{0,8},{4,12},{8,0},{12,4},{16,24},{20,28},{24,16},{28,20},{1,9},{5... | collective-permute-start | bytes 78344 | tf_op jit(solution)/shard_map/ppermute | solution.py:261
  266.1 5.2 %collective-permute-start.26 = (f32[1,6528]{1,0:T(1,128)S(1)}, f32[1,6528]{1,0:T(1,128)S(1)}, u32[]{:S(2)}, u32[]{:S(2)}) collective-permute-start(f32[1,6528]{1,0:T(1,128)S(1)} %pad_maximum_fusion.2), channel_id=1, source_target_pairs={{0,12},{4,8},{8,4},{12,0},{16,28},{20,24},{24,20},{28,16},{1,13},{... | collective-permute-start | bytes 78344 | tf_op jit(solution)/shard_map/ppermute | solution.py:261
  266.2 5.1 %collective-permute-start.24 = (f32[1,6528]{1,0:T(1,128)S(1)}, f32[1,6528]{1,0:T(1,128)S(1)}, u32[]{:S(2)}, u32[]{:S(2)}) collective-permute-start(f32[1,6528]{1,0:T(1,128)S(1)} %pad_maximum_fusion.2), channel_id=1, source_target_pairs={{0,4},{4,0},{8,12},{12,8},{16,20},{20,16},{24,28},{28,24},{1,5},{5... | collective-permute-start | bytes 78344 | tf_op jit(solution)/shard_map/ppermute | solution.py:261
  271.4 6.2 %collective-permute-start.27 = (f32[1,6528]{1,0:T(1,128)S(1)}, f32[1,6528]{1,0:T(1,128)S(1)}, u32[]{:S(2)}, u32[]{:S(2)}) collective-permute-start(f32[1,6528]{1,0:T(1,128)S(1)} %add_add_fusion.2.refs_2_.refs_4_), channel_id=1, source_target_pairs={{0,16},{4,20},{8,24},{12,28},{16,0},{20,4},{24,8},{28,12},{1,17},{... | collective-permute-start | bytes 78344 | tf_op jit(solution)/shard_map/ppermute | solution.py:261
  277.8 9.8 %copy-start.3 = (f32[128,768]{1,0:T(8,128)}, f32[128,768]{1,0:T(8,128)S(1)}, u32[]{:S(2)}) copy-start(f32[128,768]{1,0:T(8,128)S(1)} %fusion.9.refs_9_) | copy-start | bytes 1179652
  300.8 24.6 %copy-start.12 = (f32[768]{0:T(1024)S(1)}, f32[768]{0:T(1024)}, u32[]{:S(2)}) copy-start(f32[768]{0:T(1024)} %param.17) | copy-start | bytes 9220
  316.4 4.8 %collective-permute-start.33 = (f32[8,896]{1,0:T(8,128)S(1)}, f32[8,896]{1,0:T(8,128)S(1)}, u32[]{:S(2)}, u32[]{:S(2)}) collective-permute-start(f32[8,896]{1,0:T(8,128)S(1)} %get-tuple-element.42), channel_id=1, source_target_pairs={{0,3},{1,2},{2,1},{3,0},{4,7},{5,6},{6,5},{7,4},{8,11},{9,10},{10,... | collective-permute-start | bytes 86024 | tf_op jit(solution)/shard_map/ppermute | solution.py:261
  318.9 3.9 %collective-permute-start.32 = (f32[8,896]{1,0:T(8,128)S(1)}, f32[8,896]{1,0:T(8,128)S(1)}, u32[]{:S(2)}, u32[]{:S(2)}) collective-permute-start(f32[8,896]{1,0:T(8,128)S(1)} %get-tuple-element.42), channel_id=1, source_target_pairs={{0,2},{1,3},{2,0},{3,1},{4,6},{5,7},{6,4},{7,5},{8,10},{9,11},{10,... | collective-permute-start | bytes 86024 | tf_op jit(solution)/shard_map/ppermute | solution.py:261
  319.3 3.9 %collective-permute-start.31 = (f32[8,896]{1,0:T(8,128)S(1)}, f32[8,896]{1,0:T(8,128)S(1)}, u32[]{:S(2)}, u32[]{:S(2)}) collective-permute-start(f32[8,896]{1,0:T(8,128)S(1)} %get-tuple-element.42), channel_id=1, source_target_pairs={{0,1},{1,0},{2,3},{3,2},{4,5},{5,4},{6,7},{7,6},{8,9},{9,8},{10,11... | collective-permute-start | bytes 86024 | tf_op jit(solution)/shard_map/ppermute | solution.py:261
  323.2 3.9 %collective-permute-start.35 = (f32[1,6272]{1,0:T(1,128)S(1)}, f32[1,6272]{1,0:T(1,128)S(1)}, u32[]{:S(2)}, u32[]{:S(2)}) collective-permute-start(f32[1,6272]{1,0:T(1,128)S(1)} %pad_maximum_fusion.3), channel_id=1, source_target_pairs={{0,8},{4,12},{8,0},{12,4},{16,24},{20,28},{24,16},{28,20},{1,9},{5... | collective-permute-start | bytes 75272 | tf_op jit(solution)/shard_map/ppermute | solution.py:261
  323.3 3.8 %collective-permute-start.36 = (f32[1,6272]{1,0:T(1,128)S(1)}, f32[1,6272]{1,0:T(1,128)S(1)}, u32[]{:S(2)}, u32[]{:S(2)}) collective-permute-start(f32[1,6272]{1,0:T(1,128)S(1)} %pad_maximum_fusion.3), channel_id=1, source_target_pairs={{0,12},{4,8},{8,4},{12,0},{16,28},{20,24},{24,20},{28,16},{1,13},{... | collective-permute-start | bytes 75272 | tf_op jit(solution)/shard_map/ppermute | solution.py:261
  323.4 3.7 %collective-permute-start.34 = (f32[1,6272]{1,0:T(1,128)S(1)}, f32[1,6272]{1,0:T(1,128)S(1)}, u32[]{:S(2)}, u32[]{:S(2)}) collective-permute-start(f32[1,6272]{1,0:T(1,128)S(1)} %pad_maximum_fusion.3), channel_id=1, source_target_pairs={{0,4},{4,0},{8,12},{12,8},{16,20},{20,16},{24,28},{28,24},{1,5},{5... | collective-permute-start | bytes 75272 | tf_op jit(solution)/shard_map/ppermute | solution.py:261
  327.2 5.4 %collective-permute-start.37 = (f32[1,6272]{1,0:T(1,128)S(1)}, f32[1,6272]{1,0:T(1,128)S(1)}, u32[]{:S(2)}, u32[]{:S(2)}) collective-permute-start(f32[1,6272]{1,0:T(1,128)S(1)} %add_add_fusion.3.refs_2_.refs_4_), channel_id=1, source_target_pairs={{0,16},{4,20},{8,24},{12,28},{16,0},{20,4},{24,8},{28,12},{1,17},{... | collective-permute-start | bytes 75272 | tf_op jit(solution)/shard_map/ppermute | solution.py:261
  329.0 13.0 %collective-permute-start.28 = (bf16[128,768]{1,0:T(8,128)(2,1)S(1)}, bf16[128,768]{1,0:T(8,128)(2,1)S(1)}, u32[]{:S(2)}, u32[]{:S(2)}) collective-permute-start(bf16[128,768]{1,0:T(8,128)(2,1)S(1)} %get-tuple-element.51), channel_id=1, source_target_pairs={{0,1},{1,0},{2,3},{3,2},{4,5},{5,4},{6,7},{7,6},{8,9},{9,8},{10,11... | collective-permute-start | bytes 589832 | tf_op jit(solution)/shard_map/ppermute | solution.py:287
  329.7 12.4 %collective-permute-start.30 = (bf16[128,768]{1,0:T(8,128)(2,1)S(1)}, bf16[128,768]{1,0:T(8,128)(2,1)S(1)}, u32[]{:S(2)}, u32[]{:S(2)}) collective-permute-start(bf16[128,768]{1,0:T(8,128)(2,1)S(1)} %get-tuple-element.52), channel_id=1, source_target_pairs={{0,3},{1,2},{2,1},{3,0},{4,7},{5,6},{6,5},{7,4},{8,11},{9,10},{10,... | collective-permute-start | bytes 589832 | tf_op jit(solution)/shard_map/ppermute | solution.py:287
  332.0 10.3 %collective-permute-start.29 = (bf16[128,768]{1,0:T(8,128)(2,1)S(1)}, bf16[128,768]{1,0:T(8,128)(2,1)S(1)}, u32[]{:S(2)}, u32[]{:S(2)}) collective-permute-start(bf16[128,768]{1,0:T(8,128)(2,1)S(1)} %get-tuple-element.53), channel_id=1, source_target_pairs={{0,2},{1,3},{2,0},{3,1},{4,6},{5,7},{6,4},{7,5},{8,10},{9,11},{10,... | collective-permute-start | bytes 589832 | tf_op jit(solution)/shard_map/ppermute | solution.py:287
Sparse Core Ops, SparseCore 0:
  33.6 70.0 reduce-scatter.2
  106.6 58.6 reduce-scatter.4
  169.5 64.7 all-gather.6
  236.4 64.4 all-gather.4

commit v4 on v3

--- a/solution.py
+++ b/solution.py
@@ -20,7 +20,7 @@
     return best
 
 
-def launch(kernel, grid, in_specs, out_specs, out_shape, args, after=(), carry=(), scratch=(), flops=0, name="kernel"):
+def launch(kernel, grid, in_specs, out_specs, out_shape, args, after=(), carry=(), scratch=(), flops=0, vmem=VMEM, name="kernel"):
     many = isinstance(out_shape, list)
     shapes = out_shape if many else [out_shape]
     specs = out_specs if many else [out_specs]
@@ -39,7 +39,7 @@
         out_shape=shapes + [jax.ShapeDtypeStruct(c.shape, c.dtype) for c in carry],
         input_output_aliases={len(args) + len(after) + n: len(shapes) + n for n in range(len(carry))},
         scratch_shapes=list(scratch),
-        compiler_params=pltpu.CompilerParams(vmem_limit_bytes=VMEM),
+        compiler_params=pltpu.CompilerParams(vmem_limit_bytes=vmem),
         cost_estimate=pl.CostEstimate(flops=int(flops), bytes_accessed=int(flops / 300), transcendentals=0),
         name=name,
     )(*args, *after, *carry)
@@ -70,6 +70,7 @@
         after,
         carry,
         flops=4 * count * depth * width,
+        vmem=58 * 2**20,
         name="project",
     )
 
@@ -184,15 +185,16 @@
         after,
         carry,
         flops=1e9,
+        vmem=58 * 2**20,
         name="activate",
     )
 
 
 def settle(after, carry):
-    return launch(lambda: None, (1,), [], [], [], (), after, carry, name="settle")
-
-
-def write_update(grad, feature_sum, hidden_sums, before, sizes, hidden_rows, after=(), carry=(), limit=768):
+    return launch(lambda: None, (1,), [], [], [], (), after, carry, vmem=60 * 2**20, name="settle")
+
+
+def write_update(grad, feature_sum, hidden_sums, before, sizes, hidden_rows, after=(), carry=(), limit=1536):
     total, features = grad.shape if hidden_rows else grad.shape[::-1]
     step = block(total, limit)
     model, hidden_units = sizes

time: 350 us -> 350 us (level)
  local copies, waits for them, and re-layouts: 9.52 us -> 5.34 us
    reduce_scatter x1, waiting for transfers between devices: 32 us -> 27.7 us  [share_sum(): return lax.psum_scatter(partial, 'gx', scatter_dimension=0, tiled=True)]
    unnamed x29 -> x21, local copies, waits for them, and re-layouts: 6.88 us -> 2.79 us
  transfers between devices with their start and end apart: 42 -> 42, of which waited for: 24 -> 24; matrix products, arithmetic and copies ran while one was open for 3% -> 4% of each run, Pallas kernels for 12% -> 12%
where the time goes in v4:
time: 350 us; the launch traced here: 349 us
  waiting for transfers between devices  203 us (58%)
  Pallas kernels  72.7 us (21%)
  starting transfers between devices  44.3 us (13%)
  between operations  14.2 us (4%)
  other arithmetic  9.75 us (3%)
  local copies, waits for them, and re-layouts  5.34 us (2%)
    pallas_call x8, Pallas kernels, launch(): pl.pallas_call(wrapped, grid=grid, in_specs=list(in_specs) + idle * hidde...  72.7 us
    all_gather x2, waiting for transfers between devices, all_rows(): return [lax.all_gather(share, 'gx', axis=0)]  63.4 us
    reduce_scatter x1, waiting for transfers between devices, body(): lax.psum_scatter(both, 'gx', scatter_dimension=0, axis_index_groups=[list...  61.4 us
    ppermute x25, starting transfers between devices, all_sum(): lax.ppermute(value, axis, [(i, i ^ bit * n) for i in range(size)])  28.8 us
    reduce_scatter x1, waiting for transfers between devices, share_sum(): return lax.psum_scatter(partial, 'gx', scatter_dimension=0, tiled=True)  27.7 us
    ppermute x25, waiting for transfers between devices, all_sum(): lax.ppermute(value, axis, [(i, i ^ bit * n) for i in range(size)])  18.3 us
    ppermute x6, waiting for transfers between devices, gather_rows(): lax.ppermute(share, axis, [(i, i ^ bits) for i in range(size)])  15.8 us
    ppermute x6, waiting for transfers between devices, scatter_rows(): lax.ppermute(part, axis, [(i, i ^ bits) for i in range(size)]).astype(F32)  10.3 us
  transfers between devices with their start and end apart: 42, of which 24 were waited for; matrix products, arithmetic and copies ran while one was open for 4% of the time, Pallas kernels for 12%

profile of v4, /device:TPU:0, one launch (start us, length us, event | category | flops | bytes accessed | tf_op | source)
XLA Modules:
  0.0 349.4 jit_solution(14215108255726594534)
XLA Ops:
  7.2 3.0 collective-permute-start
  10.2 1.5 collective-permute-start.2
  11.8 1.0 constant_dynamic-update-slice_fusion.3
  12.8 3.4 collective-permute-done
  16.2 6.0 %collective-permute-done.1 = bf16[128,768]{1,0:T(8,128)(2,1)S(1)} collective-permute-done((bf16[128,768]{1,0:T(8,128)(2,1)}, bf16[128,768]{1,0:T(8,128)(2,1)S(1)}, u32[]{:S(2)}, u32[]{:S(2)}) %collective-permute-start.1) | collective-permute-done | bytes 196640 | tf_op jit(solution)/shard_map/ppermute | solution.py:277
  22.3 0.9 copy-done.5
  23.2 10.2 %project.2 = (bf16[512,6144]{1,0:T(8,128)(2,1)}, s32[1]{0:T(128)}) custom-call(bf16[512,768]{1,0:T(8,128)(2,1)} %copy-done.5, bf16[6144,768]{1,0:T(8,128)(2,1)} %refs_1_.7, s32[1]{0:T(128)} %bitcast.refs_2_), custom_call_target="tpu_custom_call", output_to_operand_aliasing={{1}: (2, {})} | custom-call | flops 9663676416 | bytes 32212254 | tf_op jit(solution)/shard_map/project/pallas_call | solution.py:34
  33.4 0.8 copy-done.3
  34.4 1.6 collective-permute-start.4
  36.6 1.4 collective-permute-done.4
  38.1 1.0 collective-permute-done.5
  39.1 2.6 collective-permute-start.6
  41.7 1.9 collective-permute-done.6
  43.8 1.5 collective-permute-start.9
  45.3 1.5 collective-permute-start.8
  47.4 4.4 %collective-permute-done.9 = bf16[128,768]{1,0:T(8,128)(2,1)S(1)} collective-permute-done((bf16[128,768]{1,0:T(8,128)(2,1)S(1)}, bf16[128,768]{1,0:T(8,128)(2,1)S(1)}, u32[]{:S(2)}, u32[]{:S(2)}) %collective-permute-start.9) | collective-permute-done | bytes 196640 | tf_op jit(solution)/shard_map/ppermute | solution.py:277
  51.8 2.0 collective-permute-done.8
  53.9 1.0 pad_maximum_fusion.1
  54.9 10.7 %project.3 = (bf16[256,6144]{1,0:T(8,128)(2,1)}, bf16[256,6144]{1,0:T(8,128)(2,1)}, s32[1]{0:T(128)}) custom-call(bf16[512,768]{1,0:T(8,128)(2,1)} %bitcast.37, bf16[768,6144]{1,0:T(8,128)(2,1)} %refs_1_.6, s32[1]{0:T(128)} %get-tuple-element.26.refs_2_), custom_call_target="tpu_custom_call", output_to_operand_aliasing={{2}: (2, {})} | custom-call | flops 9663676416 | bytes 32212254 | tf_op jit(solution)/shard_map/project/pallas_call | solution.py:34
  65.7 5.9 %collective-permute-done.10 = bf16[256,6144]{1,0:T(8,128)(2,1)S(1)} collective-permute-done((bf16[256,6144]{1,0:T(8,128)(2,1)}, bf16[256,6144]{1,0:T(8,128)(2,1)S(1)}, u32[]{:S(2)}, u32[]{:S(2)}) %collective-permute-start.10) | collective-permute-done | bytes 3145760 | tf_op jit(solution)/shard_map/ppermute | solution.py:327
  71.5 4.5 %add_convert_fusion.refs_1_ = bf16[256,6144]{1,0:T(8,128)(2,1)} fusion(bf16[256,6144]{1,0:T(8,128)(2,1)S(1)} %collective-permute-done.10, bf16[256,6144]{1,0:T(8,128)(2,1)} %get-tuple-element.27), kind=kLoop, calls=%fused_computation | loop fusion | flops 6291456 | bytes 9437184 | tf_op jit(solution)/shard_map/convert_element_type | solution.py:328
  76.0 27.7 %reduce-scatter.3.cloned.1.call-done.refs_0_.refs_1_ = bf16[64,6144]{1,0:T(8,128)(2,1)} async-done(((bf16[512,6144]{1,0:T(8,128)(2,1)}), bf16[64,6144]{1,0:T(8,128)(2,1)}) %reduce-scatter.3.cloned.1.call-update) | async-done | bytes 786448 | tf_op jit(solution)/shard_map/reduce_scatter | solution.py:309
  103.8 61.4 %reduce-scatter.5.cloned.1.call-done.refs_0_ = bf16[64,6144]{1,0:T(8,128)(2,1)} async-done(((bf16[256,6144]{1,0:T(8,128)(2,1)}), bf16[64,6144]{1,0:T(8,128)(2,1)}) %reduce-scatter.5.cloned.1.call-update) | async-done | bytes 786448 | tf_op jit(solution)/shard_map/reduce_scatter | solution.py:330
  165.2 3.9 %activate.1 = (bf16[1,64,6144]{2,1,0:T(8,128)(2,1)}, bf16[1,64,6144]{2,1,0:T(8,128)(2,1)}, s32[1]{0:T(128)}) custom-call(bf16[64,6144]{1,0:T(8,128)(2,1)} %reduce-scatter.5.cloned.1.call-done.refs_0_, bf16[64,6144]{1,0:T(8,128)(2,1)} %reduce-scatter.3.cloned.1.call-done.refs_0_.refs_1_, s32[1]{0:T(128)} %get-tuple-element.29.refs_2_), custom_call_target="tpu_custom_call", output_to_operand_aliasing={{2}: (2, {})} | custom-call | flops 1000000000 | bytes 3333333 | tf_op jit(solution)/shard_map/activate/pallas_call | solution.py:34
  169.7 0.6 reduce_sum.56
  170.3 0.6 broadcast_in_dim.33
  170.9 1.1 collective-permute-start.12
  172.0 1.1 collective-permute-start.11
  173.2 0.6 reduce_sum.57
  174.3 1.5 collective-permute-start.16
  175.9 1.4 collective-permute-start.17
  177.3 0.6 collective-permute-start.15
  177.9 0.7 add_add_fusion.6
  178.5 2.5 collective-permute-start.14
  181.7 2.1 collective-permute-done.14
  183.9 1.2 copy.22.refs_0_
  185.0 49.0 %all-gather.7.cloned.1.call-done = bf16[8,64,6144]{2,1,0:T(8,128)(2,1)} async-done(((bf16[1,64,6144]{2,1,0:T(8,128)(2,1)}), bf16[8,64,6144]{2,1,0:T(8,128)(2,1)}) %all-gather.7.cloned.1.call-update) | async-done | bytes 6291472 | tf_op jit(solution)/shard_map/all_gather | solution.py:340
  234.0 15.0 %consume.2 = (bf16[768,6144]{1,0:T(8,128)(2,1)S(1)}, f32[1,6144]{1,0:T(1,128)S(1)}, f32[8,896]{1,0:T(8,128)S(1)}, bf16[512,768]{1,0:T(8,128)(2,1)S(1)}, s32[1]{0:T(128)}) custom-call(bf16[768,512]{1,0:T(8,128)(2,1)} %copy.22.refs_0_, bf16[768,6144]{1,0:T(8,128)(2,1)} %refs_1_.6, bf16[8,1,64,6144]{3,2,1,0:T(8,128)(2,1)} %bitcast.46, ...), custom_call_target="tpu_custom_call", output_to_operand_aliasing={{4}: (5, {})} | custom-call | flops 19327352832 | bytes 64424508 | tf_op jit(solution)/shard_map/consume/pallas_call | solution.py:34
  249.0 2.5 collective-permute-start.20
  252.6 1.5 collective-permute-start.21
  254.2 1.5 collective-permute-start.23
  256.2 4.3 %collective-permute-done.21 = bf16[128,768]{1,0:T(8,128)(2,1)S(1)} collective-permute-done((bf16[128,768]{1,0:T(8,128)(2,1)S(1)}, bf16[128,768]{1,0:T(8,128)(2,1)S(1)}, u32[]{:S(2)}, u32[]{:S(2)}) %collective-permute-start.21) | collective-permute-done | bytes 196640 | tf_op jit(solution)/shard_map/ppermute | solution.py:289
  260.5 3.9 %collective-permute-done.23 = bf16[128,768]{1,0:T(8,128)(2,1)S(1)} collective-permute-done((bf16[128,768]{1,0:T(8,128)(2,1)S(1)}, bf16[128,768]{1,0:T(8,128)(2,1)S(1)}, u32[]{:S(2)}, u32[]{:S(2)}) %collective-permute-start.23) | collective-permute-done | bytes 196640 | tf_op jit(solution)/shard_map/ppermute | solution.py:289
  264.5 1.1 collective-permute-done.22
  266.0 2.0 collective-permute-start.24
  268.0 3.0 collective-permute-done.25
  271.1 2.3 collective-permute-start.27
  273.5 3.8 %collective-permute-done.27.refs_3_.refs_5_ = f32[1,6528]{1,0:T(1,128)S(1)} collective-permute-done((f32[1,6528]{1,0:T(1,128)S(1)}, f32[1,6528]{1,0:T(1,128)S(1)}, u32[]{:S(2)}, u32[]{:S(2)}) %collective-permute-start.27) | collective-permute-done | bytes 26144 | tf_op jit(solution)/shard_map/ppermute | solution.py:263
  277.5 8.7 %write_update.2 = (f32[768,6144]{1,0:T(8,128)}, s32[1]{0:T(128)}) custom-call(bf16[768,6144]{1,0:T(8,128)(2,1)S(1)} %get-tuple-element.33.refs_0_, f32[8,896]{1,0:T(8,128)S(1)} %add_add_fusion.1.refs_1_, f32[1,6528]{1,0:T(1,128)S(1)} %add_add_fusion.2.refs_2_.refs_4_, ...), custom_call_target="tpu_custom_call", output_to_operand_aliasing={{1}: (10, {})} | custom-call | flops 7077888000 | bytes 23592960 | tf_op jit(solution)/shard_map/write_update/pallas_call | solution.py:34
  286.2 14.4 %all-gather.5.cloned.1.call-done = bf16[8,64,6144]{2,1,0:T(8,128)(2,1)} async-done(((bf16[1,64,6144]{2,1,0:T(8,128)(2,1)}), bf16[8,64,6144]{2,1,0:T(8,128)(2,1)}) %all-gather.5.cloned.1.call-update) | async-done | bytes 6291472 | tf_op jit(solution)/shard_map/all_gather | solution.py:340
  300.6 15.5 %consume.3 = (bf16[6144,768]{1,0:T(8,128)(2,1)S(1)}, f32[1,6144]{1,0:T(1,128)S(1)}, f32[8,896]{1,0:T(8,128)S(1)}, bf16[512,768]{1,0:T(8,128)(2,1)S(1)}, s32[1]{0:T(128)}) custom-call(bf16[512,768]{1,0:T(8,128)(2,1)} %copy-done.5, bf16[6144,768]{1,0:T(8,128)(2,1)} %refs_1_.7, bf16[8,1,64,6144]{3,2,1,0:T(8,128)(2,1)} %bitcast.45, ...), custom_call_target="tpu_custom_call", output_to_operand_aliasing={{4}: (3, {})} | custom-call | flops 19327352832 | bytes 64424508 | tf_op jit(solution)/shard_map/consume/pallas_call | solution.py:34
  316.1 2.5 collective-permute-start.33
  319.1 0.6 collective-permute-start.31
  319.7 1.3 collective-permute-done.33
  321.0 1.6 collective-permute-done.32
  323.2 2.0 collective-permute-start.34
  325.2 1.7 collective-permute-done.35
  327.0 1.8 collective-permute-start.37
  328.8 0.6 collective-permute-start.28
  329.4 2.3 collective-permute-start.30
  331.7 0.6 collective-permute-start.29
  332.3 8.7 %write_update.3 = (f32[6144,768]{1,0:T(8,128)}, s32[1]{0:T(128)}) custom-call(bf16[6144,768]{1,0:T(8,128)(2,1)S(1)} %get-tuple-element.41.refs_0_, f32[8,896]{1,0:T(8,128)S(1)} %add_add_fusion.refs_1_, f32[1,6272]{1,0:T(1,128)S(1)} %add_add_fusion.3.refs_2_.refs_4_, ...), custom_call_target="tpu_custom_call", output_to_operand_aliasing={{1}: (9, {})} | custom-call | flops 7077888000 | bytes 23592960 | tf_op jit(solution)/shard_map/write_update/pallas_call | solution.py:34
  341.1 1.0 collective-permute-done.29
  342.0 0.8 fusion.10
  (93 shorter events, 7.3 us)
Async XLA Ops:
  7.2 96.5 %reduce-scatter.3.cloned.1.call-start = ((), (), s32[]{:S(2)}) async-start(), calls=%async_computation.2 | async-start | bytes 7077888 | tf_op jit(solution)/shard_map/reduce_scatter | solution.py:309
  7.2 8.9 %collective-permute-start = (bf16[128,768]{1,0:T(8,128)(2,1)}, bf16[128,768]{1,0:T(8,128)(2,1)S(1)}, u32[]{:S(2)}, u32[]{:S(2)}) collective-permute-start(bf16[128,768]{1,0:T(8,128)(2,1)} %param.13), channel_id=1, source_target_pairs={{0,1},{1,0},{2,3},{3,2},{4,5},{5,4},{6,7},{7,6},{8,9},{9,8},{10,11... | collective-permute-start | bytes 589832 | tf_op jit(solution)/shard_map/ppermute | solution.py:277
  10.2 12.0 %collective-permute-start.2 = (bf16[128,768]{1,0:T(8,128)(2,1)}, bf16[128,768]{1,0:T(8,128)(2,1)S(1)}, u32[]{:S(2)}, u32[]{:S(2)}) collective-permute-start(bf16[128,768]{1,0:T(8,128)(2,1)} %param.13), channel_id=1, source_target_pairs={{0,3},{1,2},{2,1},{3,0},{4,7},{5,6},{6,5},{7,4},{8,11},{9,10},{10,... | collective-permute-start | bytes 589832 | tf_op jit(solution)/shard_map/ppermute | solution.py:277
  11.7 10.5 %collective-permute-start.1 = (bf16[128,768]{1,0:T(8,128)(2,1)}, bf16[128,768]{1,0:T(8,128)(2,1)S(1)}, u32[]{:S(2)}, u32[]{:S(2)}) collective-permute-start(bf16[128,768]{1,0:T(8,128)(2,1)} %param.13), channel_id=1, source_target_pairs={{0,2},{1,3},{2,0},{3,1},{4,6},{5,7},{6,4},{7,5},{8,10},{9,11},{10,... | collective-permute-start | bytes 589832 | tf_op jit(solution)/shard_map/ppermute | solution.py:277
  22.3 0.9 copy-start.5
  33.4 0.9 copy-start.3
  33.4 10.3 %copy-start.6 = (f32[768]{0:T(1024)S(1)}, f32[768]{0:T(1024)}, u32[]{:S(2)}) copy-start(f32[768]{0:T(1024)} %param.10) | copy-start | bytes 9220
  33.4 131.8 %reduce-scatter.5.cloned.1.call-start = ((), (), s32[]{:S(2)}) async-start(), calls=%async_computation.3 | async-start | bytes 3932160 | tf_op jit(solution)/shard_map/reduce_scatter | solution.py:330
  34.4 3.6 %collective-permute-start.4 = (f32[2,128]{1,0:T(2,128)S(1)}, f32[2,128]{1,0:T(2,128)S(1)}, u32[]{:S(2)}, u32[]{:S(2)}) collective-permute-start(f32[2,128]{1,0:T(2,128)S(1)} %pad_maximum_fusion.4), channel_id=1, source_target_pairs={{0,8},{4,12},{8,0},{12,4},{16,24},{20,28},{24,16},{28,20},{1,9},{5... | collective-permute-start | bytes 3080 | tf_op jit(solution)/shard_map/ppermute | solution.py:263
  36.1 3.0 collective-permute-start.5
  36.1 3.0 collective-permute-start.3
  39.1 4.5 %collective-permute-start.6 = (f32[2,128]{1,0:T(2,128)S(1)}, f32[2,128]{1,0:T(2,128)S(1)}, u32[]{:S(2)}, u32[]{:S(2)}) collective-permute-start(f32[2,128]{1,0:T(2,128)S(1)} %add_add_fusion.4), channel_id=1, source_target_pairs={{0,16},{4,20},{8,24},{12,28},{16,0},{20,4},{24,8},{28,12},{1,17},{... | collective-permute-start | bytes 3080 | tf_op jit(solution)/shard_map/ppermute | solution.py:263
  43.8 8.0 %collective-permute-start.9 = (bf16[128,768]{1,0:T(8,128)(2,1)S(1)}, bf16[128,768]{1,0:T(8,128)(2,1)S(1)}, u32[]{:S(2)}, u32[]{:S(2)}) collective-permute-start(bf16[128,768]{1,0:T(8,128)(2,1)S(1)} %fusion.5), channel_id=1, source_target_pairs={{0,3},{1,2},{2,1},{3,0},{4,7},{5,6},{6,5},{7,4},{8,11},{9,10},{10,... | collective-permute-start | bytes 589832 | tf_op jit(solution)/shard_map/ppermute | solution.py:277
  45.3 8.4 %collective-permute-start.8 = (bf16[128,768]{1,0:T(8,128)(2,1)S(1)}, bf16[128,768]{1,0:T(8,128)(2,1)S(1)}, u32[]{:S(2)}, u32[]{:S(2)}) collective-permute-start(bf16[128,768]{1,0:T(8,128)(2,1)S(1)} %fusion.5), channel_id=1, source_target_pairs={{0,2},{1,3},{2,0},{3,1},{4,6},{5,7},{6,4},{7,5},{8,10},{9,11},{10,... | collective-permute-start | bytes 589832 | tf_op jit(solution)/shard_map/ppermute | solution.py:277
  46.8 6.9 %collective-permute-start.7 = (bf16[128,768]{1,0:T(8,128)(2,1)S(1)}, bf16[128,768]{1,0:T(8,128)(2,1)S(1)}, u32[]{:S(2)}, u32[]{:S(2)}) collective-permute-start(bf16[128,768]{1,0:T(8,128)(2,1)S(1)} %fusion.5), channel_id=1, source_target_pairs={{0,1},{1,0},{2,3},{3,2},{4,5},{5,4},{6,7},{7,6},{8,9},{9,8},{10,11... | collective-permute-start | bytes 589832 | tf_op jit(solution)/shard_map/ppermute | solution.py:277
  65.6 5.9 %collective-permute-start.10 = (bf16[256,6144]{1,0:T(8,128)(2,1)}, bf16[256,6144]{1,0:T(8,128)(2,1)S(1)}, u32[]{:S(2)}, u32[]{:S(2)}) collective-permute-start(bf16[256,6144]{1,0:T(8,128)(2,1)} %get-tuple-element.28), channel_id=1, source_target_pairs={{0,4},{4,0},{8,12},{12,8},{16,20},{20,16},{24,28},{28,24},{1,5},{5... | collective-permute-start | bytes 9437192 | tf_op jit(solution)/shard_map/ppermute | solution.py:327
  103.7 66.0 %copy-start.7 = (f32[768]{0:T(1024)S(1)}, f32[768]{0:T(1024)}, u32[]{:S(2)}) copy-start(f32[768]{0:T(1024)} %param.14) | copy-start | bytes 9220
  103.7 69.5 %copy-start.1 = (f32[6144]{0:T(1024)S(1)}, f32[6144]{0:T(1024)}, u32[]{:S(2)}) copy-start(f32[6144]{0:T(1024)} %param.16) | copy-start | bytes 73732
  103.7 130.3 %all-gather.7.cloned.1.call-start = ((), (), s32[]{:S(2)}) async-start(), calls=%async_computation.5 | async-start | bytes 7077888 | tf_op jit(solution)/shard_map/all_gather | solution.py:340
  169.1 131.5 %all-gather.5.cloned.1.call-start = ((), (), s32[]{:S(2)}) async-start(), calls=%async_computation.4 | async-start | bytes 7077888 | tf_op jit(solution)/shard_map/all_gather | solution.py:340
  170.9 6.4 %collective-permute-start.12 = (f32[128]{0:T(128)S(1)}, f32[128]{0:T(128)S(1)}, u32[]{:S(2)}, u32[]{:S(2)}) collective-permute-start(f32[128]{0:T(128)S(1)} %broadcast_in_dim.33), channel_id=1, source_target_pairs={{0,8},{4,12},{8,0},{12,4},{16,24},{20,28},{24,16},{28,20},{1,9},{5... | collective-permute-start | bytes 1544 | tf_op jit(solution)/shard_map/ppermute | solution.py:263
  172.0 5.9 %collective-permute-start.13 = (f32[128]{0:T(128)S(1)}, f32[128]{0:T(128)S(1)}, u32[]{:S(2)}, u32[]{:S(2)}) collective-permute-start(f32[128]{0:T(128)S(1)} %broadcast_in_dim.33), channel_id=1, source_target_pairs={{0,12},{4,8},{8,4},{12,0},{16,28},{20,24},{24,20},{28,16},{1,13},{... | collective-permute-start | bytes 1544 | tf_op jit(solution)/shard_map/ppermute | solution.py:263
  172.0 5.9 %collective-permute-start.11 = (f32[128]{0:T(128)S(1)}, f32[128]{0:T(128)S(1)}, u32[]{:S(2)}, u32[]{:S(2)}) collective-permute-start(f32[128]{0:T(128)S(1)} %broadcast_in_dim.33), channel_id=1, source_target_pairs={{0,4},{4,0},{8,12},{12,8},{16,20},{20,16},{24,28},{28,24},{1,5},{5... | collective-permute-start | bytes 1544 | tf_op jit(solution)/shard_map/ppermute | solution.py:263
  174.3 6.8 %collective-permute-start.16 = (f32[128]{0:T(128)S(1)}, f32[128]{0:T(128)S(1)}, u32[]{:S(2)}, u32[]{:S(2)}) collective-permute-start(f32[128]{0:T(128)S(1)} %broadcast_in_dim.35), channel_id=1, source_target_pairs={{0,2},{1,3},{2,0},{3,1},{4,6},{5,7},{6,4},{7,5},{8,10},{9,11},{10,... | collective-permute-start | bytes 1544 | tf_op jit(solution)/shard_map/ppermute | solution.py:263
  175.9 5.2 %collective-permute-start.17 = (f32[128]{0:T(128)S(1)}, f32[128]{0:T(128)S(1)}, u32[]{:S(2)}, u32[]{:S(2)}) collective-permute-start(f32[128]{0:T(128)S(1)} %broadcast_in_dim.35), channel_id=1, source_target_pairs={{0,3},{1,2},{2,1},{3,0},{4,7},{5,6},{6,5},{7,4},{8,11},{9,10},{10,... | collective-permute-start | bytes 1544 | tf_op jit(solution)/shard_map/ppermute | solution.py:263
  177.3 3.8 %collective-permute-start.15 = (f32[128]{0:T(128)S(1)}, f32[128]{0:T(128)S(1)}, u32[]{:S(2)}, u32[]{:S(2)}) collective-permute-start(f32[128]{0:T(128)S(1)} %broadcast_in_dim.35), channel_id=1, source_target_pairs={{0,1},{1,0},{2,3},{3,2},{4,5},{5,4},{6,7},{7,6},{8,9},{9,8},{10,11... | collective-permute-start | bytes 1544 | tf_op jit(solution)/shard_map/ppermute | solution.py:263
  178.5 5.3 %collective-permute-start.14 = (f32[128]{0:T(128)S(1)}, f32[128]{0:T(128)S(1)}, u32[]{:S(2)}, u32[]{:S(2)}) collective-permute-start(f32[128]{0:T(128)S(1)} %add_add_fusion.6), channel_id=1, source_target_pairs={{0,16},{4,20},{8,24},{12,28},{16,0},{20,4},{24,8},{28,12},{1,17},{... | collective-permute-start | bytes 1544 | tf_op jit(solution)/shard_map/ppermute | solution.py:263
  234.0 43.2 %copy-start.4 = (bf16[128,768]{1,0:T(8,128)(2,1)S(1)}, bf16[128,768]{1,0:T(8,128)(2,1)}, u32[]{:S(2)}) copy-start(bf16[128,768]{1,0:T(8,128)(2,1)} %param.13) | copy-start | bytes 589828
  249.0 28.5 %copy-start.2 = (f32[6144]{0:T(1024)S(1)}, f32[6144]{0:T(1024)}, u32[]{:S(2)}) copy-start(f32[6144]{0:T(1024)} %param.15) | copy-start | bytes 73732
  249.0 6.6 %collective-permute-start.20 = (f32[8,896]{1,0:T(8,128)S(1)}, f32[8,896]{1,0:T(8,128)S(1)}, u32[]{:S(2)}, u32[]{:S(2)}) collective-permute-start(f32[8,896]{1,0:T(8,128)S(1)} %get-tuple-element.34), channel_id=1, source_target_pairs={{0,3},{1,2},{2,1},{3,0},{4,7},{5,6},{6,5},{7,4},{8,11},{9,10},{10,... | collective-permute-start | bytes 86024 | tf_op jit(solution)/shard_map/ppermute | solution.py:263
  251.5 4.7 %collective-permute-start.19 = (f32[8,896]{1,0:T(8,128)S(1)}, f32[8,896]{1,0:T(8,128)S(1)}, u32[]{:S(2)}, u32[]{:S(2)}) collective-permute-start(f32[8,896]{1,0:T(8,128)S(1)} %get-tuple-element.34), channel_id=1, source_target_pairs={{0,2},{1,3},{2,0},{3,1},{4,6},{5,7},{6,4},{7,5},{8,10},{9,11},{10,... | collective-permute-start | bytes 86024 | tf_op jit(solution)/shard_map/ppermute | solution.py:263
  252.0 4.2 %collective-permute-start.18 = (f32[8,896]{1,0:T(8,128)S(1)}, f32[8,896]{1,0:T(8,128)S(1)}, u32[]{:S(2)}, u32[]{:S(2)}) collective-permute-start(f32[8,896]{1,0:T(8,128)S(1)} %get-tuple-element.34), channel_id=1, source_target_pairs={{0,1},{1,0},{2,3},{3,2},{4,5},{5,4},{6,7},{7,6},{8,9},{9,8},{10,11... | collective-permute-start | bytes 86024 | tf_op jit(solution)/shard_map/ppermute | solution.py:263
  252.6 7.9 %collective-permute-start.21 = (bf16[128,768]{1,0:T(8,128)(2,1)S(1)}, bf16[128,768]{1,0:T(8,128)(2,1)S(1)}, u32[]{:S(2)}, u32[]{:S(2)}) collective-permute-start(bf16[128,768]{1,0:T(8,128)(2,1)S(1)} %get-tuple-element.54), channel_id=1, source_target_pairs={{0,1},{1,0},{2,3},{3,2},{4,5},{5,4},{6,7},{7,6},{8,9},{9,8},{10,11... | collective-permute-start | bytes 589832 | tf_op jit(solution)/shard_map/ppermute | solution.py:289
  254.2 10.3 %collective-permute-start.23 = (bf16[128,768]{1,0:T(8,128)(2,1)S(1)}, bf16[128,768]{1,0:T(8,128)(2,1)S(1)}, u32[]{:S(2)}, u32[]{:S(2)}) collective-permute-start(bf16[128,768]{1,0:T(8,128)(2,1)S(1)} %get-tuple-element.55), channel_id=1, source_target_pairs={{0,3},{1,2},{2,1},{3,0},{4,7},{5,6},{6,5},{7,4},{8,11},{9,10},{10,... | collective-permute-start | bytes 589832 | tf_op jit(solution)/shard_map/ppermute | solution.py:289
  255.6 9.9 %collective-permute-start.22 = (bf16[128,768]{1,0:T(8,128)(2,1)S(1)}, bf16[128,768]{1,0:T(8,128)(2,1)S(1)}, u32[]{:S(2)}, u32[]{:S(2)}) collective-permute-start(bf16[128,768]{1,0:T(8,128)(2,1)S(1)} %get-tuple-element.56), channel_id=1, source_target_pairs={{0,2},{1,3},{2,0},{3,1},{4,6},{5,7},{6,4},{7,5},{8,10},{9,11},{10,... | collective-permute-start | bytes 589832 | tf_op jit(solution)/shard_map/ppermute | solution.py:289
  265.8 5.2 %collective-permute-start.25 = (f32[1,6528]{1,0:T(1,128)S(1)}, f32[1,6528]{1,0:T(1,128)S(1)}, u32[]{:S(2)}, u32[]{:S(2)}) collective-permute-start(f32[1,6528]{1,0:T(1,128)S(1)} %pad_maximum_fusion.2), channel_id=1, source_target_pairs={{0,8},{4,12},{8,0},{12,4},{16,24},{20,28},{24,16},{28,20},{1,9},{5... | collective-permute-start | bytes 78344 | tf_op jit(solution)/shard_map/ppermute | solution.py:263
  265.9 5.2 %collective-permute-start.26 = (f32[1,6528]{1,0:T(1,128)S(1)}, f32[1,6528]{1,0:T(1,128)S(1)}, u32[]{:S(2)}, u32[]{:S(2)}) collective-permute-start(f32[1,6528]{1,0:T(1,128)S(1)} %pad_maximum_fusion.2), channel_id=1, source_target_pairs={{0,12},{4,8},{8,4},{12,0},{16,28},{20,24},{24,20},{28,16},{1,13},{... | collective-permute-start | bytes 78344 | tf_op jit(solution)/shard_map/ppermute | solution.py:263
  266.0 5.1 %collective-permute-start.24 = (f32[1,6528]{1,0:T(1,128)S(1)}, f32[1,6528]{1,0:T(1,128)S(1)}, u32[]{:S(2)}, u32[]{:S(2)}) collective-permute-start(f32[1,6528]{1,0:T(1,128)S(1)} %pad_maximum_fusion.2), channel_id=1, source_target_pairs={{0,4},{4,0},{8,12},{12,8},{16,20},{20,16},{24,28},{28,24},{1,5},{5... | collective-permute-start | bytes 78344 | tf_op jit(solution)/shard_map/ppermute | solution.py:263
  271.1 6.1 %collective-permute-start.27 = (f32[1,6528]{1,0:T(1,128)S(1)}, f32[1,6528]{1,0:T(1,128)S(1)}, u32[]{:S(2)}, u32[]{:S(2)}) collective-permute-start(f32[1,6528]{1,0:T(1,128)S(1)} %add_add_fusion.2.refs_2_.refs_4_), channel_id=1, source_target_pairs={{0,16},{4,20},{8,24},{12,28},{16,0},{20,4},{24,8},{28,12},{1,17},{... | collective-permute-start | bytes 78344 | tf_op jit(solution)/shard_map/ppermute | solution.py:263
  277.5 8.7 %copy-start = (f32[128,768]{1,0:T(8,128)}, f32[128,768]{1,0:T(8,128)S(1)}, u32[]{:S(2)}) copy-start(f32[128,768]{1,0:T(8,128)S(1)} %fusion.9.refs_9_) | copy-start | bytes 1179652
  300.6 24.6 %copy-start.8 = (f32[768]{0:T(1024)S(1)}, f32[768]{0:T(1024)}, u32[]{:S(2)}) copy-start(f32[768]{0:T(1024)} %param.17) | copy-start | bytes 9220
  316.1 4.8 %collective-permute-start.33 = (f32[8,896]{1,0:T(8,128)S(1)}, f32[8,896]{1,0:T(8,128)S(1)}, u32[]{:S(2)}, u32[]{:S(2)}) collective-permute-start(f32[8,896]{1,0:T(8,128)S(1)} %get-tuple-element.42), channel_id=1, source_target_pairs={{0,3},{1,2},{2,1},{3,0},{4,7},{5,6},{6,5},{7,4},{8,11},{9,10},{10,... | collective-permute-start | bytes 86024 | tf_op jit(solution)/shard_map/ppermute | solution.py:263
  318.7 3.9 %collective-permute-start.32 = (f32[8,896]{1,0:T(8,128)S(1)}, f32[8,896]{1,0:T(8,128)S(1)}, u32[]{:S(2)}, u32[]{:S(2)}) collective-permute-start(f32[8,896]{1,0:T(8,128)S(1)} %get-tuple-element.42), channel_id=1, source_target_pairs={{0,2},{1,3},{2,0},{3,1},{4,6},{5,7},{6,4},{7,5},{8,10},{9,11},{10,... | collective-permute-start | bytes 86024 | tf_op jit(solution)/shard_map/ppermute | solution.py:263
  319.1 3.9 %collective-permute-start.31 = (f32[8,896]{1,0:T(8,128)S(1)}, f32[8,896]{1,0:T(8,128)S(1)}, u32[]{:S(2)}, u32[]{:S(2)}) collective-permute-start(f32[8,896]{1,0:T(8,128)S(1)} %get-tuple-element.42), channel_id=1, source_target_pairs={{0,1},{1,0},{2,3},{3,2},{4,5},{5,4},{6,7},{7,6},{8,9},{9,8},{10,11... | collective-permute-start | bytes 86024 | tf_op jit(solution)/shard_map/ppermute | solution.py:263
  323.0 3.9 %collective-permute-start.35 = (f32[1,6272]{1,0:T(1,128)S(1)}, f32[1,6272]{1,0:T(1,128)S(1)}, u32[]{:S(2)}, u32[]{:S(2)}) collective-permute-start(f32[1,6272]{1,0:T(1,128)S(1)} %pad_maximum_fusion.3), channel_id=1, source_target_pairs={{0,8},{4,12},{8,0},{12,4},{16,24},{20,28},{24,16},{28,20},{1,9},{5... | collective-permute-start | bytes 75272 | tf_op jit(solution)/shard_map/ppermute | solution.py:263
  323.1 3.8 %collective-permute-start.36 = (f32[1,6272]{1,0:T(1,128)S(1)}, f32[1,6272]{1,0:T(1,128)S(1)}, u32[]{:S(2)}, u32[]{:S(2)}) collective-permute-start(f32[1,6272]{1,0:T(1,128)S(1)} %pad_maximum_fusion.3), channel_id=1, source_target_pairs={{0,12},{4,8},{8,4},{12,0},{16,28},{20,24},{24,20},{28,16},{1,13},{... | collective-permute-start | bytes 75272 | tf_op jit(solution)/shard_map/ppermute | solution.py:263
  323.2 3.7 %collective-permute-start.34 = (f32[1,6272]{1,0:T(1,128)S(1)}, f32[1,6272]{1,0:T(1,128)S(1)}, u32[]{:S(2)}, u32[]{:S(2)}) collective-permute-start(f32[1,6272]{1,0:T(1,128)S(1)} %pad_maximum_fusion.3), channel_id=1, source_target_pairs={{0,4},{4,0},{8,12},{12,8},{16,20},{20,16},{24,28},{28,24},{1,5},{5... | collective-permute-start | bytes 75272 | tf_op jit(solution)/shard_map/ppermute | solution.py:263
  327.0 5.4 %collective-permute-start.37 = (f32[1,6272]{1,0:T(1,128)S(1)}, f32[1,6272]{1,0:T(1,128)S(1)}, u32[]{:S(2)}, u32[]{:S(2)}) collective-permute-start(f32[1,6272]{1,0:T(1,128)S(1)} %add_add_fusion.3.refs_2_.refs_4_), channel_id=1, source_target_pairs={{0,16},{4,20},{8,24},{12,28},{16,0},{20,4},{24,8},{28,12},{1,17},{... | collective-permute-start | bytes 75272 | tf_op jit(solution)/shard_map/ppermute | solution.py:263
  328.8 12.3 %collective-permute-start.28 = (bf16[128,768]{1,0:T(8,128)(2,1)S(1)}, bf16[128,768]{1,0:T(8,128)(2,1)S(1)}, u32[]{:S(2)}, u32[]{:S(2)}) collective-permute-start(bf16[128,768]{1,0:T(8,128)(2,1)S(1)} %get-tuple-element.51), channel_id=1, source_target_pairs={{0,1},{1,0},{2,3},{3,2},{4,5},{5,4},{6,7},{7,6},{8,9},{9,8},{10,11... | collective-permute-start | bytes 589832 | tf_op jit(solution)/shard_map/ppermute | solution.py:289
  329.4 11.6 %collective-permute-start.30 = (bf16[128,768]{1,0:T(8,128)(2,1)S(1)}, bf16[128,768]{1,0:T(8,128)(2,1)S(1)}, u32[]{:S(2)}, u32[]{:S(2)}) collective-permute-start(bf16[128,768]{1,0:T(8,128)(2,1)S(1)} %get-tuple-element.52), channel_id=1, source_target_pairs={{0,3},{1,2},{2,1},{3,0},{4,7},{5,6},{6,5},{7,4},{8,11},{9,10},{10,... | collective-permute-start | bytes 589832 | tf_op jit(solution)/shard_map/ppermute | solution.py:289
  331.7 10.3 %collective-permute-start.29 = (bf16[128,768]{1,0:T(8,128)(2,1)S(1)}, bf16[128,768]{1,0:T(8,128)(2,1)S(1)}, u32[]{:S(2)}, u32[]{:S(2)}) collective-permute-start(bf16[128,768]{1,0:T(8,128)(2,1)S(1)} %get-tuple-element.53), channel_id=1, source_target_pairs={{0,2},{1,3},{2,0},{3,1},{4,6},{5,7},{6,4},{7,5},{8,10},{9,11},{10,... | collective-permute-start | bytes 589832 | tf_op jit(solution)/shard_map/ppermute | solution.py:289
Sparse Core Ops, SparseCore 0:
  33.5 70.0 reduce-scatter.2
  106.5 58.6 reduce-scatter.4
  169.2 64.7 all-gather.6
  236.1 64.4 all-gather.4

commit v5 on v4

--- a/solution.py
+++ b/solution.py
@@ -187,6 +187,29 @@
         flops=1e9,
         vmem=58 * 2**20,
         name="activate",
+    )
+
+
+def add_partials(first, second, after=(), carry=()):
+    rows, width = first.shape
+    step = block(width, 1536)
+
+    def kernel(a, b, o):
+        o[...] = (a[...].astype(F32) + b[...].astype(F32)).astype(BF16)
+
+    spec = pl.BlockSpec((rows, step), lambda i: (0, i))
+    return launch(
+        kernel,
+        (width // step,),
+        [spec, spec],
+        spec,
+        jax.ShapeDtypeStruct((rows, width), BF16),
+        (first, second),
+        after,
+        carry,
+        flops=1e9,
+        vmem=58 * 2**20,
+        name="add_partials",
     )
 
 
@@ -325,7 +348,7 @@
     halves = jnp.concatenate([own, other]).reshape(normed_full.shape)
     pre_own, pre_other = run(project, halves, weight_in, 0, 2)
     pre_other = lax.ppermute(pre_other, "gx", [(i, i ^ 1) for i in range(gx)])
-    both = (pre_own.astype(F32) + pre_other.astype(F32)).astype(BF16)
+    both = run(add_partials, pre_own, pre_other)
     (both,) = settle([grad], [both])[1]
     pre = lax.psum_scatter(
         both,

time: 350 us -> 349 us (level)
  Pallas kernels: 72.7 us -> 79.2 us
  other arithmetic: 9.75 us -> 5.4 us
    pallas_call x8 -> x9, Pallas kernels: 72.7 us -> 79.2 us  [launch(): pl.pallas_call(wrapped, grid=grid, in_specs=list(in_specs) + idle * hidde...]
    convert_element_type x1 -> x0, other arithmetic: 4.47 us -> none  [body(): both = (pre_own.astype(F32) + pre_other.astype(F32)).astype(BF16)]
  transfers between devices with their start and end apart: 42 -> 42, of which waited for: 24 -> 24; matrix products, arithmetic and copies ran while one was open for 4% -> 2% of each run, Pallas kernels for 12% -> 14%
where the time goes in v5:
time: 349 us
  waiting for transfers between devices  200 us (57%)
  Pallas kernels  79.2 us (23%)
  starting transfers between devices  44.3 us (13%)
  between operations  14.2 us (4%)
  local copies, waits for them, and re-layouts  5.41 us (2%)
  other arithmetic  5.4 us (2%)
    pallas_call x9, Pallas kernels, launch(): pl.pallas_call(wrapped, grid=grid, in_specs=list(in_specs) + idle * hidde...  79.2 us
    all_gather x2, waiting for transfers between devices, all_rows(): return [lax.all_gather(share, 'gx', axis=0)]  63.3 us
    reduce_scatter x1, waiting for transfers between devices, body(): lax.psum_scatter(both, 'gx', scatter_dimension=0, axis_index_groups=[list...  60.9 us
    ppermute x25, starting transfers between devices, all_sum(): lax.ppermute(value, axis, [(i, i ^ bit * n) for i in range(size)])  28.8 us
    reduce_scatter x1, waiting for transfers between devices, share_sum(): return lax.psum_scatter(partial, 'gx', scatter_dimension=0, tiled=True)  25.5 us
    ppermute x25, waiting for transfers between devices, all_sum(): lax.ppermute(value, axis, [(i, i ^ bit * n) for i in range(size)])  18.2 us
    ppermute x6, waiting for transfers between devices, gather_rows(): lax.ppermute(share, axis, [(i, i ^ bits) for i in range(size)])  15.8 us
    ppermute x6, waiting for transfers between devices, scatter_rows(): lax.ppermute(part, axis, [(i, i ^ bits) for i in range(size)]).astype(F32)  10.3 us
  transfers between devices with their start and end apart: 42, of which 24 were waited for; matrix products, arithmetic and copies ran while one was open for 2% of the time, Pallas kernels for 14%

profile of v5, /device:TPU:0, one launch (start us, length us, event | category | flops | bytes accessed | tf_op | source)
XLA Modules:
  0.0 348.8 jit_solution(7311748043830011876)
XLA Ops:
  7.2 3.0 collective-permute-start
  10.2 1.5 collective-permute-start.2
  11.8 1.0 constant_dynamic-update-slice_fusion.3
  12.8 3.4 collective-permute-done
  16.2 6.0 %collective-permute-done.1 = bf16[128,768]{1,0:T(8,128)(2,1)S(1)} collective-permute-done((bf16[128,768]{1,0:T(8,128)(2,1)}, bf16[128,768]{1,0:T(8,128)(2,1)S(1)}, u32[]{:S(2)}, u32[]{:S(2)}) %collective-permute-start.1) | collective-permute-done | bytes 196640 | tf_op jit(solution)/shard_map/ppermute | solution.py:300
  22.3 0.9 copy-done.5
  23.1 10.2 %project.2 = (bf16[512,6144]{1,0:T(8,128)(2,1)}, s32[1]{0:T(128)}) custom-call(bf16[512,768]{1,0:T(8,128)(2,1)} %copy-done.5, bf16[6144,768]{1,0:T(8,128)(2,1)} %refs_1_.7, s32[1]{0:T(128)} %bitcast.refs_2_), custom_call_target="tpu_custom_call", output_to_operand_aliasing={{1}: (2, {})} | custom-call | flops 9663676416 | bytes 32212254 | tf_op jit(solution)/shard_map/project/pallas_call | solution.py:34
  33.4 0.8 copy-done.3
  34.4 1.6 collective-permute-start.4
  36.6 1.4 collective-permute-done.4
  38.1 1.0 collective-permute-done.5
  39.1 2.7 collective-permute-start.6
  41.7 1.9 collective-permute-done.6
  43.8 1.5 collective-permute-start.9
  45.3 1.5 collective-permute-start.8
  47.4 4.4 %collective-permute-done.9 = bf16[128,768]{1,0:T(8,128)(2,1)S(1)} collective-permute-done((bf16[128,768]{1,0:T(8,128)(2,1)S(1)}, bf16[128,768]{1,0:T(8,128)(2,1)S(1)}, u32[]{:S(2)}, u32[]{:S(2)}) %collective-permute-start.9) | collective-permute-done | bytes 196640 | tf_op jit(solution)/shard_map/ppermute | solution.py:300
  51.8 2.0 collective-permute-done.8
  53.9 1.0 pad_maximum_fusion.1
  54.9 10.8 %project.3 = (bf16[256,6144]{1,0:T(8,128)(2,1)}, bf16[256,6144]{1,0:T(8,128)(2,1)}, s32[1]{0:T(128)}) custom-call(bf16[512,768]{1,0:T(8,128)(2,1)} %bitcast.37, bf16[768,6144]{1,0:T(8,128)(2,1)} %refs_1_.6, s32[1]{0:T(128)} %get-tuple-element.28.refs_2_), custom_call_target="tpu_custom_call", output_to_operand_aliasing={{2}: (2, {})} | custom-call | flops 9663676416 | bytes 32212254 | tf_op jit(solution)/shard_map/project/pallas_call | solution.py:34
  65.7 6.0 %collective-permute-done.10.refs_1_ = bf16[256,6144]{1,0:T(8,128)(2,1)} collective-permute-done((bf16[256,6144]{1,0:T(8,128)(2,1)}, bf16[256,6144]{1,0:T(8,128)(2,1)}, u32[]{:S(2)}, u32[]{:S(2)}) %collective-permute-start.10) | collective-permute-done | bytes 3145760 | tf_op jit(solution)/shard_map/ppermute | solution.py:350
  71.7 6.4 %add_partials.1 = (bf16[256,6144]{1,0:T(8,128)(2,1)}, s32[1]{0:T(128)}) custom-call(bf16[256,6144]{1,0:T(8,128)(2,1)} %get-tuple-element.29.refs_0_, bf16[256,6144]{1,0:T(8,128)(2,1)} %collective-permute-done.10.refs_1_, s32[1]{0:T(128)} %get-tuple-element.31.refs_2_), custom_call_target="tpu_custom_call", output_to_operand_aliasing={{1}: (2, {})} | custom-call | flops 1000000000 | bytes 3333333 | tf_op jit(solution)/shard_map/add_partials/pallas_call | solution.py:34
  78.1 25.5 %reduce-scatter.3.cloned.1.call-done.refs_0_.refs_1_ = bf16[64,6144]{1,0:T(8,128)(2,1)} async-done(((bf16[512,6144]{1,0:T(8,128)(2,1)}), bf16[64,6144]{1,0:T(8,128)(2,1)}) %reduce-scatter.3.cloned.1.call-update) | async-done | bytes 786448 | tf_op jit(solution)/shard_map/reduce_scatter | solution.py:332
  103.7 60.9 %reduce-scatter.5.cloned.1.call-done.refs_0_ = bf16[64,6144]{1,0:T(8,128)(2,1)} async-done(((bf16[256,6144]{1,0:T(8,128)(2,1)}), bf16[64,6144]{1,0:T(8,128)(2,1)}) %reduce-scatter.5.cloned.1.call-update) | async-done | bytes 786448 | tf_op jit(solution)/shard_map/reduce_scatter | solution.py:353
  164.6 3.9 %activate.1 = (bf16[1,64,6144]{2,1,0:T(8,128)(2,1)}, bf16[1,64,6144]{2,1,0:T(8,128)(2,1)}, s32[1]{0:T(128)}) custom-call(bf16[64,6144]{1,0:T(8,128)(2,1)} %reduce-scatter.5.cloned.1.call-done.refs_0_, bf16[64,6144]{1,0:T(8,128)(2,1)} %reduce-scatter.3.cloned.1.call-done.refs_0_.refs_1_, s32[1]{0:T(128)} %get-tuple-element.33.refs_2_), custom_call_target="tpu_custom_call", output_to_operand_aliasing={{2}: (2, {})} | custom-call | flops 1000000000 | bytes 3333333 | tf_op jit(solution)/shard_map/activate/pallas_call | solution.py:34
  169.1 0.6 reduce_sum.56
  169.7 0.6 broadcast_in_dim.33
  170.4 1.1 collective-permute-start.12
  171.4 1.1 collective-permute-start.11
  172.6 0.7 reduce_sum.57
  173.2 0.6 broadcast_in_dim.35
  173.9 1.5 collective-permute-start.16
  175.4 1.5 collective-permute-start.17
  177.4 0.7 add_add_fusion.6
  178.1 2.5 collective-permute-start.14
  180.6 0.6 add_add_fusion.5
  181.3 2.0 collective-permute-done.14
  183.3 1.2 copy.23.refs_0_
  184.5 49.0 %all-gather.7.cloned.1.call-done = bf16[8,64,6144]{2,1,0:T(8,128)(2,1)} async-done(((bf16[1,64,6144]{2,1,0:T(8,128)(2,1)}), bf16[8,64,6144]{2,1,0:T(8,128)(2,1)}) %all-gather.7.cloned.1.call-update) | async-done | bytes 6291472 | tf_op jit(solution)/shard_map/all_gather | solution.py:363
  233.5 14.9 %consume.2 = (bf16[768,6144]{1,0:T(8,128)(2,1)S(1)}, f32[1,6144]{1,0:T(1,128)S(1)}, f32[8,896]{1,0:T(8,128)S(1)}, bf16[512,768]{1,0:T(8,128)(2,1)S(1)}, s32[1]{0:T(128)}) custom-call(bf16[768,512]{1,0:T(8,128)(2,1)} %copy.23.refs_0_, bf16[768,6144]{1,0:T(8,128)(2,1)} %refs_1_.6, bf16[8,1,64,6144]{3,2,1,0:T(8,128)(2,1)} %bitcast.46, ...), custom_call_target="tpu_custom_call", output_to_operand_aliasing={{4}: (5, {})} | custom-call | flops 19327352832 | bytes 64424508 | tf_op jit(solution)/shard_map/consume/pallas_call | solution.py:34
  248.4 2.5 collective-permute-start.20
  252.0 1.5 collective-permute-start.21
  253.6 1.5 collective-permute-start.23
  255.6 4.3 %collective-permute-done.21 = bf16[128,768]{1,0:T(8,128)(2,1)S(1)} collective-permute-done((bf16[128,768]{1,0:T(8,128)(2,1)S(1)}, bf16[128,768]{1,0:T(8,128)(2,1)S(1)}, u32[]{:S(2)}, u32[]{:S(2)}) %collective-permute-start.21) | collective-permute-done | bytes 196640 | tf_op jit(solution)/shard_map/ppermute | solution.py:312
  259.9 3.9 %collective-permute-done.23 = bf16[128,768]{1,0:T(8,128)(2,1)S(1)} collective-permute-done((bf16[128,768]{1,0:T(8,128)(2,1)S(1)}, bf16[128,768]{1,0:T(8,128)(2,1)S(1)}, u32[]{:S(2)}, u32[]{:S(2)}) %collective-permute-start.23) | collective-permute-done | bytes 196640 | tf_op jit(solution)/shard_map/ppermute | solution.py:312
  263.8 1.1 collective-permute-done.22
  265.4 2.0 collective-permute-start.24
  267.4 3.0 collective-permute-done.25
  270.5 2.3 collective-permute-start.27
  272.9 3.9 %collective-permute-done.27.refs_3_.refs_5_ = f32[1,6528]{1,0:T(1,128)S(1)} collective-permute-done((f32[1,6528]{1,0:T(1,128)S(1)}, f32[1,6528]{1,0:T(1,128)S(1)}, u32[]{:S(2)}, u32[]{:S(2)}) %collective-permute-start.27) | collective-permute-done | bytes 26144 | tf_op jit(solution)/shard_map/ppermute | solution.py:286
  277.0 8.7 %write_update.2 = (f32[768,6144]{1,0:T(8,128)}, s32[1]{0:T(128)}) custom-call(bf16[768,6144]{1,0:T(8,128)(2,1)S(1)} %get-tuple-element.37.refs_0_, f32[8,896]{1,0:T(8,128)S(1)} %add_add_fusion.1.refs_1_, f32[1,6528]{1,0:T(1,128)S(1)} %add_add_fusion.2.refs_2_.refs_4_, ...), custom_call_target="tpu_custom_call", output_to_operand_aliasing={{1}: (10, {})} | custom-call | flops 7077888000 | bytes 23592960 | tf_op jit(solution)/shard_map/write_update/pallas_call | solution.py:34
  285.6 14.4 %all-gather.5.cloned.1.call-done = bf16[8,64,6144]{2,1,0:T(8,128)(2,1)} async-done(((bf16[1,64,6144]{2,1,0:T(8,128)(2,1)}), bf16[8,64,6144]{2,1,0:T(8,128)(2,1)}) %all-gather.5.cloned.1.call-update) | async-done | bytes 6291472 | tf_op jit(solution)/shard_map/all_gather | solution.py:363
  300.0 15.5 %consume.3 = (bf16[6144,768]{1,0:T(8,128)(2,1)S(1)}, f32[1,6144]{1,0:T(1,128)S(1)}, f32[8,896]{1,0:T(8,128)S(1)}, bf16[512,768]{1,0:T(8,128)(2,1)S(1)}, s32[1]{0:T(128)}) custom-call(bf16[512,768]{1,0:T(8,128)(2,1)} %copy-done.5, bf16[6144,768]{1,0:T(8,128)(2,1)} %refs_1_.7, bf16[8,1,64,6144]{3,2,1,0:T(8,128)(2,1)} %bitcast.45, ...), custom_call_target="tpu_custom_call", output_to_operand_aliasing={{4}: (3, {})} | custom-call | flops 19327352832 | bytes 64424508 | tf_op jit(solution)/shard_map/consume/pallas_call | solution.py:34
  315.5 2.5 collective-permute-start.33
  319.1 1.3 collective-permute-done.33
  320.4 1.6 collective-permute-done.32
  322.6 2.0 collective-permute-start.34
  324.6 1.7 collective-permute-done.35
  326.4 1.8 collective-permute-start.37
  328.2 0.6 collective-permute-start.28
  328.8 2.3 collective-permute-start.30
  331.2 0.6 collective-permute-start.29
  331.8 8.7 %write_update.3 = (f32[6144,768]{1,0:T(8,128)}, s32[1]{0:T(128)}) custom-call(bf16[6144,768]{1,0:T(8,128)(2,1)S(1)} %get-tuple-element.45.refs_0_, f32[8,896]{1,0:T(8,128)S(1)} %add_add_fusion.refs_1_, f32[1,6272]{1,0:T(1,128)S(1)} %add_add_fusion.3.refs_2_.refs_4_, ...), custom_call_target="tpu_custom_call", output_to_operand_aliasing={{1}: (9, {})} | custom-call | flops 7077888000 | bytes 23592960 | tf_op jit(solution)/shard_map/write_update/pallas_call | solution.py:34
  340.5 1.0 collective-permute-done.29
  341.5 0.8 fusion.10
  (93 shorter events, 7.3 us)
Async XLA Ops:
  7.2 96.5 %reduce-scatter.3.cloned.1.call-start = ((), (), s32[]{:S(2)}) async-start(), calls=%async_computation.2 | async-start | bytes 7077888 | tf_op jit(solution)/shard_map/reduce_scatter | solution.py:332
  7.2 8.9 %collective-permute-start = (bf16[128,768]{1,0:T(8,128)(2,1)}, bf16[128,768]{1,0:T(8,128)(2,1)S(1)}, u32[]{:S(2)}, u32[]{:S(2)}) collective-permute-start(bf16[128,768]{1,0:T(8,128)(2,1)} %param.13), channel_id=1, source_target_pairs={{0,1},{1,0},{2,3},{3,2},{4,5},{5,4},{6,7},{7,6},{8,9},{9,8},{10,11... | collective-permute-start | bytes 589832 | tf_op jit(solution)/shard_map/ppermute | solution.py:300
  10.2 12.0 %collective-permute-start.2 = (bf16[128,768]{1,0:T(8,128)(2,1)}, bf16[128,768]{1,0:T(8,128)(2,1)S(1)}, u32[]{:S(2)}, u32[]{:S(2)}) collective-permute-start(bf16[128,768]{1,0:T(8,128)(2,1)} %param.13), channel_id=1, source_target_pairs={{0,3},{1,2},{2,1},{3,0},{4,7},{5,6},{6,5},{7,4},{8,11},{9,10},{10,... | collective-permute-start | bytes 589832 | tf_op jit(solution)/shard_map/ppermute | solution.py:300
  11.7 10.5 %collective-permute-start.1 = (bf16[128,768]{1,0:T(8,128)(2,1)}, bf16[128,768]{1,0:T(8,128)(2,1)S(1)}, u32[]{:S(2)}, u32[]{:S(2)}) collective-permute-start(bf16[128,768]{1,0:T(8,128)(2,1)} %param.13), channel_id=1, source_target_pairs={{0,2},{1,3},{2,0},{3,1},{4,6},{5,7},{6,4},{7,5},{8,10},{9,11},{10,... | collective-permute-start | bytes 589832 | tf_op jit(solution)/shard_map/ppermute | solution.py:300
  22.3 0.9 copy-start.5
  33.4 0.9 copy-start.3
  33.4 10.3 %copy-start.6 = (f32[768]{0:T(1024)S(1)}, f32[768]{0:T(1024)}, u32[]{:S(2)}) copy-start(f32[768]{0:T(1024)} %param.10) | copy-start | bytes 9220
  33.4 131.2 %reduce-scatter.5.cloned.1.call-start = ((), (), s32[]{:S(2)}) async-start(), calls=%async_computation.3 | async-start | bytes 3932160 | tf_op jit(solution)/shard_map/reduce_scatter | solution.py:353
  34.4 3.6 %collective-permute-start.4 = (f32[2,128]{1,0:T(2,128)S(1)}, f32[2,128]{1,0:T(2,128)S(1)}, u32[]{:S(2)}, u32[]{:S(2)}) collective-permute-start(f32[2,128]{1,0:T(2,128)S(1)} %pad_maximum_fusion.4), channel_id=1, source_target_pairs={{0,8},{4,12},{8,0},{12,4},{16,24},{20,28},{24,16},{28,20},{1,9},{5... | collective-permute-start | bytes 3080 | tf_op jit(solution)/shard_map/ppermute | solution.py:286
  36.1 3.0 collective-permute-start.5
  36.1 3.0 collective-permute-start.3
  39.1 4.5 %collective-permute-start.6 = (f32[2,128]{1,0:T(2,128)S(1)}, f32[2,128]{1,0:T(2,128)S(1)}, u32[]{:S(2)}, u32[]{:S(2)}) collective-permute-start(f32[2,128]{1,0:T(2,128)S(1)} %add_add_fusion.4), channel_id=1, source_target_pairs={{0,16},{4,20},{8,24},{12,28},{16,0},{20,4},{24,8},{28,12},{1,17},{... | collective-permute-start | bytes 3080 | tf_op jit(solution)/shard_map/ppermute | solution.py:286
  43.8 8.0 %collective-permute-start.9 = (bf16[128,768]{1,0:T(8,128)(2,1)S(1)}, bf16[128,768]{1,0:T(8,128)(2,1)S(1)}, u32[]{:S(2)}, u32[]{:S(2)}) collective-permute-start(bf16[128,768]{1,0:T(8,128)(2,1)S(1)} %fusion.5), channel_id=1, source_target_pairs={{0,3},{1,2},{2,1},{3,0},{4,7},{5,6},{6,5},{7,4},{8,11},{9,10},{10,... | collective-permute-start | bytes 589832 | tf_op jit(solution)/shard_map/ppermute | solution.py:300
  45.3 8.4 %collective-permute-start.8 = (bf16[128,768]{1,0:T(8,128)(2,1)S(1)}, bf16[128,768]{1,0:T(8,128)(2,1)S(1)}, u32[]{:S(2)}, u32[]{:S(2)}) collective-permute-start(bf16[128,768]{1,0:T(8,128)(2,1)S(1)} %fusion.5), channel_id=1, source_target_pairs={{0,2},{1,3},{2,0},{3,1},{4,6},{5,7},{6,4},{7,5},{8,10},{9,11},{10,... | collective-permute-start | bytes 589832 | tf_op jit(solution)/shard_map/ppermute | solution.py:300
  46.8 6.9 %collective-permute-start.7 = (bf16[128,768]{1,0:T(8,128)(2,1)S(1)}, bf16[128,768]{1,0:T(8,128)(2,1)S(1)}, u32[]{:S(2)}, u32[]{:S(2)}) collective-permute-start(bf16[128,768]{1,0:T(8,128)(2,1)S(1)} %fusion.5), channel_id=1, source_target_pairs={{0,1},{1,0},{2,3},{3,2},{4,5},{5,4},{6,7},{7,6},{8,9},{9,8},{10,11... | collective-permute-start | bytes 589832 | tf_op jit(solution)/shard_map/ppermute | solution.py:300
  65.7 6.0 %collective-permute-start.10 = (bf16[256,6144]{1,0:T(8,128)(2,1)}, bf16[256,6144]{1,0:T(8,128)(2,1)}, u32[]{:S(2)}, u32[]{:S(2)}) collective-permute-start(bf16[256,6144]{1,0:T(8,128)(2,1)} %get-tuple-element.30), channel_id=1, source_target_pairs={{0,4},{4,0},{8,12},{12,8},{16,20},{20,16},{24,28},{28,24},{1,5},{5... | collective-permute-start | bytes 9437192 | tf_op jit(solution)/shard_map/ppermute | solution.py:350
  103.7 65.4 %copy-start.7 = (f32[768]{0:T(1024)S(1)}, f32[768]{0:T(1024)}, u32[]{:S(2)}) copy-start(f32[768]{0:T(1024)} %param.14) | copy-start | bytes 9220
  103.7 68.9 %copy-start.1 = (f32[6144]{0:T(1024)S(1)}, f32[6144]{0:T(1024)}, u32[]{:S(2)}) copy-start(f32[6144]{0:T(1024)} %param.16) | copy-start | bytes 73732
  103.7 129.8 %all-gather.7.cloned.1.call-start = ((), (), s32[]{:S(2)}) async-start(), calls=%async_computation.5 | async-start | bytes 7077888 | tf_op jit(solution)/shard_map/all_gather | solution.py:363
  168.5 131.5 %all-gather.5.cloned.1.call-start = ((), (), s32[]{:S(2)}) async-start(), calls=%async_computation.4 | async-start | bytes 7077888 | tf_op jit(solution)/shard_map/all_gather | solution.py:363
  170.4 6.5 %collective-permute-start.12 = (f32[128]{0:T(128)S(1)}, f32[128]{0:T(128)S(1)}, u32[]{:S(2)}, u32[]{:S(2)}) collective-permute-start(f32[128]{0:T(128)S(1)} %broadcast_in_dim.33), channel_id=1, source_target_pairs={{0,8},{4,12},{8,0},{12,4},{16,24},{20,28},{24,16},{28,20},{1,9},{5... | collective-permute-start | bytes 1544 | tf_op jit(solution)/shard_map/ppermute | solution.py:286
  171.4 6.0 %collective-permute-start.13 = (f32[128]{0:T(128)S(1)}, f32[128]{0:T(128)S(1)}, u32[]{:S(2)}, u32[]{:S(2)}) collective-permute-start(f32[128]{0:T(128)S(1)} %broadcast_in_dim.33), channel_id=1, source_target_pairs={{0,12},{4,8},{8,4},{12,0},{16,28},{20,24},{24,20},{28,16},{1,13},{... | collective-permute-start | bytes 1544 | tf_op jit(solution)/shard_map/ppermute | solution.py:286
  171.4 6.0 %collective-permute-start.11 = (f32[128]{0:T(128)S(1)}, f32[128]{0:T(128)S(1)}, u32[]{:S(2)}, u32[]{:S(2)}) collective-permute-start(f32[128]{0:T(128)S(1)} %broadcast_in_dim.33), channel_id=1, source_target_pairs={{0,4},{4,0},{8,12},{12,8},{16,20},{20,16},{24,28},{28,24},{1,5},{5... | collective-permute-start | bytes 1544 | tf_op jit(solution)/shard_map/ppermute | solution.py:286
  173.9 6.8 %collective-permute-start.16 = (f32[128]{0:T(128)S(1)}, f32[128]{0:T(128)S(1)}, u32[]{:S(2)}, u32[]{:S(2)}) collective-permute-start(f32[128]{0:T(128)S(1)} %broadcast_in_dim.35), channel_id=1, source_target_pairs={{0,2},{1,3},{2,0},{3,1},{4,6},{5,7},{6,4},{7,5},{8,10},{9,11},{10,... | collective-permute-start | bytes 1544 | tf_op jit(solution)/shard_map/ppermute | solution.py:286
  175.4 5.2 %collective-permute-start.17 = (f32[128]{0:T(128)S(1)}, f32[128]{0:T(128)S(1)}, u32[]{:S(2)}, u32[]{:S(2)}) collective-permute-start(f32[128]{0:T(128)S(1)} %broadcast_in_dim.35), channel_id=1, source_target_pairs={{0,3},{1,2},{2,1},{3,0},{4,7},{5,6},{6,5},{7,4},{8,11},{9,10},{10,... | collective-permute-start | bytes 1544 | tf_op jit(solution)/shard_map/ppermute | solution.py:286
  176.8 3.8 %collective-permute-start.15 = (f32[128]{0:T(128)S(1)}, f32[128]{0:T(128)S(1)}, u32[]{:S(2)}, u32[]{:S(2)}) collective-permute-start(f32[128]{0:T(128)S(1)} %broadcast_in_dim.35), channel_id=1, source_target_pairs={{0,1},{1,0},{2,3},{3,2},{4,5},{5,4},{6,7},{7,6},{8,9},{9,8},{10,11... | collective-permute-start | bytes 1544 | tf_op jit(solution)/shard_map/ppermute | solution.py:286
  178.1 5.2 %collective-permute-start.14 = (f32[128]{0:T(128)S(1)}, f32[128]{0:T(128)S(1)}, u32[]{:S(2)}, u32[]{:S(2)}) collective-permute-start(f32[128]{0:T(128)S(1)} %add_add_fusion.6), channel_id=1, source_target_pairs={{0,16},{4,20},{8,24},{12,28},{16,0},{20,4},{24,8},{28,12},{1,17},{... | collective-permute-start | bytes 1544 | tf_op jit(solution)/shard_map/ppermute | solution.py:286
  233.5 43.3 %copy-start.4 = (bf16[128,768]{1,0:T(8,128)(2,1)S(1)}, bf16[128,768]{1,0:T(8,128)(2,1)}, u32[]{:S(2)}) copy-start(bf16[128,768]{1,0:T(8,128)(2,1)} %param.13) | copy-start | bytes 589828
  248.4 28.5 %copy-start.2 = (f32[6144]{0:T(1024)S(1)}, f32[6144]{0:T(1024)}, u32[]{:S(2)}) copy-start(f32[6144]{0:T(1024)} %param.15) | copy-start | bytes 73732
  248.4 6.6 %collective-permute-start.20 = (f32[8,896]{1,0:T(8,128)S(1)}, f32[8,896]{1,0:T(8,128)S(1)}, u32[]{:S(2)}, u32[]{:S(2)}) collective-permute-start(f32[8,896]{1,0:T(8,128)S(1)} %get-tuple-element.38), channel_id=1, source_target_pairs={{0,3},{1,2},{2,1},{3,0},{4,7},{5,6},{6,5},{7,4},{8,11},{9,10},{10,... | collective-permute-start | bytes 86024 | tf_op jit(solution)/shard_map/ppermute | solution.py:286
  250.9 4.7 %collective-permute-start.19 = (f32[8,896]{1,0:T(8,128)S(1)}, f32[8,896]{1,0:T(8,128)S(1)}, u32[]{:S(2)}, u32[]{:S(2)}) collective-permute-start(f32[8,896]{1,0:T(8,128)S(1)} %get-tuple-element.38), channel_id=1, source_target_pairs={{0,2},{1,3},{2,0},{3,1},{4,6},{5,7},{6,4},{7,5},{8,10},{9,11},{10,... | collective-permute-start | bytes 86024 | tf_op jit(solution)/shard_map/ppermute | solution.py:286
  251.4 4.2 %collective-permute-start.18 = (f32[8,896]{1,0:T(8,128)S(1)}, f32[8,896]{1,0:T(8,128)S(1)}, u32[]{:S(2)}, u32[]{:S(2)}) collective-permute-start(f32[8,896]{1,0:T(8,128)S(1)} %get-tuple-element.38), channel_id=1, source_target_pairs={{0,1},{1,0},{2,3},{3,2},{4,5},{5,4},{6,7},{7,6},{8,9},{9,8},{10,11... | collective-permute-start | bytes 86024 | tf_op jit(solution)/shard_map/ppermute | solution.py:286
  252.0 7.9 %collective-permute-start.21 = (bf16[128,768]{1,0:T(8,128)(2,1)S(1)}, bf16[128,768]{1,0:T(8,128)(2,1)S(1)}, u32[]{:S(2)}, u32[]{:S(2)}) collective-permute-start(bf16[128,768]{1,0:T(8,128)(2,1)S(1)} %get-tuple-element.58), channel_id=1, source_target_pairs={{0,1},{1,0},{2,3},{3,2},{4,5},{5,4},{6,7},{7,6},{8,9},{9,8},{10,11... | collective-permute-start | bytes 589832 | tf_op jit(solution)/shard_map/ppermute | solution.py:312
  253.6 10.3 %collective-permute-start.23 = (bf16[128,768]{1,0:T(8,128)(2,1)S(1)}, bf16[128,768]{1,0:T(8,128)(2,1)S(1)}, u32[]{:S(2)}, u32[]{:S(2)}) collective-permute-start(bf16[128,768]{1,0:T(8,128)(2,1)S(1)} %get-tuple-element.59), channel_id=1, source_target_pairs={{0,3},{1,2},{2,1},{3,0},{4,7},{5,6},{6,5},{7,4},{8,11},{9,10},{10,... | collective-permute-start | bytes 589832 | tf_op jit(solution)/shard_map/ppermute | solution.py:312
  255.0 9.9 %collective-permute-start.22 = (bf16[128,768]{1,0:T(8,128)(2,1)S(1)}, bf16[128,768]{1,0:T(8,128)(2,1)S(1)}, u32[]{:S(2)}, u32[]{:S(2)}) collective-permute-start(bf16[128,768]{1,0:T(8,128)(2,1)S(1)} %get-tuple-element.60), channel_id=1, source_target_pairs={{0,2},{1,3},{2,0},{3,1},{4,6},{5,7},{6,4},{7,5},{8,10},{9,11},{10,... | collective-permute-start | bytes 589832 | tf_op jit(solution)/shard_map/ppermute | solution.py:312
  265.2 5.2 %collective-permute-start.25 = (f32[1,6528]{1,0:T(1,128)S(1)}, f32[1,6528]{1,0:T(1,128)S(1)}, u32[]{:S(2)}, u32[]{:S(2)}) collective-permute-start(f32[1,6528]{1,0:T(1,128)S(1)} %pad_maximum_fusion.2), channel_id=1, source_target_pairs={{0,8},{4,12},{8,0},{12,4},{16,24},{20,28},{24,16},{28,20},{1,9},{5... | collective-permute-start | bytes 78344 | tf_op jit(solution)/shard_map/ppermute | solution.py:286
  265.3 5.2 %collective-permute-start.26 = (f32[1,6528]{1,0:T(1,128)S(1)}, f32[1,6528]{1,0:T(1,128)S(1)}, u32[]{:S(2)}, u32[]{:S(2)}) collective-permute-start(f32[1,6528]{1,0:T(1,128)S(1)} %pad_maximum_fusion.2), channel_id=1, source_target_pairs={{0,12},{4,8},{8,4},{12,0},{16,28},{20,24},{24,20},{28,16},{1,13},{... | collective-permute-start | bytes 78344 | tf_op jit(solution)/shard_map/ppermute | solution.py:286
  265.4 5.1 %collective-permute-start.24 = (f32[1,6528]{1,0:T(1,128)S(1)}, f32[1,6528]{1,0:T(1,128)S(1)}, u32[]{:S(2)}, u32[]{:S(2)}) collective-permute-start(f32[1,6528]{1,0:T(1,128)S(1)} %pad_maximum_fusion.2), channel_id=1, source_target_pairs={{0,4},{4,0},{8,12},{12,8},{16,20},{20,16},{24,28},{28,24},{1,5},{5... | collective-permute-start | bytes 78344 | tf_op jit(solution)/shard_map/ppermute | solution.py:286
  270.5 6.2 %collective-permute-start.27 = (f32[1,6528]{1,0:T(1,128)S(1)}, f32[1,6528]{1,0:T(1,128)S(1)}, u32[]{:S(2)}, u32[]{:S(2)}) collective-permute-start(f32[1,6528]{1,0:T(1,128)S(1)} %add_add_fusion.2.refs_2_.refs_4_), channel_id=1, source_target_pairs={{0,16},{4,20},{8,24},{12,28},{16,0},{20,4},{24,8},{28,12},{1,17},{... | collective-permute-start | bytes 78344 | tf_op jit(solution)/shard_map/ppermute | solution.py:286
  276.9 8.7 %copy-start = (f32[128,768]{1,0:T(8,128)}, f32[128,768]{1,0:T(8,128)S(1)}, u32[]{:S(2)}) copy-start(f32[128,768]{1,0:T(8,128)S(1)} %fusion.9.refs_9_) | copy-start | bytes 1179652
  300.0 24.6 %copy-start.8 = (f32[768]{0:T(1024)S(1)}, f32[768]{0:T(1024)}, u32[]{:S(2)}) copy-start(f32[768]{0:T(1024)} %param.17) | copy-start | bytes 9220
  315.5 4.8 %collective-permute-start.33 = (f32[8,896]{1,0:T(8,128)S(1)}, f32[8,896]{1,0:T(8,128)S(1)}, u32[]{:S(2)}, u32[]{:S(2)}) collective-permute-start(f32[8,896]{1,0:T(8,128)S(1)} %get-tuple-element.46), channel_id=1, source_target_pairs={{0,3},{1,2},{2,1},{3,0},{4,7},{5,6},{6,5},{7,4},{8,11},{9,10},{10,... | collective-permute-start | bytes 86024 | tf_op jit(solution)/shard_map/ppermute | solution.py:286
  318.1 3.9 %collective-permute-start.32 = (f32[8,896]{1,0:T(8,128)S(1)}, f32[8,896]{1,0:T(8,128)S(1)}, u32[]{:S(2)}, u32[]{:S(2)}) collective-permute-start(f32[8,896]{1,0:T(8,128)S(1)} %get-tuple-element.46), channel_id=1, source_target_pairs={{0,2},{1,3},{2,0},{3,1},{4,6},{5,7},{6,4},{7,5},{8,10},{9,11},{10,... | collective-permute-start | bytes 86024 | tf_op jit(solution)/shard_map/ppermute | solution.py:286
  318.5 3.9 %collective-permute-start.31 = (f32[8,896]{1,0:T(8,128)S(1)}, f32[8,896]{1,0:T(8,128)S(1)}, u32[]{:S(2)}, u32[]{:S(2)}) collective-permute-start(f32[8,896]{1,0:T(8,128)S(1)} %get-tuple-element.46), channel_id=1, source_target_pairs={{0,1},{1,0},{2,3},{3,2},{4,5},{5,4},{6,7},{7,6},{8,9},{9,8},{10,11... | collective-permute-start | bytes 86024 | tf_op jit(solution)/shard_map/ppermute | solution.py:286
  322.4 3.9 %collective-permute-start.35 = (f32[1,6272]{1,0:T(1,128)S(1)}, f32[1,6272]{1,0:T(1,128)S(1)}, u32[]{:S(2)}, u32[]{:S(2)}) collective-permute-start(f32[1,6272]{1,0:T(1,128)S(1)} %pad_maximum_fusion.3), channel_id=1, source_target_pairs={{0,8},{4,12},{8,0},{12,4},{16,24},{20,28},{24,16},{28,20},{1,9},{5... | collective-permute-start | bytes 75272 | tf_op jit(solution)/shard_map/ppermute | solution.py:286
  322.5 3.8 %collective-permute-start.36 = (f32[1,6272]{1,0:T(1,128)S(1)}, f32[1,6272]{1,0:T(1,128)S(1)}, u32[]{:S(2)}, u32[]{:S(2)}) collective-permute-start(f32[1,6272]{1,0:T(1,128)S(1)} %pad_maximum_fusion.3), channel_id=1, source_target_pairs={{0,12},{4,8},{8,4},{12,0},{16,28},{20,24},{24,20},{28,16},{1,13},{... | collective-permute-start | bytes 75272 | tf_op jit(solution)/shard_map/ppermute | solution.py:286
  322.6 3.7 %collective-permute-start.34 = (f32[1,6272]{1,0:T(1,128)S(1)}, f32[1,6272]{1,0:T(1,128)S(1)}, u32[]{:S(2)}, u32[]{:S(2)}) collective-permute-start(f32[1,6272]{1,0:T(1,128)S(1)} %pad_maximum_fusion.3), channel_id=1, source_target_pairs={{0,4},{4,0},{8,12},{12,8},{16,20},{20,16},{24,28},{28,24},{1,5},{5... | collective-permute-start | bytes 75272 | tf_op jit(solution)/shard_map/ppermute | solution.py:286
  326.4 5.4 %collective-permute-start.37 = (f32[1,6272]{1,0:T(1,128)S(1)}, f32[1,6272]{1,0:T(1,128)S(1)}, u32[]{:S(2)}, u32[]{:S(2)}) collective-permute-start(f32[1,6272]{1,0:T(1,128)S(1)} %add_add_fusion.3.refs_2_.refs_4_), channel_id=1, source_target_pairs={{0,16},{4,20},{8,24},{12,28},{16,0},{20,4},{24,8},{28,12},{1,17},{... | collective-permute-start | bytes 75272 | tf_op jit(solution)/shard_map/ppermute | solution.py:286
  328.2 12.3 %collective-permute-start.28 = (bf16[128,768]{1,0:T(8,128)(2,1)S(1)}, bf16[128,768]{1,0:T(8,128)(2,1)S(1)}, u32[]{:S(2)}, u32[]{:S(2)}) collective-permute-start(bf16[128,768]{1,0:T(8,128)(2,1)S(1)} %get-tuple-element.55), channel_id=1, source_target_pairs={{0,1},{1,0},{2,3},{3,2},{4,5},{5,4},{6,7},{7,6},{8,9},{9,8},{10,11... | collective-permute-start | bytes 589832 | tf_op jit(solution)/shard_map/ppermute | solution.py:312
  328.8 11.6 %collective-permute-start.30 = (bf16[128,768]{1,0:T(8,128)(2,1)S(1)}, bf16[128,768]{1,0:T(8,128)(2,1)S(1)}, u32[]{:S(2)}, u32[]{:S(2)}) collective-permute-start(bf16[128,768]{1,0:T(8,128)(2,1)S(1)} %get-tuple-element.56), channel_id=1, source_target_pairs={{0,3},{1,2},{2,1},{3,0},{4,7},{5,6},{6,5},{7,4},{8,11},{9,10},{10,... | collective-permute-start | bytes 589832 | tf_op jit(solution)/shard_map/ppermute | solution.py:312
  331.2 10.3 %collective-permute-start.29 = (bf16[128,768]{1,0:T(8,128)(2,1)S(1)}, bf16[128,768]{1,0:T(8,128)(2,1)S(1)}, u32[]{:S(2)}, u32[]{:S(2)}) collective-permute-start(bf16[128,768]{1,0:T(8,128)(2,1)S(1)} %get-tuple-element.57), channel_id=1, source_target_pairs={{0,2},{1,3},{2,0},{3,1},{4,6},{5,7},{6,4},{7,5},{8,10},{9,11},{10,... | collective-permute-start | bytes 589832 | tf_op jit(solution)/shard_map/ppermute | solution.py:312
Sparse Core Ops, SparseCore 0:
  33.5 70.0 reduce-scatter.2
  105.9 58.6 reduce-scatter.4
  168.6 64.7 all-gather.6
  235.5 64.4 all-gather.4
